TPU v7x, 256 devices: a whole 4x4x8 slice. The times are simulated.
256 devices in a mesh: vel: 16 (over x, y_lo, core), space: 16 (over z, y_hi).
Axes of the slice: x: 4, y: 4 (y_hi: 2, y_lo: 2; y = y_hi * 2 + y_lo), z: 8, core: 2. Of those that a mesh axis runs over, the one named last changes fastest.
Arguments:
- state: float32 [13824, 64, 256], P('vel', 'space'), as said below
- velocity_order: int32 [13824], P('vel'), may hold values from 0 to 13823, as said below
- wall_tag: int32 [64, 2, 32], replicated, may hold values from 0 to 2
Outputs:
- state_next: float32 [13824, 64, 256], P('vel', 'space')
- wall_heat: float32 [64, 2, 32], P('space')
Inputs may be any that keep to these rules, and one draw needn't show every extreme that they name: `velocity_order`: a permutation; the slots below 6912 hold exactly the velocities with negative cx. `state`: every entry is positive.
All inputs are finite; a program needn't handle non-finite values.
Results may differ from a plain program's by a relative error of at most 0.0001.
Values sent between devices are 32-bit elements; how exact they have to be, the bound alone decides.
No kernel may reach another device: no remote copies, remote signals or barrier semaphores. Data moves between devices by JAX's collectives and lax.ppermute only.
A program may use at most 256 MiB of HBM per device.

v0:
```python
import math

import jax
import jax.numpy as jnp
from jax import lax
from jax.sharding import PartitionSpec as P

NV1 = 24
NY = 32
NZ = 8
STEPS = 2


VSPAN = 12.0
RAREFACTION = 0.05
SHEAR_EXPONENT = 0.81
PRANDTL = 2.0 / 3.0
COURANT = 0.3
BOTTOM_TEMP = 1.4
TOP_TEMP = 0.7
HIGHEST = lax.Precision.HIGHEST


def extended_2(cells, sides, width):
    for axis, dim in sides:
        count = lax.axis_size(axis)
        head = lax.slice_in_dim(cells, 0, width, axis=dim)
        tail = lax.slice_in_dim(cells, cells.shape[dim] - width, cells.shape[dim], axis=dim)
        cells = jnp.concatenate(
            [
                lax.ppermute(tail, axis, [(i, (i + 1) % count) for i in range(count)]),
                cells,
                lax.ppermute(head, axis, [((i + 1) % count, i) for i in range(count)]),
            ],
            axis=dim,
        )
    return cells


def velocity_parts(index_all, per_dim):
    spacing = VSPAN / per_dim

    def coordinate(level_index):
        return (2 * level_index - (per_dim - 1)).astype(jnp.float32) * (0.5 * spacing)

    return (
        coordinate(index_all // (per_dim * per_dim)),
        coordinate(index_all // per_dim % per_dim),
        coordinate(index_all % per_dim),
    )


def velocity_weight(per_dim):
    return (VSPAN / per_dim) ** 3 / (2.0 * math.pi) ** 1.5


def wall_tables(per_dim):
    index_all = jnp.arange(per_dim**3, dtype=jnp.int32)
    vel_x, vel_y, vel_z = velocity_parts(index_all, per_dim)
    speed_sq = vel_x * vel_x + vel_y * vel_y + vel_z * vel_z
    levels = 0.7 + 0.3 * jnp.arange(3, dtype=jnp.float32)
    wall_temps = jnp.stack([BOTTOM_TEMP * levels, TOP_TEMP * levels])
    normal = jnp.stack([jnp.maximum(vel_z, 0.0), jnp.maximum(-vel_z, 0.0)]) * velocity_weight(
        per_dim
    )
    profile = wall_temps[:, :, None] ** (-1.5) * jnp.exp(
        -speed_sq[None, None, :] / (2.0 * wall_temps[:, :, None])
    )
    mass_flux = jnp.sum(normal[:, None, :] * profile, axis=-1)
    energy = jnp.sum(normal[:, None, :] * profile * (0.5 * speed_sq)[None, None, :], axis=-1)
    return (wall_temps, mass_flux, energy)


def pick(lookup, wall_tags):
    onehot = (wall_tags[..., None] == jnp.arange(3, dtype=jnp.int32)).astype(jnp.float32)
    return jnp.sum(onehot * lookup[None, :, None, :], axis=-1)


def block_moments(centre, vel_x, vel_y, vel_z):
    number = centre.shape[0]
    speed_sq = vel_x * vel_x + vel_y * vel_y + vel_z * vel_z
    coefficients = jnp.stack(
        [jnp.ones_like(vel_x), vel_x, vel_y, vel_z, speed_sq]
    ) * velocity_weight(NV1)
    return jnp.dot(coefficients, centre.reshape(number, -1), precision=HIGHEST)


def block_walls(centre, vel_x, vel_y, vel_z, depth):
    number = centre.shape[0]
    speed_sq = vel_x * vel_x + vel_y * vel_y + vel_z * vel_z
    bottom = centre[:, :, 0::depth].reshape(number, -1)
    top_layer = centre[:, :, depth - 1 :: depth].reshape(number, -1)
    inward_bottom = jnp.maximum(-vel_z, 0.0) * velocity_weight(NV1)
    inward_top = jnp.maximum(vel_z, 0.0) * velocity_weight(NV1)
    low_sums = jnp.dot(
        jnp.stack([inward_bottom, inward_bottom * 0.5 * speed_sq]), bottom, precision=HIGHEST
    )
    high_sums = jnp.dot(
        jnp.stack([inward_top, inward_top * 0.5 * speed_sq]), top_layer, precision=HIGHEST
    )
    return jnp.concatenate([low_sums, high_sums], axis=0)


def site_average_arrays(hydrodynamic_averages):
    particle_concentration = hydrodynamic_averages[0]
    mean_flow_first = hydrodynamic_averages[1] / particle_concentration
    mean_flow_second = hydrodynamic_averages[2] / particle_concentration
    mean_flow_third = hydrodynamic_averages[3] / particle_concentration
    pointwise_thermal_level = (
        hydrodynamic_averages[4] / particle_concentration
        - (
            mean_flow_first * mean_flow_first
            + mean_flow_second * mean_flow_second
            + mean_flow_third * mean_flow_third
        )
    ) / 3.0
    return (
        particle_concentration,
        mean_flow_first,
        mean_flow_second,
        mean_flow_third,
        pointwise_thermal_level,
    )


def heat_terms(centre, vel_x, vel_y, vel_z, mean_flow_first, mean_flow_second, mean_flow_third):
    flat_block = centre.reshape(centre.shape[0], -1)
    rel_x = vel_x[:, None] - mean_flow_first[None]
    rel_y = vel_y[:, None] - mean_flow_second[None]
    rel_z = vel_z[:, None] - mean_flow_third[None]
    scaled = (
        0.5 * velocity_weight(NV1) * (rel_x * rel_x + rel_y * rel_y + rel_z * rel_z) * flat_block
    )
    return jnp.stack(
        [
            jnp.sum(rel_x * scaled, axis=0),
            jnp.sum(rel_y * scaled, axis=0),
            jnp.sum(rel_z * scaled, axis=0),
        ]
    )


def wall_state(wall_sums, wall_tags, tables):
    wall_temps, mass_flux, energy = tables
    columns = wall_tags.shape[0]
    wall_parts = wall_sums.reshape(2, 2, columns, wall_tags.shape[2])
    incoming_mass = jnp.transpose(wall_parts[:, 0], (1, 0, 2))
    incoming_energy = jnp.transpose(wall_parts[:, 1], (1, 0, 2))
    wall_density = incoming_mass / pick(mass_flux, wall_tags)
    wall_heat = wall_density * pick(energy, wall_tags) - incoming_energy
    return (wall_density, pick(wall_temps, wall_tags), wall_heat)


def relax(extended, vel_x, vel_y, vel_z, averaged_arrays, wall_density, plate_temp, depth):
    centre = extended[:, 1:-1]
    left_cells = extended[:, :-2]
    right_cells = extended[:, 2:]
    number, columns, plane_size = centre.shape
    (
        particle_concentration,
        mean_flow_first,
        mean_flow_second,
        mean_flow_third,
        pointwise_thermal_level,
        thermal_current_first,
        thermal_current_second,
        thermal_current_third,
    ) = [field.reshape(columns, plane_size)[None] for field in averaged_arrays]

    def spread_v(velocity):
        return velocity[:, None, None]

    def transport(velocity, upwind_low, upwind_high):
        return spread_v(jnp.maximum(velocity, 0.0)) * (centre - upwind_low) + spread_v(
            jnp.minimum(velocity, 0.0)
        ) * (upwind_high - centre)

    speed_sq = vel_x * vel_x + vel_y * vel_y + vel_z * vel_z

    def emitted(wall_side):
        wall_t = plate_temp[:, wall_side][None]
        averaged_entries = (wall_density[:, wall_side] * plate_temp[:, wall_side] ** (-1.5))[
            None
        ] * jnp.exp(-spread_v(speed_sq) / (2.0 * wall_t))
        return jnp.repeat(averaged_entries, depth, axis=-1)

    z_layer = jnp.arange(plane_size, dtype=jnp.int32) % depth
    below_cells = jnp.where(z_layer == 0, emitted(0), jnp.roll(centre, 1, axis=-1))
    above_cells = jnp.where(z_layer == depth - 1, emitted(1), jnp.roll(centre, -1, axis=-1))
    transport_sum = (
        transport(vel_x, left_cells, right_cells)
        + transport(vel_y, jnp.roll(centre, depth, axis=-1), jnp.roll(centre, -depth, axis=-1))
        + transport(vel_z, below_cells, above_cells)
    )
    rel_x = spread_v(vel_x) - mean_flow_first
    rel_y = spread_v(vel_y) - mean_flow_second
    rel_z = spread_v(vel_z) - mean_flow_third
    relative_motion_norm = rel_x * rel_x + rel_y * rel_y + rel_z * rel_z
    target_maxwellian = (
        particle_concentration
        * pointwise_thermal_level ** (-1.5)
        * jnp.exp(-relative_motion_norm / (2.0 * pointwise_thermal_level))
    )
    factor = 1.0 + (1.0 - PRANDTL) * (
        rel_x * thermal_current_first
        + rel_y * thermal_current_second
        + rel_z * thermal_current_third
    ) / (5.0 * particle_concentration * pointwise_thermal_level * pointwise_thermal_level) * (
        relative_motion_norm / pointwise_thermal_level - 5.0
    )
    relaxation_rate = (
        particle_concentration
        * jnp.exp((1.0 - SHEAR_EXPONENT) * jnp.log(pointwise_thermal_level))
        / RAREFACTION
    )
    top_speed = (NV1 - 1) * 0.5 * VSPAN / NV1
    courant_ratio = COURANT / top_speed
    step_time = COURANT / (depth * top_speed)
    return (
        centre
        - courant_ratio * transport_sum
        + step_time * relaxation_rate * (target_maxwellian * factor - centre)
    )


def advance(extended, wall_tags, vel_x, vel_y, vel_z, tables):
    centre = extended[:, 1:-1]
    wall_local = block_walls(centre, vel_x, vel_y, vel_z, NZ)
    hydrodynamic_averages, wall_sums = lax.psum(
        (block_moments(centre, vel_x, vel_y, vel_z), wall_local), "vel"
    )
    (
        particle_concentration,
        mean_flow_first,
        mean_flow_second,
        mean_flow_third,
        pointwise_thermal_level,
    ) = site_average_arrays(hydrodynamic_averages)
    thermal_current_triple = lax.psum(
        heat_terms(centre, vel_x, vel_y, vel_z, mean_flow_first, mean_flow_second, mean_flow_third),
        "vel",
    )
    averaged_arrays = (
        particle_concentration,
        mean_flow_first,
        mean_flow_second,
        mean_flow_third,
        pointwise_thermal_level,
        thermal_current_triple[0],
        thermal_current_triple[1],
        thermal_current_triple[2],
    )
    wall_density, plate_temp, wall_heat = wall_state(wall_sums, wall_tags, tables)
    return (
        relax(extended, vel_x, vel_y, vel_z, averaged_arrays, wall_density, plate_temp, NZ),
        wall_heat,
    )


def body(state, velocity_order, wall_tag):
    vel_x, vel_y, vel_z = velocity_parts(velocity_order, NV1)
    tables = wall_tables(NV1)
    columns = state.shape[1]
    padded_tags = jnp.concatenate([wall_tag[-2:], wall_tag, wall_tag[:2]], axis=0)
    first_column = lax.axis_index("space") * columns
    current = state
    wall_heat = jnp.zeros((columns, 2, NY), jnp.float32)
    for step_index in range(STEPS):
        extended = extended_2(current, (("space", 1),), 1)
        current, wall_heat = advance(
            extended,
            lax.dynamic_slice_in_dim(padded_tags, first_column + 2, columns, 0),
            vel_x,
            vel_y,
            vel_z,
            tables,
        )
    return (current, wall_heat)


def solution(mesh):
    placed = (P("vel", "space", None), P("vel"), P())
    return jax.shard_map(
        body,
        mesh=mesh,
        in_specs=placed,
        out_specs=(P("vel", "space", None), P("space", None, None)),
        check_vma=False,
    )
```

profile of v0, /device:TPU:4, one launch (start us, length us, event | category | flops | bytes accessed | tf_op | source)
XLA Modules:
  0.0 447.4 jit_solution(4869679155041325200)
XLA Ops:
  0.6 4.7 %fusion.175 = (f32[864,1,256]{2,1,0:T(1,128)S(1)}, f32[864,1,256]{2,1,0:T(1,128)S(1)}) fusion(f32[864,4,256]{2,1,0:T(4,128)} %param.3), kind=kLoop, calls=%fused_computation.308 | loop fusion | bytes 3538944 | tf_op jit(solution)/shard_map/slice | solution.py:28
  6.4 8.5 %collective-permute-start.1 = (f32[864,1,256]{2,0,1:T(8,128)}, f32[864,1,256]{2,0,1:T(8,128)}, u32[]{:S(2)}, u32[]{:S(2)}) collective-permute-start(f32[864,1,256]{2,0,1:T(8,128)} %copy.107), channel_id=1, source_target_pairs={{1,0},{2,1},{3,2},{4,3},{5,4},{6,5},{7,6},{8,7},{9,8},{10,9},{11,1... | collective-permute-start | bytes 2654216 | tf_op jit(solution)/shard_map/ppermute | solution.py:33
  21.7 23.8 %slice.191 = f32[864,4,32]{2,1,0:T(4,128)} slice(f32[864,4,256]{2,1,0:T(4,128)S(1)} %copy-done.4), slice={[0:864:1], [0:4:1], [0:256:8]} | slice | bytes 884736 | tf_op jit(solution)/shard_map/slice | solution.py:91
  45.5 24.0 %slice.192 = f32[864,4,32]{2,1,0:T(4,128)} slice(f32[864,4,256]{2,1,0:T(4,128)S(1)} %copy-done.4), slice={[0:864:1], [0:4:1], [7:256:8]} | slice | bytes 884736 | tf_op jit(solution)/shard_map/slice | solution.py:92
  69.6 3.9 copy.95
  92.2 2.1 multiply_reduce_fusion
  96.9 2.5 copy.82
  99.5 2.5 copy.83
  108.4 2.6 copy.108
  111.8 3.8 fusion.124
  115.6 43.4 %psum.43 = f32[5,1024]{1,0:T(8,128)S(1)} all-reduce(f32[5,1024]{1,0:T(8,128)S(1)} %fusion.124), channel_id=1, replica_groups=mesh['vel'=16,'space'=16] {'vel'}, use_global_device_ids=true, to_apply=%region_4.5 | all-reduce | flops 5120 | bytes 40960 | tf_op jit(solution)/shard_map/psum | solution.py:229
  160.4 4.2 fusion.22
  164.7 50.8 %all-reduce.1 = (f32[3,1024]{1,0:T(4,128)S(1)}, f32[2,2,4,32]{3,2,0,1:T(4,128)S(1)}) all-reduce(f32[3,1024]{1,0:T(4,128)S(1)} %pad_maximum_fusion.4, f32[2,2,4,32]{3,2,0,1:T(4,128)S(1)} %copy-done.20), channel_id=1, replica_groups=mesh['vel'=16,'space'=16] {'vel'}, use_global_device_ids=true, to_apply=%region_8.9 | all-reduce | flops 3584 | bytes 28672 | tf_op jit(solution)/shard_map/psum | solution.py:239
  220.5 5.5 %fusion.173 = (f32[864,4,248]{0,2,1:T(8,128)S(1)}, f32[864,4,248]{0,2,1:T(8,128)}) fusion(f32[864,4,256]{0,2,1:T(8,128)} %copy.95), kind=kLoop, calls=%fused_computation.306 | loop fusion | bytes 13713408 | tf_op jit(solution)/shard_map/jit(_roll_static)/slice | solution.py:192
  226.0 3.6 fusion.171
  229.7 2.4 copy.74
  232.1 2.4 copy.69
  234.5 13.7 %fusion.17 = f32[864,4,256]{0,2,1:T(8,128)S(1)} fusion(f32[864,4,256]{0,2,1:T(8,128)} %copy.95, f32[864,1,256]{0,2,1:T(8,128)} %copy.74, f32[864,1,256]{0,2,1:T(8,128)} %copy.69, f32[864,4,248]{0,2,1:T(8,128)} %get-tuple-element.76, f32[864,4,8]{0,2,1:T(8,128)} %get-tuple-element.78, f32[864,4,8]{0,2,1:T(8,128)} %get-tuple-element.77, ...), kind=kLoop, calls=%fused_computation.41 | loop fusion | flops 46891008 | bytes 23964544 | tf_op jit(solution)/shard_map/add | solution.py:220
  250.7 2.8 slice.220
  253.5 2.8 slice.221
  258.9 3.1 fusion.122
  262.0 52.9 %psum.46 = f32[5,1024]{1,0:T(8,128)S(1)} all-reduce(f32[5,1024]{1,0:T(8,128)S(1)} %fusion.122), channel_id=1, replica_groups=mesh['vel'=16,'space'=16] {'vel'}, use_global_device_ids=true, to_apply=%region_10.11 | all-reduce | flops 5120 | bytes 40960 | tf_op jit(solution)/shard_map/psum | solution.py:229
  315.1 4.2 fusion.47
  321.9 53.1 %all-reduce = (f32[3,1024]{1,0:T(4,128)S(1)}, f32[2,2,4,32]{3,2,0,1:T(4,128)S(1)}) all-reduce(f32[3,1024]{1,0:T(4,128)S(1)} %pad_maximum_fusion.5, f32[2,2,4,32]{3,2,0,1:T(4,128)S(1)} %copy.102), channel_id=1, replica_groups=mesh['vel'=16,'space'=16] {'vel'}, use_global_device_ids=true, to_apply=%region_14.15 | all-reduce | flops 3584 | bytes 28672 | tf_op jit(solution)/shard_map/psum | solution.py:239
  379.9 6.0 %collective-permute-start.3 = (f32[864,1,256]{2,0,1:T(8,128)}, f32[864,1,256]{2,0,1:T(8,128)}, u32[]{:S(2)}, u32[]{:S(2)}) collective-permute-start(f32[864,1,256]{2,0,1:T(8,128)} %copy.100), channel_id=1, source_target_pairs={{1,0},{2,1},{3,2},{4,3},{5,4},{6,5},{7,6},{8,7},{9,8},{10,9},{11,1... | collective-permute-start | bytes 2654216 | tf_op jit(solution)/shard_map/ppermute | solution.py:33
  387.0 5.4 %fusion.168 = (f32[864,4,248]{0,2,1:T(8,128)S(1)}, f32[864,4,248]{0,2,1:T(8,128)}) fusion(f32[864,4,256]{0,2,1:T(8,128)} %copy-done), kind=kLoop, calls=%fused_computation.301 | loop fusion | bytes 13713408 | tf_op jit(solution)/shard_map/jit(_roll_static)/slice | solution.py:192
  392.5 3.6 fusion.166
  396.1 27.0 %collective-permute-done.3 = f32[864,1,256]{2,0,1:T(8,128)} collective-permute-done((f32[864,1,256]{2,0,1:T(8,128)}, f32[864,1,256]{2,0,1:T(8,128)}, u32[]{:S(2)}, u32[]{:S(2)}) %collective-permute-start.3) | collective-permute-done | bytes 884768 | tf_op jit(solution)/shard_map/ppermute | solution.py:33
  423.2 2.4 copy.101
  425.6 2.4 copy.99
  428.0 14.4 %fusion.42 = f32[864,4,256]{0,2,1:T(8,128)} fusion(f32[864,4,256]{0,2,1:T(8,128)} %copy-done, f32[864,1,256]{0,2,1:T(8,128)} %copy.101, f32[864,1,256]{0,2,1:T(8,128)} %copy.99, f32[864,4,248]{0,2,1:T(8,128)} %get-tuple-element.66, f32[864,4,8]{0,2,1:T(8,128)} %get-tuple-element.68, f32[864,4,8]{0,2,1:T(8,128)} %get-tuple-element.67, ...), kind=kLoop, calls=%fused_computation.66 | loop fusion | flops 46891008 | bytes 23964544 | tf_op jit(solution)/shard_map/add | solution.py:220
  442.4 5.0 %copy.104 = f32[864,4,256]{2,1,0:T(4,128)} copy(f32[864,4,256]{0,2,1:T(8,128)} %fusion.42) | data formatting | bytes 7077888
  (164 shorter events, 56.3 us)
Async XLA Ops:
  0.6 21.1 %copy-start.4 = (f32[864,4,256]{2,1,0:T(4,128)S(1)}, f32[864,4,256]{2,1,0:T(4,128)}, u32[]{:S(2)}) copy-start(f32[864,4,256]{2,1,0:T(4,128)} %param.3) | copy-start | bytes 10616836
  0.6 16.3 %copy-start.19 = (s32[864]{0:T(1024)S(1)}, s32[864]{0:T(1024)}, u32[]{:S(2)}) copy-start(s32[864]{0:T(1024)} %param.4) | copy-start | bytes 10372
  6.4 223.3 %collective-permute-start.1 = (f32[864,1,256]{2,0,1:T(8,128)}, f32[864,1,256]{2,0,1:T(8,128)}, u32[]{:S(2)}, u32[]{:S(2)}) collective-permute-start(f32[864,1,256]{2,0,1:T(8,128)} %copy.107), channel_id=1, source_target_pairs={{1,0},{2,1},{3,2},{4,3},{5,4},{6,5},{7,6},{8,7},{9,8},{10,9},{11,1... | collective-permute-start | bytes 2654216 | tf_op jit(solution)/shard_map/ppermute | solution.py:33
  15.8 216.2 %collective-permute-start = (f32[864,1,256]{2,0,1:T(8,128)}, f32[864,1,256]{2,0,1:T(8,128)}, u32[]{:S(2)}, u32[]{:S(2)}) collective-permute-start(f32[864,1,256]{2,0,1:T(8,128)} %copy.106), channel_id=1, source_target_pairs={{0,1},{1,2},{2,3},{3,4},{4,5},{5,6},{6,7},{7,8},{8,9},{9,10},{10,1... | collective-permute-start | bytes 2654216 | tf_op jit(solution)/shard_map/ppermute | solution.py:31
  17.6 142.8 %copy-start.7 = (f32[864]{0:T(1024)}, f32[864]{0:T(1024)S(1)}, u32[]{:S(2)}) copy-start(f32[864]{0:T(1024)S(1)} %get-tuple-element.53) | copy-start | bytes 10372
  18.8 141.6 %copy-start.9 = (f32[864]{0:T(1024)}, f32[864]{0:T(1024)S(1)}, u32[]{:S(2)}) copy-start(f32[864]{0:T(1024)S(1)} %get-tuple-element.106) | copy-start | bytes 10372
  18.8 141.6 %copy-start.11 = (f32[864]{0:T(1024)}, f32[864]{0:T(1024)S(1)}, u32[]{:S(2)}) copy-start(f32[864]{0:T(1024)S(1)} %get-tuple-element.107) | copy-start | bytes 10372
  18.8 199.9 %copy-start.13 = (f32[864]{0:T(1024)}, f32[864]{0:T(1024)S(1)}, u32[]{:S(2)}) copy-start(f32[864]{0:T(1024)S(1)} %get-tuple-element.101) | copy-start | bytes 10372
  111.7 52.9 %copy-start.5 = (f32[5,864]{1,0:T(8,128)}, f32[5,864]{1,0:T(8,128)S(1)}, u32[]{:S(2)}) copy-start(f32[5,864]{1,0:T(8,128)S(1)} %stack.90) | copy-start | bytes 51844
  111.7 53.0 %copy-start.20 = (f32[2,2,4,32]{3,2,0,1:T(4,128)S(1)}, f32[2,2,4,32]{3,2,0,1:T(4,128)}, u32[]{:S(2)}) copy-start(f32[2,2,4,32]{3,2,0,1:T(4,128)} %copy.84) | copy-start | bytes 6148
  111.7 105.6 %copy-start.29 = (s32[4,2,32]{2,0,1:T(4,128)S(1)}, s32[4,2,32]{2,0,1:T(4,128)}, u32[]{:S(2)}) copy-start(s32[4,2,32]{2,0,1:T(4,128)} %copy.85) | copy-start | bytes 3076
  111.8 105.6 %copy-start.31 = (f32[2,3]{1,0:T(2,128)S(1)}, f32[2,3]{1,0:T(2,128)}, u32[]{:S(2)}) copy-start(f32[2,3]{1,0:T(2,128)} %copy.103) | copy-start | bytes 76
  111.8 105.6 %copy-start.32 = (f32[2,3]{1,0:T(2,128)S(1)}, f32[2,3]{1,0:T(2,128)}, u32[]{:S(2)}) copy-start(f32[2,3]{1,0:T(2,128)} %copy.88) | copy-start | bytes 76
  111.8 105.6 %copy-start.33 = (f32[2,3]{1,0:T(2,128)S(1)}, f32[2,3]{1,0:T(2,128)}, u32[]{:S(2)}) copy-start(f32[2,3]{1,0:T(2,128)} %get-tuple-element.114) | copy-start | bytes 76
  220.5 5.5 %copy-start.3 = (f32[864,4,256]{0,2,1:T(8,128)S(1)}, f32[864,4,256]{0,2,1:T(8,128)}, u32[]{:S(2)}) copy-start(f32[864,4,256]{0,2,1:T(8,128)} %copy.95) | copy-start | bytes 10616836
  248.2 9.9 %copy-start.6 = (f32[5,864]{1,0:T(8,128)S(1)}, f32[5,864]{1,0:T(8,128)}, u32[]{:S(2)}) copy-start(f32[5,864]{1,0:T(8,128)} %copy-done.5) | copy-start | bytes 51844
  256.3 58.8 %copy-start.8 = (f32[864]{0:T(1024)S(1)}, f32[864]{0:T(1024)}, u32[]{:S(2)}) copy-start(f32[864]{0:T(1024)} %copy-done.7) | copy-start | bytes 10372
  256.3 58.8 %copy-start.10 = (f32[864]{0:T(1024)S(1)}, f32[864]{0:T(1024)}, u32[]{:S(2)}) copy-start(f32[864]{0:T(1024)} %copy-done.9) | copy-start | bytes 10372
  256.3 58.8 %copy-start.12 = (f32[864]{0:T(1024)S(1)}, f32[864]{0:T(1024)}, u32[]{:S(2)}) copy-start(f32[864]{0:T(1024)} %copy-done.11) | copy-start | bytes 10372
  258.9 61.8 %copy-start.22 = (f32[1,864]{1,0:T(1,128)S(1)}, f32[1,864]{1,0:T(1,128)}, u32[]{:S(2)}) copy-start(f32[1,864]{1,0:T(1,128)} %stack.78) | copy-start | bytes 10372
  258.9 61.8 %copy-start.24 = (f32[1,864]{1,0:T(1,128)S(1)}, f32[1,864]{1,0:T(1,128)}, u32[]{:S(2)}) copy-start(f32[1,864]{1,0:T(1,128)} %stack.79) | copy-start | bytes 10372
  258.9 62.3 %copy-start.21 = (f32[1,864]{1,0:T(1,128)S(1)}, f32[1,864]{1,0:T(1,128)}, u32[]{:S(2)}) copy-start(f32[1,864]{1,0:T(1,128)} %stack.81) | copy-start | bytes 10372
  258.9 62.3 %copy-start.23 = (f32[1,864]{1,0:T(1,128)S(1)}, f32[1,864]{1,0:T(1,128)}, u32[]{:S(2)}) copy-start(f32[1,864]{1,0:T(1,128)} %stack.82) | copy-start | bytes 10372
  258.9 116.8 %copy-start.18 = (f32[4,2,32]{2,0,1:T(4,128)S(1)}, f32[4,2,32]{2,0,1:T(4,128)}, u32[]{:S(2)}) copy-start(f32[4,2,32]{2,0,1:T(4,128)} %copy-done.17) | copy-start | bytes 3076
  258.9 116.8 %copy-start.30 = (f32[4,2,32]{2,0,1:T(4,128)S(1)}, f32[4,2,32]{2,0,1:T(4,128)}, u32[]{:S(2)}) copy-start(f32[4,2,32]{2,0,1:T(4,128)} %get-tuple-element.38) | copy-start | bytes 3076
  258.9 117.4 %copy-start.16 = (f32[4,2,32]{2,0,1:T(4,128)S(1)}, f32[4,2,32]{2,0,1:T(4,128)}, u32[]{:S(2)}) copy-start(f32[4,2,32]{2,0,1:T(4,128)} %copy-done.15) | copy-start | bytes 3076
  315.1 70.8 %copy-start.14 = (f32[864]{0:T(1024)S(1)}, f32[864]{0:T(1024)}, u32[]{:S(2)}) copy-start(f32[864]{0:T(1024)} %copy-done.13) | copy-start | bytes 10372
  315.1 70.7 %copy-start.26 = (f32[4,32]{1,0:T(4,128)S(1)}, f32[4,32]{1,0:T(4,128)}, u32[]{:S(2)}) copy-start(f32[4,32]{1,0:T(4,128)} %copy-done.25) | copy-start | bytes 1540
  315.1 70.7 %copy-start.28 = (f32[4,32]{1,0:T(4,128)S(1)}, f32[4,32]{1,0:T(4,128)}, u32[]{:S(2)}) copy-start(f32[4,32]{1,0:T(4,128)} %copy-done.27) | copy-start | bytes 1540
  379.9 43.3 %collective-permute-start.3 = (f32[864,1,256]{2,0,1:T(8,128)}, f32[864,1,256]{2,0,1:T(8,128)}, u32[]{:S(2)}, u32[]{:S(2)}) collective-permute-start(f32[864,1,256]{2,0,1:T(8,128)} %copy.100), channel_id=1, source_target_pairs={{1,0},{2,1},{3,2},{4,3},{5,4},{6,5},{7,6},{8,7},{9,8},{10,9},{11,1... | collective-permute-start | bytes 2654216 | tf_op jit(solution)/shard_map/ppermute | solution.py:33
  385.9 39.7 %collective-permute-start.2 = (f32[864,1,256]{2,0,1:T(8,128)}, f32[864,1,256]{2,0,1:T(8,128)}, u32[]{:S(2)}, u32[]{:S(2)}) collective-permute-start(f32[864,1,256]{2,0,1:T(8,128)} %copy.98), channel_id=1, source_target_pairs={{0,1},{1,2},{2,3},{3,4},{4,5},{5,6},{6,7},{7,8},{8,9},{9,10},{10,1... | collective-permute-start | bytes 2654216 | tf_op jit(solution)/shard_map/ppermute | solution.py:31
  387.0 5.4 %copy-start.2 = (f32[864,4,256]{0,2,1:T(8,128)S(1)}, f32[864,4,256]{0,2,1:T(8,128)}, u32[]{:S(2)}) copy-start(f32[864,4,256]{0,2,1:T(8,128)} %copy-done) | copy-start | bytes 10616836
  (6 other events, 6.7 us)
where the time goes:
time: 456 us; the launch traced here: 447 us
  blocking collectives  200 us (44%)
  local copies, waits for them, and re-layouts  140 us (31%)
  other arithmetic  53.5 us (12%)
  waiting for transfers between devices  27 us (6%)
  starting transfers between devices  14.5 us (3%)
  matrix products  11 us (2%)
    psum x2, blocking collectives, advance(): lax.psum(heat_terms(centre, vel_x, vel_y, vel_z, mean_flow_first, mean_fl...  104 us
    psum x2, blocking collectives, advance(): lax.psum((block_moments(centre, vel_x, vel_y, vel_z), wall_local), 'vel')  96.3 us
    slice x3, local copies, waits for them, and re-layouts, block_walls(): top_layer = centre[:, :, depth - 1::depth].reshape(number, -1)  29.4 us
    slice x3, local copies, waits for them, and re-layouts, block_walls(): bottom = centre[:, :, 0::depth].reshape(number, -1)  29.1 us
    add x2, other arithmetic, relax(): centre - courant_ratio * transport_sum  28.1 us
    ppermute x2, waiting for transfers between devices, extended_2(): lax.ppermute(head, axis, [((i + 1) % count, i) for i in range(count)])  27 us
    unnamed x80, local copies, waits for them, and re-layouts  17.3 us
    ppermute x2, starting transfers between devices, extended_2(): lax.ppermute(head, axis, [((i + 1) % count, i) for i in range(count)])  14.4 us
  transfers between devices with their start and end apart: 4, of which 1 were waited for; matrix products, arithmetic and copies ran while one was open for 30% of the time, Pallas kernels for 0%

commit v1 on v0

v1 whole, which is shorter than its diff:
```python
import math

import jax
import jax.numpy as jnp
import numpy as np
from jax import lax
from jax.experimental import pallas as pl
from jax.experimental.pallas import tpu as pltpu
from jax.sharding import PartitionSpec as P

NV1 = 24
NSLOT = 864
NPAD = 896
CELLS = 1024
COL = 256
SPACING = 12.0 / NV1
TOP = (NV1 - 1) * 0.5 * SPACING
KD = 0.3 / TOP
DT = 0.3 / (8 * TOP)
WEIGHT = SPACING**3 / (2.0 * math.pi) ** 1.5
LOG2E = 1.0 / math.log(2.0)
WALL_T = [[b * (0.7 + 0.3 * level) for level in range(3)] for b in (1.4, 0.7)]
AXES = ("vel", "space")
F32 = jnp.float32
BF16 = jnp.bfloat16


def wall_norms():
    line = (2 * np.arange(NV1) - (NV1 - 1)) * 0.5 * SPACING
    cx, cy, cz = np.meshgrid(line, line, line, indexing="ij")
    sq = cx**2 + cy**2 + cz**2
    mass, energy = [], []
    for side in range(2):
        out = np.maximum(cz if side == 0 else -cz, 0.0) * WEIGHT
        prof = [out * t**-1.5 * np.exp(-sq / (2.0 * t)) for t in WALL_T[side]]
        mass.append([float(p.sum()) for p in prof])
        energy.append([float((p * 0.5 * sq).sum()) for p in prof])
    return mass, energy


MASS, ENERGY = wall_norms()


def device_of(i):
    v, s = divmod(i, 16)
    x, r = divmod(v, 4)
    return x, r >> 1, r & 1, s


def index_of(x, y, core, s):
    return ((x % 4 * 2 + y % 2) * 2 + core % 2) * 16 + s % 16


def permute(value, move):
    return lax.ppermute(value, AXES, [(i, index_of(*move(*device_of(i)))) for i in range(256)])


def downstream(value):
    return permute(value, lambda x, y, c, s: (x, y, c, s - 1 if x < 2 else s + 1))


def reduce_vel(part):
    core = permute(part, lambda x, y, c, s: (x, y, c ^ 1, s))
    near = permute(part, lambda x, y, c, s: (x, y ^ 1, c, s))
    both = permute(part, lambda x, y, c, s: (x, y ^ 1, c ^ 1, s))
    part = (part + core) + (near + both)
    one = permute(part, lambda x, y, c, s: (x + 1, y, c, s))
    three = permute(part, lambda x, y, c, s: (x - 1, y, c, s))
    two = permute(part, lambda x, y, c, s: (x + 2, y, c, s))
    return (part + two) + (one + three)


def upstream_first():
    return (lax.axis_index("vel") >= 8).astype(jnp.int32)


def column_of(forward, i):
    return jnp.where(forward == 1, i, 3 - i)


def spec():
    return pl.BlockSpec(memory_space=pltpu.VMEM)


def smem():
    return pl.BlockSpec(memory_space=pltpu.SMEM)


def params():
    return pltpu.CompilerParams(vmem_limit_bytes=48 * 2**20)


def shape(*dims, dtype=F32):
    return jax.ShapeDtypeStruct(dims, dtype)


def unpack_kernel(dir_ref, in_ref, h_ref, near_ref, far_ref):
    rows = h_ref.shape[0]
    forward = dir_ref[0]
    for i in range(4):
        col = column_of(forward, i)
        for half in range(2):
            part = in_ref[pl.ds(half * 4 + col, rows, stride=8), :]
            h_ref[:, pl.ds(i * COL + half * 128, 128)] = part
            if i == 3:
                near_ref[:, pl.ds(half * 128, 128)] = part
            if i == 2:
                far_ref[:, pl.ds(half * 128, 128)] = part


def unpack(forward, flat):
    rows = 96
    return pl.pallas_call(
        unpack_kernel,
        grid=(NSLOT // rows,),
        in_specs=[smem(), pl.BlockSpec((rows * 8, 128), lambda i: (i, 0))],
        out_specs=[
            pl.BlockSpec((rows, CELLS), lambda i: (i, 0)),
            pl.BlockSpec((rows, COL), lambda i: (i, 0)),
            pl.BlockSpec((rows, COL), lambda i: (i, 0)),
        ],
        out_shape=[shape(NSLOT, CELLS), shape(NSLOT, COL), shape(NSLOT, COL)],
        name="unpack",
    )(forward, flat)


def velocity_kernel(order_ref, left_ref, phi_ref, coef_ref, table):
    order = order_ref[...]
    upper = (order * 43691) >> 20
    kx = (upper * 43691) >> 20
    ky = upper - kx * NV1
    kz = order - upper * NV1
    live = (lax.broadcasted_iota(jnp.int32, (1, NPAD), 1) < NSLOT).astype(F32)

    def coordinate(k):
        return (2 * k - (NV1 - 1)).astype(F32) * (0.5 * SPACING) * live

    cx, cy, cz = coordinate(kx), coordinate(ky), coordinate(kz)
    sq = cx * cx + cy * cy + cz * cz
    zero = jnp.zeros_like(cx)
    down, up = jnp.maximum(-cz, 0.0), jnp.maximum(cz, 0.0)
    phi = [live, cx, cy, cz, cx * cx, cy * cy, cz * cz, cx * cy, cx * cz, cy * cz, cx * sq, cy * sq, cz * sq]
    sums = phi + [down, down * (0.5 * sq), zero] + [zero] * 5 + [up, up * (0.5 * sq), zero]

    def high(a):
        return a.astype(BF16).astype(F32)

    for r, a in enumerate(sums):
        table[pl.ds(r, 1), :] = high(a)
        table[pl.ds(24 + r, 1), :] = a - high(a)
    left_ref[...] = table[pl.ds(0, 48), :].astype(BF16)
    ghost = []
    for side, out in ((0, up), (1, down)):
        ghost += [out * KD * jnp.exp(sq * (-0.5 / t)) for t in WALL_T[side]]
    rows = []
    for _ in range(3):
        rows += [high(a) for a in phi] + [zero] * 3
    for _ in range(2):
        rows += [a - high(a) for a in phi] + [zero] * 3
    rows += [high(a) for a in ghost] + [high(a - high(a)) for a in ghost] + [zero] * 4
    rows += [high(a) for a in ghost] + [zero] * 10
    rows += [jnp.abs(cx), jnp.maximum(cy, 0.0), jnp.maximum(-cy, 0.0), up, down]
    rows += [jnp.abs(cx) + jnp.abs(cy) + jnp.abs(cz)] + [zero] * 10
    for r, a in enumerate(rows):
        table[pl.ds(r, 1), :] = a
    turned = table[...].T.astype(BF16)
    phi_ref[...] = turned[:NSLOT]
    row = lax.broadcasted_iota(jnp.int32, (128, 768), 0)
    lane = lax.broadcasted_iota(jnp.int32, (128, 768), 1)
    kind, z = lane >> 7, lane & 7
    drop = ((kind == 3) & (z == 0)) | ((kind == 4) & (z == 7))
    pick = ((row == 112 + kind) & jnp.logical_not(drop)).astype(F32).astype(BF16)
    coef_ref[...] = jnp.dot(turned, pick, preferred_element_type=F32)[:NSLOT] * KD


def velocities(order):
    return pl.pallas_call(
        velocity_kernel,
        in_specs=[spec()],
        out_specs=[spec()] * 3,
        out_shape=[shape(48, NPAD, dtype=BF16), shape(NSLOT, 128, dtype=BF16), shape(NSLOT, 768)],
        scratch_shapes=[pltpu.VMEM((128, NPAD), F32)],
        compiler_params=params(),
        name="velocities",
    )(order)


def clear_tail(high_ref, low_ref):
    tail = jnp.zeros((NPAD - NSLOT, high_ref.shape[1]), BF16)
    high_ref[pl.ds(NSLOT, NPAD - NSLOT), :] = tail
    low_ref[pl.ds(NSLOT, NPAD - NSLOT), :] = tail


def put_moments(forward, left_ref, high_ref, low_ref, out_ref):
    left = left_ref[...]
    sub = lax.broadcasted_iota(jnp.int32, (8, 128), 0)
    lane = lax.broadcasted_iota(jnp.int32, (8, 128), 1)
    top = (sub >= 5) & ((lane & 7) >= 4)
    for i in range(4):
        cols = pl.ds(i * COL, COL)
        first = jnp.dot(left, high_ref[:, cols], preferred_element_type=F32)
        second = jnp.dot(left, low_ref[:, cols], preferred_element_type=F32)
        total = first + second
        total = total[:24] + total[24:]
        col = column_of(forward, i)
        for half in range(2):
            part = total[:, half * 128 : half * 128 + 128]
            mid = jnp.where(top, part[16:24], part[8:16])
            out_ref[pl.ds(col * 2 + half, 8, stride=8), :] = part[0:8]
            out_ref[pl.ds(64 + col * 2 + half, 8, stride=8), :] = mid


def split_into(value, rows, cols, high_ref, low_ref):
    high = value.astype(BF16)
    high_ref[rows, cols] = high
    low_ref[rows, cols] = (value - high.astype(F32)).astype(BF16)


def moment_kernel(dir_ref, h_ref, left_ref, out_ref, high_ref, low_ref):
    clear_tail(high_ref, low_ref)

    def body(k, carry):
        rows = pl.ds(pl.multiple_of(k * 48, 16), 48)
        for b in range(8):
            cols = pl.ds(b * 128, 128)
            split_into(h_ref[rows, cols], rows, cols, high_ref, low_ref)
        return carry

    lax.fori_loop(0, NSLOT // 48, body, 0)
    put_moments(dir_ref[0], left_ref, high_ref, low_ref, out_ref)


def moments(forward, h, left):
    return pl.pallas_call(
        moment_kernel,
        in_specs=[smem(), spec(), spec()],
        out_specs=spec(),
        out_shape=shape(128, 128),
        scratch_shapes=[pltpu.VMEM((NPAD, CELLS), BF16)] * 2,
        compiler_params=params(),
        name="moments",
    )(forward, h, left)


def field_kernel(columns, dir_ref, m_ref, tag_ref, right_ref, keep_ref, heat_ref, table):
    m = [m_ref[pl.ds(f * 8, 8), :] * WEIGHT for f in range(15)]
    rho = m[0]
    inv = 1.0 / rho
    u = [a * inv for a in m[1:4]]
    energy = m[4] + m[5] + m[6]
    usq = u[0] * u[0] + u[1] * u[1] + u[2] * u[2]
    temp = (energy * inv - usq) * (1.0 / 3.0)
    stress = [[m[4], m[7], m[8]], [m[7], m[5], m[9]], [m[8], m[9], m[6]]]
    q = []
    for i in range(3):
        pu = stress[i][0] * u[0] + stress[i][1] * u[1] + stress[i][2] * u[2]
        q.append(0.5 * (m[10 + i] - 2.0 * pu - u[i] * energy + 2.0 * rho * usq * u[i]))
    log_t = jnp.log(temp)
    inv_t = 1.0 / temp
    rate = (DT / 0.05) * rho * jnp.exp(0.19 * log_t)
    amp = rate * rho * jnp.exp(-1.5 * log_t)
    half = (0.5 * LOG2E) * inv_t
    zero = jnp.zeros_like(rho)
    expo = [-half * usq] + [2.0 * half * a for a in u] + [-half] * 3 + [zero] * 9
    scale = inv * inv_t * inv_t * (1.0 / 15.0)
    a = [b * scale for b in q]
    s0 = u[0] * a[0] + u[1] * a[1] + u[2] * a[2]
    s1 = usq * inv_t - 5.0
    poly = [amp * (1.0 - s0 * s1)]
    poly += [amp * (a[i] * s1 + 2.0 * s0 * u[i] * inv_t) for i in range(3)]
    front = amp * inv_t
    poly += [-front * (2.0 * a[i] * u[i] + s0) for i in range(3)]
    poly += [-2.0 * front * (a[i] * u[j] + a[j] * u[i]) for i, j in ((0, 1), (0, 2), (1, 2))]
    poly += [front * a[i] for i in range(3)] + [zero] * 3
    z = lax.broadcasted_iota(jnp.int32, (8, 128), 1) & 7
    tag = tag_ref[...]
    density, heat = zero, zero
    walls = []
    for side, at in ((0, 0), (1, 7)):
        for level in range(3):
            here = (z == at) & (tag == level)
            n = jnp.where(here, m[13] * (1.0 / MASS[side][level]), 0.0)
            heat = jnp.where(here, n * ENERGY[side][level] - m[14], heat)
            walls.append(n * WALL_T[side][level] ** -1.5)
    heat_ref[...] = heat
    for r, c in enumerate(expo + poly + walls + [zero] * 10):
        table[pl.ds(r * 8, 8), :] = c
    keep = 1.0 - rate
    table[pl.ds(384, 8), :] = keep
    forward = dir_ref[0]
    n = len(columns)
    right_ref[...] = jnp.zeros(right_ref.shape, BF16)

    def pieces(value, count):
        out = []
        for _ in range(count):
            piece = value.astype(BF16)
            out.append(piece)
            value = value - piece.astype(F32)
        return out

    for k, i in enumerate(columns):
        col = column_of(forward, i)
        for hf in range(2):
            j = col * 2 + hf
            at = k * COL + hf * 128
            keep_ref[pl.ds(k * 2 + hf, 1), :] = table[pl.ds(384 + j, 1), :]
            for kind in range(2):
                lanes = pl.ds(kind * n * COL + at, 128)
                first, second, third = pieces(table[pl.ds(kind * 128 + j, 16, stride=8), :], 3)
                for g, piece in enumerate((first, second, third, first, second)):
                    right_ref[pl.ds(g * 16, 16), lanes] = piece
            wall = table[pl.ds(256 + j, 16, stride=8), :]
            twice = table[pl.ds(256 + j, 6, stride=8), :]
            twice = jnp.concatenate([twice, twice, jnp.zeros((4, 128), F32)], axis=0)
            lanes = pl.ds(2 * n * COL + at, 128)
            right_ref[pl.ds(80, 16), lanes] = pieces(twice, 1)[0]
            right_ref[pl.ds(96, 16), lanes] = pieces(wall, 2)[1]


def fields(forward, m, tags, columns):
    n = len(columns)

    def kernel(*refs):
        field_kernel(columns, *refs)

    return pl.pallas_call(
        kernel,
        in_specs=[smem(), spec(), spec()],
        out_specs=[spec()] * 3,
        out_shape=[shape(128, 3 * n * COL, dtype=BF16), shape(2 * n, 128), shape(8, 128)],
        scratch_shapes=[pltpu.VMEM((392, 128), F32)],
        compiler_params=params(),
        name="fields",
    )(forward, m, tags)


def products(n, phi_ref, right_ref, prod):
    phi = phi_ref[...]
    for k in range(3 * n):
        cols = pl.ds(k * COL, COL)
        prod[:, cols] = jnp.dot(phi, right_ref[:, cols], preferred_element_type=F32)


def updated(n, i, rows, coefs, h, upwind, keep, prod):
    cx, cyp, cym, czp, czm, spill = coefs
    lane = lax.broadcasted_iota(jnp.int32, (1, 128), 1)
    plus = [pltpu.roll(a, 8, 1) for a in h]
    minus = [pltpu.roll(a, 120, 1) for a in h]
    out = []
    for hf in range(2):
        at = i * COL + hf * 128
        before = jnp.where(lane < 8, plus[1 - hf], plus[hf])
        after = jnp.where(lane >= 120, minus[1 - hf], minus[hf])
        expo = prod[rows, pl.ds(at, 128)]
        poly = prod[rows, pl.ds(n * COL + at, 128)]
        ghost = prod[rows, pl.ds(2 * n * COL + at, 128)]
        new = jnp.exp2(expo) * poly + ghost
        new = new + h[hf] * (keep[2 * i + hf] - spill)
        new = new + (cyp * before + cym * after)
        new = new + (czp * pltpu.roll(h[hf], 1, 1) + czm * pltpu.roll(h[hf], 127, 1))
        if upwind is not None:
            new = new + cx * upwind[hf]
        out.append(new)
    return out


def read_coefs(coef_ref, rows):
    return [coef_ref[rows, pl.ds(c * 128, 128)] for c in range(6)]


def first_kernel(dir_ref, h_ref, halo_ref, right_ref, keep_ref, phi_ref, coef_ref, left_ref, out_ref, m_ref, prod, high_ref, low_ref):
    clear_tail(high_ref, low_ref)
    products(4, phi_ref, right_ref, prod)
    step = 16

    def body(k, carry):
        rows = pl.ds(pl.multiple_of(k * step, step), step)
        coefs = read_coefs(coef_ref, rows)
        keep = [keep_ref[pl.ds(b, 1), :] for b in range(8)]
        upwind = [halo_ref[rows, pl.ds(hf * 128, 128)] for hf in range(2)]
        for i in range(4):
            h = [h_ref[rows, pl.ds(i * COL + hf * 128, 128)] for hf in range(2)]
            new = updated(4, i, rows, coefs, h, upwind, keep, prod)
            for hf in range(2):
                cols = pl.ds(i * COL + hf * 128, 128)
                out_ref[rows, cols] = new[hf]
                split_into(new[hf], rows, cols, high_ref, low_ref)
            upwind = h
        return carry

    lax.fori_loop(0, NSLOT // step, body, 0)
    put_moments(dir_ref[0], left_ref, high_ref, low_ref, m_ref)


def first_step(forward, h, halo, right, keep, phi, coef, left):
    return pl.pallas_call(
        first_kernel,
        in_specs=[smem()] + [spec()] * 7,
        out_specs=[spec()] * 2,
        out_shape=[shape(NSLOT, CELLS), shape(128, 128)],
        scratch_shapes=[pltpu.VMEM((NSLOT, 3 * CELLS), F32)] + [pltpu.VMEM((NPAD, CELLS), BF16)] * 2,
        compiler_params=params(),
        name="first_step",
    )(forward, h, halo, right, keep, phi, coef, left)


def edge_kernel(halo_ref, right_ref, keep_ref, phi_ref, coef_ref, out_ref, prod):
    products(1, phi_ref, right_ref, prod)
    step = 16

    def body(k, carry):
        rows = pl.ds(pl.multiple_of(k * step, step), step)
        coefs = read_coefs(coef_ref, rows)
        keep = [keep_ref[pl.ds(b, 1), :] for b in range(2)]
        h = [halo_ref[rows, pl.ds(hf * 128, 128)] for hf in range(2)]
        new = updated(1, 0, rows, coefs, h, None, keep, prod)
        for hf in range(2):
            out_ref[rows, pl.ds(hf * 128, 128)] = new[hf]
        return carry

    lax.fori_loop(0, NSLOT // step, body, 0)


def edge_step(halo, right, keep, phi, coef):
    return pl.pallas_call(
        edge_kernel,
        in_specs=[spec()] * 5,
        out_specs=spec(),
        out_shape=shape(NSLOT, COL),
        scratch_shapes=[pltpu.VMEM((NSLOT, 3 * COL), F32)],
        compiler_params=params(),
        name="edge_step",
    )(halo, right, keep, phi, coef)


def last_kernel(dir_ref, h_ref, edge_ref, far_ref, right_ref, keep_ref, phi_ref, coef_ref, out_ref, prod):
    products(4, phi_ref, right_ref, prod)
    step = 16
    forward = dir_ref[0]

    def body(k, carry):
        rows = pl.ds(pl.multiple_of(k * step, step), step)
        coefs = read_coefs(coef_ref, rows)
        keep = [keep_ref[pl.ds(b, 1), :] for b in range(8)]
        upwind = [
            edge_ref[rows, pl.ds(hf * 128, 128)] + coefs[0] * far_ref[rows, pl.ds(hf * 128, 128)] for hf in range(2)
        ]
        for i in range(4):
            h = [h_ref[rows, pl.ds(i * COL + hf * 128, 128)] for hf in range(2)]
            new = updated(4, i, rows, coefs, h, upwind, keep, prod)
            for hf in range(2):
                out_ref[pl.ds(k * (8 * step) + hf * 4 + column_of(forward, i), step, stride=8), :] = new[hf]
            upwind = h
        return carry

    lax.fori_loop(0, NSLOT // step, body, 0)


def last_step(forward, h, edge, far, right, keep, phi, coef):
    return pl.pallas_call(
        last_kernel,
        in_specs=[smem()] + [spec()] * 7,
        out_specs=spec(),
        out_shape=shape(NSLOT * 8, 128),
        scratch_shapes=[pltpu.VMEM((NSLOT, 3 * CELLS), F32)],
        compiler_params=params(),
        name="last_step",
    )(forward, h, edge, far, right, keep, phi, coef)


def body(state, velocity_order, wall_tag):
    forward = upstream_first()
    flag = forward.reshape(1)
    flat = state.reshape(NSLOT, 4, 2, 128).transpose(0, 2, 1, 3).reshape(NSLOT * 8, 128)
    h0, near, far = unpack(flag, flat)
    halo = downstream(near)
    far_halo = downstream(far)
    left, phi, coef = velocities(jnp.pad(velocity_order, (0, NPAD - NSLOT)).reshape(1, NPAD))

    s = lax.axis_index("space")
    spread = jnp.repeat(jnp.transpose(wall_tag, (0, 2, 1)), 4, axis=2).reshape(128, 128)
    tags = lax.dynamic_slice_in_dim(spread, s * 8, 8, 0)
    up = (s + jnp.where(forward == 1, 15, 1)) % 16
    tags_up = lax.dynamic_slice_in_dim(spread, up * 8, 8, 0)

    m1 = reduce_vel(moments(flag, h0, left))
    m_up = downstream(m1)
    right, keep, _ = fields(flag, m1, tags, (0, 1, 2, 3))
    h1, part = first_step(flag, h0, halo, right, keep, phi, coef, left)
    m2 = reduce_vel(part)
    right_up, keep_up, _ = fields(flag, m_up, tags_up, (3,))
    edge = edge_step(halo, right_up, keep_up, phi, coef)
    right, keep, heat = fields(flag, m2, tags, (0, 1, 2, 3))
    out = last_step(flag, h1, edge, far_halo, right, keep, phi, coef)
    state_next = out.reshape(NSLOT, 2, 4, 128).transpose(0, 2, 1, 3).reshape(NSLOT, 4, 256)
    heat = heat.reshape(4, 32, 8)
    wall_heat = jnp.stack([heat[:, :, 0], heat[:, :, 7]], axis=1)
    return state_next, wall_heat


def solution(mesh):
    return jax.shard_map(
        body,
        mesh=mesh,
        in_specs=(P("vel", "space", None), P("vel"), P()),
        out_specs=(P("vel", "space", None), P("space", None, None)),
        check_vma=False,
    )
```

time: 456 us -> 117 us (0.26); the launches traced: 447 us -> 115 us
  blocking collectives: 200 us -> 0 us
  local copies, waits for them, and re-layouts: 140 us -> 23.4 us
  other arithmetic: 53.5 us -> 1.02 us
  Pallas kernels: 0 us -> 43.6 us
  starting transfers between devices: 14.5 us -> 42.5 us
  waiting for transfers between devices: 27 us -> 3.61 us
  matrix products: 11 us -> 0 us
    psum x4 -> x0, blocking collectives: 200 us -> none  [the longest x2 104 us: advance(): lax.psum(heat_terms(centre, vel_x, vel_y, vel_z, mean_flow_first, mean_fl...]
    slice x21 -> x1, local copies, waits for them, and re-layouts: 91.8 us -> 0.16 us  [body(): wall_heat = jnp.stack([heat[:, :, 0], heat[:, :, 7]], axis=1)]
    pallas_call x0 -> x9, Pallas kernels: none -> 43.6 us  [the longest x1 13.6 us: first_step(): pl.pallas_call(first_kernel, in_specs=[smem()] + [spec()] * 7, out_specs=...]
    ppermute x4 -> x15, starting transfers between devices: 14.5 us -> 42.5 us  [permute(): lax.ppermute(value, AXES, [(i, index_of(*move(*device_of(i)))) for i in r...]
    add x2 -> x4, other arithmetic: 28.1 us -> 1.01 us  [the longest x2 0.97 us: reduce_vel(): part = part + core + (near + both)]
    ppermute x4 -> x15, waiting for transfers between devices: 27 us -> 3.61 us  [permute(): lax.ppermute(value, AXES, [(i, index_of(*move(*device_of(i)))) for i in r...]
    reduce_sum x4 -> x0, other arithmetic: 11.3 us -> none  [the longest x2 8.45 us: heat_terms(): jnp.sum(rel_x * scaled, axis=0)]
    dot_general x6 -> x0, matrix products: 11 us -> none  [the longest x2 6.9 us: block_moments(): return jnp.dot(coefficients, centre.reshape(number, -1), precision=HIGHEST)]
  transfers between devices with their start and end apart: 4 -> 15, of which waited for: 1 -> 2; matrix products, arithmetic and copies ran while one was open for 30% -> 15% of each run, Pallas kernels for 0% -> 20%
where the time goes in v1:
time: 117 us; the launch traced here: 115 us
  Pallas kernels  43.6 us (37%)
  starting transfers between devices  42.5 us (36%)
  local copies, waits for them, and re-layouts  23.4 us (20%)
  waiting for transfers between devices  3.61 us (3%)
    ppermute x15, starting transfers between devices, permute(): lax.ppermute(value, AXES, [(i, index_of(*move(*device_of(i)))) for i in r...  42.5 us
    pallas_call x1, Pallas kernels, first_step(): pl.pallas_call(first_kernel, in_specs=[smem()] + [spec()] * 7, out_specs=...  13.6 us
    pallas_call x1, Pallas kernels, last_step(): pl.pallas_call(last_kernel, in_specs=[smem()] + [spec()] * 7, out_specs=s...  13.1 us
    unnamed x21, local copies, waits for them, and re-layouts  8.16 us
    pallas_call x1, Pallas kernels, unpack(): pl.pallas_call(unpack_kernel, grid=(NSLOT // rows,), in_specs=[smem(), pl...  7.23 us
    broadcast_in_dim x1, local copies, waits for them, and re-layouts, body(): jnp.repeat(jnp.transpose(wall_tag, (0, 2, 1)), 4, axis=2).reshape(128, 128)  6.61 us
    pallas_call x1, Pallas kernels, edge_step(): pl.pallas_call(edge_kernel, in_specs=[spec()] * 5, out_specs=spec(), out_...  5.26 us
    another operation x1, local copies, waits for them, and re-layouts, body(): jnp.repeat(jnp.transpose(wall_tag, (0, 2, 1)), 4, axis=2).reshape(128, 128)  5.12 us
  transfers between devices with their start and end apart: 15, of which 2 were waited for; matrix products, arithmetic and copies ran while one was open for 15% of the time, Pallas kernels for 20%

profile of v1, /device:TPU:4, one launch (start us, length us, event | category | flops | bytes accessed | tf_op | source)
XLA Modules:
  0.0 114.8 jit_solution(17890680041326152264)
XLA Ops:
  0.6 7.2 %unpack.1 = (f32[864,1024]{1,0:T(8,128)}, f32[864,256]{1,0:T(8,128)}, f32[864,256]{1,0:T(8,128)}) custom-call(s32[1]{0:T(128)} %bitcast.dir_ref.refs_0_, f32[6912,128]{1,0:T(8,128)} %bitcast.15), custom_call_target="tpu_custom_call" | custom-call | tf_op jit(solution)/shard_map/unpack/pallas_call | solution.py:113
  7.9 3.2 %collective-permute-start = (f32[864,256]{1,0:T(8,128)}, f32[864,256]{1,0:T(8,128)S(1)}, u32[]{:S(2)}, u32[]{:S(2)}) collective-permute-start(f32[864,256]{1,0:T(8,128)} %get-tuple-element.18), channel_id=1, source_target_pairs={{0,15},{1,0},{2,1},{3,2},{4,3},{5,4},{6,5},{7,6},{8,7},{9,8},{10,9... | collective-permute-start | bytes 2654216 | tf_op jit(solution)/shard_map/ppermute | solution.py:55
  11.1 0.8 velocities.1
  11.9 0.7 copy-done.3
  12.6 2.0 %copy-done = f32[864,1024]{1,0:T(8,128)S(1)} copy-done((f32[864,1024]{1,0:T(8,128)S(1)}, f32[864,1024]{1,0:T(8,128)}, u32[]{:S(2)}) %copy-start) | copy-done | bytes 3538968
  14.6 2.1 %moments.1 = f32[128,128]{1,0:T(8,128)} custom-call(s32[1]{0:T(128)} %bitcast.dir_ref.refs_0_, f32[864,1024]{1,0:T(8,128)S(1)} %copy-done, bf16[48,896]{1,0:T(8,128)(2,1)S(1)} %get-tuple-element.19.left_ref), custom_call_target="tpu_custom_call" | custom-call | tf_op jit(solution)/shard_map/moments/pallas_call | solution.py:234
  16.7 0.7 collective-permute-start.2
  17.4 1.2 %collective-permute-start.3 = (f32[128,128]{1,0:T(8,128)}, f32[128,128]{1,0:T(8,128)}, u32[]{:S(2)}, u32[]{:S(2)}) collective-permute-start(f32[128,128]{1,0:T(8,128)} %moments.1), channel_id=1, source_target_pairs={{0,48},{1,49},{2,50},{3,51},{4,52},{5,53},{6,54},{7,55},{8,56},{9,... | collective-permute-start | bytes 196616 | tf_op jit(solution)/shard_map/ppermute | solution.py:55
  18.6 2.2 %collective-permute-start.8 = (f32[864,256]{1,0:T(8,128)}, f32[864,256]{1,0:T(8,128)}, u32[]{:S(2)}, u32[]{:S(2)}) collective-permute-start(f32[864,256]{1,0:T(8,128)} %get-tuple-element.27), channel_id=1, source_target_pairs={{0,15},{1,0},{2,1},{3,2},{4,3},{5,4},{6,5},{7,6},{8,7},{9,8},{10,9... | collective-permute-start | bytes 2654216 | tf_op jit(solution)/shard_map/ppermute | solution.py:55
  20.7 2.6 %copy.16 = s32[64,32,2]{2,1,0:T(8,128)} copy(s32[64,32,2]{0,1,2:T(8,128)} %bitcast.16) | data formatting | bytes 32768 | tf_op jit(solution)/shard_map/transpose | solution.py:482
  23.3 6.6 %broadcast_in_dim.3 = s32[64,32,2,4]{3,2,1,0:T(2,128)} broadcast(s32[64,32,2]{2,1,0:T(8,128)} %copy.16), dimensions={0,1,2} | broadcast | bytes 81920 | tf_op jit(solution)/shard_map/broadcast_in_dim | solution.py:482
  29.9 5.1 %reshape_reshape.3 = s32[128,128]{1,0:T(8,128)} reshape(s32[64,32,2,4]{3,2,1,0:T(2,128)} %broadcast_in_dim.3) | data formatting | bytes 131072 | tf_op jit(solution)/shard_map/reshape;reshape | solution.py:482
  35.0 1.0 add_add_fusion.3
  36.0 19.6 %collective-permute-start.4 = (f32[128,128]{1,0:T(8,128)S(1)}, f32[128,128]{1,0:T(8,128)S(1)}, u32[]{:S(2)}, u32[]{:S(2)}) collective-permute-start(f32[128,128]{1,0:T(8,128)S(1)} %add_add_fusion.3), channel_id=1, source_target_pairs={{0,128},{1,129},{2,130},{3,131},{4,132},{5,133},{6,134},{7,135},{8... | collective-permute-start | bytes 196616 | tf_op jit(solution)/shard_map/ppermute | solution.py:55
  55.6 2.1 %collective-permute-start.5 = (f32[128,128]{1,0:T(8,128)S(1)}, f32[128,128]{1,0:T(8,128)S(1)}, u32[]{:S(2)}, u32[]{:S(2)}) collective-permute-start(f32[128,128]{1,0:T(8,128)S(1)} %add_add_fusion.3), channel_id=1, source_target_pairs={{0,64},{1,65},{2,66},{3,67},{4,68},{5,69},{6,70},{7,71},{8,72},{9,... | collective-permute-start | bytes 196616 | tf_op jit(solution)/shard_map/ppermute | solution.py:55
  57.7 0.7 constant_dynamic-slice_fusion
  58.4 1.5 %collective-permute-done.5 = f32[128,128]{1,0:T(8,128)S(1)} collective-permute-done((f32[128,128]{1,0:T(8,128)S(1)}, f32[128,128]{1,0:T(8,128)S(1)}, u32[]{:S(2)}, u32[]{:S(2)}) %collective-permute-start.5) | collective-permute-done | bytes 65568 | tf_op jit(solution)/shard_map/ppermute | solution.py:55
  59.9 2.1 %collective-permute-done.6 = f32[128,128]{1,0:T(8,128)S(1)} collective-permute-done((f32[128,128]{1,0:T(8,128)S(1)}, f32[128,128]{1,0:T(8,128)S(1)}, u32[]{:S(2)}, u32[]{:S(2)}) %collective-permute-start.6) | collective-permute-done | bytes 65568 | tf_op jit(solution)/shard_map/ppermute | solution.py:55
  62.6 0.9 copy-done.4
  63.6 0.9 copy-done.8
  64.5 13.6 %first_step.1 = (f32[864,1024]{1,0:T(8,128)}, f32[128,128]{1,0:T(8,128)S(1)}) custom-call(s32[1]{0:T(128)} %bitcast.dir_ref.refs_0_, f32[864,1024]{1,0:T(8,128)} %get-tuple-element.17.h_ref, f32[864,256]{1,0:T(8,128)S(1)} %collective-permute-done.halo_ref, bf16[128,3072]{1,0:T(8,128)(2,1)S(1)} %get-tuple-element.20.right_ref, ...), custom_call_target="tpu_custom_call" | custom-call | tf_op jit(solution)/shard_map/first_step/pallas_call | solution.py:397
  78.1 1.3 %collective-permute-start.10 = (f32[128,128]{1,0:T(8,128)S(1)}, f32[128,128]{1,0:T(8,128)S(1)}, u32[]{:S(2)}, u32[]{:S(2)}) collective-permute-start(f32[128,128]{1,0:T(8,128)S(1)} %get-tuple-element.28), channel_id=1, source_target_pairs={{0,32},{1,33},{2,34},{3,35},{4,36},{5,37},{6,38},{7,39},{8,40},{9,... | collective-permute-start | bytes 196616 | tf_op jit(solution)/shard_map/ppermute | solution.py:55
  79.4 0.8 collective-permute-start.9
  80.2 5.4 %collective-permute-start.7 = (f32[128,128]{1,0:T(8,128)S(1)}, f32[128,128]{1,0:T(8,128)S(1)}, u32[]{:S(2)}, u32[]{:S(2)}) collective-permute-start(f32[128,128]{1,0:T(8,128)S(1)} %add_add_fusion.2.refs_1_), channel_id=1, source_target_pairs={{0,15},{1,0},{2,1},{3,2},{4,3},{5,4},{6,5},{7,6},{8,7},{9,8},{10,9... | collective-permute-start | bytes 196616 | tf_op jit(solution)/shard_map/ppermute | solution.py:55
  85.7 4.0 %collective-permute-start.12 = (f32[128,128]{1,0:T(8,128)S(1)}, f32[128,128]{1,0:T(8,128)S(1)}, u32[]{:S(2)}, u32[]{:S(2)}) collective-permute-start(f32[128,128]{1,0:T(8,128)S(1)} %add_add_fusion.1), channel_id=1, source_target_pairs={{0,128},{1,129},{2,130},{3,131},{4,132},{5,133},{6,134},{7,135},{8... | collective-permute-start | bytes 196616 | tf_op jit(solution)/shard_map/ppermute | solution.py:55
  89.6 0.7 collective-permute-start.13
  90.3 1.3 %collective-permute-start.14 = (f32[128,128]{1,0:T(8,128)S(1)}, f32[128,128]{1,0:T(8,128)S(1)}, u32[]{:S(2)}, u32[]{:S(2)}) collective-permute-start(f32[128,128]{1,0:T(8,128)S(1)} %add_add_fusion.1), channel_id=1, source_target_pairs={{0,192},{1,193},{2,194},{3,195},{4,196},{5,197},{6,198},{7,199},{8... | collective-permute-start | bytes 196616 | tf_op jit(solution)/shard_map/ppermute | solution.py:55
  92.3 5.3 %edge_step.1.edge_ref = f32[864,256]{1,0:T(8,128)S(1)} custom-call(f32[864,256]{1,0:T(8,128)S(1)} %collective-permute-done.halo_ref, bf16[128,768]{1,0:T(8,128)(2,1)S(1)} %get-tuple-element.25.right_ref, f32[2,128]{1,0:T(2,128)S(1)} %get-tuple-element.26.keep_ref, bf16[864,128]{1,0:T(8,128)(2,1)S(1)} %copy-done.5, f32[864,768]{1,0:T(8,128)S(1)} %get-tuple-element.23.coef_ref), custom_call_target="tpu_custom_call" | custom-call | tf_op jit(solution)/shard_map/edge_step/pallas_call | solution.py:426
  97.6 0.9 copy-done.1
  99.6 1.2 %copy-done.2 = f32[864,256]{1,0:T(8,128)S(1)} copy-done((f32[864,256]{1,0:T(8,128)S(1)}, f32[864,256]{1,0:T(8,128)}, u32[]{:S(2)}) %copy-start.2) | copy-done | bytes 884760
  100.8 0.9 copy-done.6
  101.7 13.1 %last_step.1 = f32[6912,128]{1,0:T(8,128)} custom-call(s32[1]{0:T(128)} %bitcast.dir_ref.refs_0_, f32[864,1024]{1,0:T(8,128)} %get-tuple-element.24.h_ref, f32[864,256]{1,0:T(8,128)S(1)} %copy-done.2, f32[864,256]{1,0:T(8,128)} %collective-permute-done.8.far_ref, bf16[128,3072]{1,0:T(8,128)(2,1)S(1)} %get-tuple-element.29.right_ref, ...), custom_call_target="tpu_custom_call" | custom-call | tf_op jit(solution)/shard_map/last_step/pallas_call | solution.py:461
  (41 shorter events, 2.4 us)
Async XLA Ops:
  0.6 10.4 %copy-start.9 = (s32[864]{0:T(1024)S(1)}, s32[864]{0:T(1024)}, u32[]{:S(2)}) copy-start(s32[864]{0:T(1024)} %param.4) | copy-start | bytes 10372
  7.9 54.8 %collective-permute-start = (f32[864,256]{1,0:T(8,128)}, f32[864,256]{1,0:T(8,128)S(1)}, u32[]{:S(2)}, u32[]{:S(2)}) collective-permute-start(f32[864,256]{1,0:T(8,128)} %get-tuple-element.18), channel_id=1, source_target_pairs={{0,15},{1,0},{2,1},{3,2},{4,3},{5,4},{6,5},{7,6},{8,7},{9,8},{10,9... | collective-permute-start | bytes 2654216 | tf_op jit(solution)/shard_map/ppermute | solution.py:55
  11.9 0.7 copy-start.3
  12.6 4.1 %copy-start.7 = (bf16[48,896]{1,0:T(8,128)(2,1)}, bf16[48,896]{1,0:T(8,128)(2,1)S(1)}, u32[]{:S(2)}) copy-start(bf16[48,896]{1,0:T(8,128)(2,1)S(1)} %get-tuple-element.19.left_ref) | copy-start | bytes 258052
  12.6 2.0 %copy-start = (f32[864,1024]{1,0:T(8,128)S(1)}, f32[864,1024]{1,0:T(8,128)}, u32[]{:S(2)}) copy-start(f32[864,1024]{1,0:T(8,128)} %get-tuple-element.17.h_ref) | copy-start | bytes 10616836
  16.7 18.3 %collective-permute-start.1 = (f32[128,128]{1,0:T(8,128)}, f32[128,128]{1,0:T(8,128)}, u32[]{:S(2)}, u32[]{:S(2)}) collective-permute-start(f32[128,128]{1,0:T(8,128)} %moments.1), channel_id=1, source_target_pairs={{0,16},{1,17},{2,18},{3,19},{4,20},{5,21},{6,22},{7,23},{8,24},{9,... | collective-permute-start | bytes 196616 | tf_op jit(solution)/shard_map/ppermute | solution.py:55
  16.7 18.3 %collective-permute-start.2 = (f32[128,128]{1,0:T(8,128)}, f32[128,128]{1,0:T(8,128)}, u32[]{:S(2)}, u32[]{:S(2)}) collective-permute-start(f32[128,128]{1,0:T(8,128)} %moments.1), channel_id=1, source_target_pairs={{0,32},{1,33},{2,34},{3,35},{4,36},{5,37},{6,38},{7,39},{8,40},{9,... | collective-permute-start | bytes 196616 | tf_op jit(solution)/shard_map/ppermute | solution.py:55
  17.4 17.7 %collective-permute-start.3 = (f32[128,128]{1,0:T(8,128)}, f32[128,128]{1,0:T(8,128)}, u32[]{:S(2)}, u32[]{:S(2)}) collective-permute-start(f32[128,128]{1,0:T(8,128)} %moments.1), channel_id=1, source_target_pairs={{0,48},{1,49},{2,50},{3,51},{4,52},{5,53},{6,54},{7,55},{8,56},{9,... | collective-permute-start | bytes 196616 | tf_op jit(solution)/shard_map/ppermute | solution.py:55
  18.6 81.0 %collective-permute-start.8 = (f32[864,256]{1,0:T(8,128)}, f32[864,256]{1,0:T(8,128)}, u32[]{:S(2)}, u32[]{:S(2)}) collective-permute-start(f32[864,256]{1,0:T(8,128)} %get-tuple-element.27), channel_id=1, source_target_pairs={{0,15},{1,0},{2,1},{3,2},{4,3},{5,4},{6,5},{7,6},{8,7},{9,8},{10,9... | collective-permute-start | bytes 2654216 | tf_op jit(solution)/shard_map/ppermute | solution.py:55
  36.0 22.4 %collective-permute-start.4 = (f32[128,128]{1,0:T(8,128)S(1)}, f32[128,128]{1,0:T(8,128)S(1)}, u32[]{:S(2)}, u32[]{:S(2)}) collective-permute-start(f32[128,128]{1,0:T(8,128)S(1)} %add_add_fusion.3), channel_id=1, source_target_pairs={{0,128},{1,129},{2,130},{3,131},{4,132},{5,133},{6,134},{7,135},{8... | collective-permute-start | bytes 196616 | tf_op jit(solution)/shard_map/ppermute | solution.py:55
  55.6 4.3 %collective-permute-start.5 = (f32[128,128]{1,0:T(8,128)S(1)}, f32[128,128]{1,0:T(8,128)S(1)}, u32[]{:S(2)}, u32[]{:S(2)}) collective-permute-start(f32[128,128]{1,0:T(8,128)S(1)} %add_add_fusion.3), channel_id=1, source_target_pairs={{0,64},{1,65},{2,66},{3,67},{4,68},{5,69},{6,70},{7,71},{8,72},{9,... | collective-permute-start | bytes 196616 | tf_op jit(solution)/shard_map/ppermute | solution.py:55
  57.7 4.3 %collective-permute-start.6 = (f32[128,128]{1,0:T(8,128)S(1)}, f32[128,128]{1,0:T(8,128)S(1)}, u32[]{:S(2)}, u32[]{:S(2)}) collective-permute-start(f32[128,128]{1,0:T(8,128)S(1)} %add_add_fusion.3), channel_id=1, source_target_pairs={{0,192},{1,193},{2,194},{3,195},{4,196},{5,197},{6,198},{7,199},{8... | collective-permute-start | bytes 196616 | tf_op jit(solution)/shard_map/ppermute | solution.py:55
  62.6 0.9 copy-start.4
  63.6 0.9 copy-start.8
  64.5 27.8 %copy-start.5 = (bf16[864,128]{1,0:T(8,128)(2,1)S(1)}, bf16[864,128]{1,0:T(8,128)(2,1)}, u32[]{:S(2)}) copy-start(bf16[864,128]{1,0:T(8,128)(2,1)} %copy-done.3) | copy-start | bytes 663556
  78.1 7.5 %collective-permute-start.10 = (f32[128,128]{1,0:T(8,128)S(1)}, f32[128,128]{1,0:T(8,128)S(1)}, u32[]{:S(2)}, u32[]{:S(2)}) collective-permute-start(f32[128,128]{1,0:T(8,128)S(1)} %get-tuple-element.28), channel_id=1, source_target_pairs={{0,32},{1,33},{2,34},{3,35},{4,36},{5,37},{6,38},{7,39},{8,40},{9,... | collective-permute-start | bytes 196616 | tf_op jit(solution)/shard_map/ppermute | solution.py:55
  79.4 6.2 %collective-permute-start.11 = (f32[128,128]{1,0:T(8,128)S(1)}, f32[128,128]{1,0:T(8,128)S(1)}, u32[]{:S(2)}, u32[]{:S(2)}) collective-permute-start(f32[128,128]{1,0:T(8,128)S(1)} %get-tuple-element.28), channel_id=1, source_target_pairs={{0,48},{1,49},{2,50},{3,51},{4,52},{5,53},{6,54},{7,55},{8,56},{9,... | collective-permute-start | bytes 196616 | tf_op jit(solution)/shard_map/ppermute | solution.py:55
  79.4 6.2 %collective-permute-start.9 = (f32[128,128]{1,0:T(8,128)S(1)}, f32[128,128]{1,0:T(8,128)S(1)}, u32[]{:S(2)}, u32[]{:S(2)}) collective-permute-start(f32[128,128]{1,0:T(8,128)S(1)} %get-tuple-element.28), channel_id=1, source_target_pairs={{0,16},{1,17},{2,18},{3,19},{4,20},{5,21},{6,22},{7,23},{8,24},{9,... | collective-permute-start | bytes 196616 | tf_op jit(solution)/shard_map/ppermute | solution.py:55
  80.2 11.4 %collective-permute-start.7 = (f32[128,128]{1,0:T(8,128)S(1)}, f32[128,128]{1,0:T(8,128)S(1)}, u32[]{:S(2)}, u32[]{:S(2)}) collective-permute-start(f32[128,128]{1,0:T(8,128)S(1)} %add_add_fusion.2.refs_1_), channel_id=1, source_target_pairs={{0,15},{1,0},{2,1},{3,2},{4,3},{5,4},{6,5},{7,6},{8,7},{9,8},{10,9... | collective-permute-start | bytes 196616 | tf_op jit(solution)/shard_map/ppermute | solution.py:55
  85.7 12.8 %collective-permute-start.12 = (f32[128,128]{1,0:T(8,128)S(1)}, f32[128,128]{1,0:T(8,128)S(1)}, u32[]{:S(2)}, u32[]{:S(2)}) collective-permute-start(f32[128,128]{1,0:T(8,128)S(1)} %add_add_fusion.1), channel_id=1, source_target_pairs={{0,128},{1,129},{2,130},{3,131},{4,132},{5,133},{6,134},{7,135},{8... | collective-permute-start | bytes 196616 | tf_op jit(solution)/shard_map/ppermute | solution.py:55
  89.6 8.8 %collective-permute-start.13 = (f32[128,128]{1,0:T(8,128)S(1)}, f32[128,128]{1,0:T(8,128)S(1)}, u32[]{:S(2)}, u32[]{:S(2)}) collective-permute-start(f32[128,128]{1,0:T(8,128)S(1)} %add_add_fusion.1), channel_id=1, source_target_pairs={{0,64},{1,65},{2,66},{3,67},{4,68},{5,69},{6,70},{7,71},{8,72},{9,... | collective-permute-start | bytes 196616 | tf_op jit(solution)/shard_map/ppermute | solution.py:55
  90.3 8.2 %collective-permute-start.14 = (f32[128,128]{1,0:T(8,128)S(1)}, f32[128,128]{1,0:T(8,128)S(1)}, u32[]{:S(2)}, u32[]{:S(2)}) collective-permute-start(f32[128,128]{1,0:T(8,128)S(1)} %add_add_fusion.1), channel_id=1, source_target_pairs={{0,192},{1,193},{2,194},{3,195},{4,196},{5,197},{6,198},{7,199},{8... | collective-permute-start | bytes 196616 | tf_op jit(solution)/shard_map/ppermute | solution.py:55
  97.6 0.9 copy-start.1
  99.6 1.2 %copy-start.2 = (f32[864,256]{1,0:T(8,128)S(1)}, f32[864,256]{1,0:T(8,128)}, u32[]{:S(2)}) copy-start(f32[864,256]{1,0:T(8,128)} %copy-done.1) | copy-start | bytes 2654212
  100.7 0.9 copy-start.6

commit v2 on v1

v2 whole, which is shorter than its diff:
```python
import math

import jax
import jax.numpy as jnp
import numpy as np
from jax import lax
from jax.experimental import pallas as pl
from jax.experimental.pallas import tpu as pltpu
from jax.sharding import PartitionSpec as P

NV1 = 24
NSLOT = 864
NPAD = 896
CELLS = 1024
COL = 256
SPACING = 12.0 / NV1
TOP = (NV1 - 1) * 0.5 * SPACING
KD = 0.3 / TOP
DT = 0.3 / (8 * TOP)
WEIGHT = SPACING**3 / (2.0 * math.pi) ** 1.5
LOG2E = 1.0 / math.log(2.0)
WALL_T = [[b * (0.7 + 0.3 * level) for level in range(3)] for b in (1.4, 0.7)]
AXES = ("vel", "space")
F32 = jnp.float32
BF16 = jnp.bfloat16


def wall_norms():
    line = (2 * np.arange(NV1) - (NV1 - 1)) * 0.5 * SPACING
    cx, cy, cz = np.meshgrid(line, line, line, indexing="ij")
    sq = cx**2 + cy**2 + cz**2
    mass, energy = [], []
    for side in range(2):
        out = np.maximum(cz if side == 0 else -cz, 0.0) * WEIGHT
        prof = [out * t**-1.5 * np.exp(-sq / (2.0 * t)) for t in WALL_T[side]]
        mass.append([float(p.sum()) for p in prof])
        energy.append([float((p * 0.5 * sq).sum()) for p in prof])
    return mass, energy


MASS, ENERGY = wall_norms()


def device_of(i):
    v, s = divmod(i, 16)
    x, r = divmod(v, 4)
    return x, r >> 1, r & 1, s


def index_of(x, y, core, s):
    return ((x % 4 * 2 + y % 2) * 2 + core % 2) * 16 + s % 16


def permute(value, move):
    return lax.ppermute(value, AXES, [(i, index_of(*move(*device_of(i)))) for i in range(256)])


def downstream(value):
    return permute(value, lambda x, y, c, s: (x, y, c, s - 1 if x < 2 else s + 1))


def over_near(part):
    return part + permute(part, lambda x, y, c, s: (x, y ^ 1, c, s))


def over_rest(part):
    part = part + permute(part, lambda x, y, c, s: (x, y, c ^ 1, s))
    one = permute(part, lambda x, y, c, s: (x + 1, y, c, s))
    three = permute(part, lambda x, y, c, s: (x - 1, y, c, s))
    two = permute(part, lambda x, y, c, s: (x + 2, y, c, s))
    return (part + two) + (one + three)


def upstream_first():
    return (lax.axis_index("vel") >= 8).astype(jnp.int32)


def column_of(forward, i):
    return jnp.where(forward == 1, i, 3 - i)


def spec():
    return pl.BlockSpec(memory_space=pltpu.VMEM)


def anywhere():
    return pl.BlockSpec(memory_space=pl.ANY)


def smem():
    return pl.BlockSpec(memory_space=pltpu.SMEM)


def params(mib=8):
    return pltpu.CompilerParams(vmem_limit_bytes=mib * 2**20)


def shape(*dims, dtype=F32):
    return jax.ShapeDtypeStruct(dims, dtype)


def fetch(sems, *pairs):
    copies = [pltpu.make_async_copy(src, dst, sems.at[k]) for k, (src, dst) in enumerate(pairs)]
    for copy in copies:
        copy.start()
    return copies


def high(a):
    return a.astype(BF16).astype(F32)


def velocity_rows(order_ref, padded):
    padded[...] = jnp.zeros((1, NPAD), jnp.int32)
    padded[:, pl.ds(0, NSLOT)] = order_ref[...].reshape(1, NSLOT)
    order = padded[...]
    upper = (order * 43691) >> 20
    kx = (upper * 43691) >> 20
    ky = upper - kx * NV1
    kz = order - upper * NV1
    live = (lax.broadcasted_iota(jnp.int32, (1, NPAD), 1) < NSLOT).astype(F32)

    def coordinate(k):
        return (2 * k - (NV1 - 1)).astype(F32) * (0.5 * SPACING) * live

    cx, cy, cz = coordinate(kx), coordinate(ky), coordinate(kz)
    sq = cx * cx + cy * cy + cz * cz
    phi = [live, cx, cy, cz, cx * cx, cy * cy, cz * cz, cx * cy, cx * cz, cy * cz, cx * sq, cy * sq, cz * sq]
    return cx, cy, cz, sq, phi


def put_left(order_ref, padded, table, left_ref):
    _, _, cz, sq, phi = velocity_rows(order_ref, padded)
    zero = jnp.zeros_like(cz)
    down, up = jnp.maximum(-cz, 0.0), jnp.maximum(cz, 0.0)
    sums = phi + [down, down * (0.5 * sq), zero] + [zero] * 5 + [up, up * (0.5 * sq), zero]
    for r, a in enumerate(sums):
        table[pl.ds(r, 1), :] = high(a)
        table[pl.ds(24 + r, 1), :] = a - high(a)
    left_ref[...] = table[...].astype(BF16)


def velocity_kernel(order_ref, phi_ref, coef_ref, table, padded):
    cx, cy, cz, sq, phi = velocity_rows(order_ref, padded)
    zero = jnp.zeros_like(cx)
    down, up = jnp.maximum(-cz, 0.0), jnp.maximum(cz, 0.0)
    ghost = []
    for side, out in ((0, up), (1, down)):
        ghost += [out * KD * jnp.exp(sq * (-0.5 / t)) for t in WALL_T[side]]
    rows = []
    for _ in range(3):
        rows += [high(a) for a in phi] + [zero] * 3
    for _ in range(2):
        rows += [a - high(a) for a in phi] + [zero] * 3
    rows += [high(a) for a in ghost] + [high(a - high(a)) for a in ghost] + [zero] * 4
    rows += [high(a) for a in ghost] + [zero] * 10
    rows += [jnp.abs(cx), jnp.maximum(cy, 0.0), jnp.maximum(-cy, 0.0), up, down]
    rows += [jnp.abs(cx) + jnp.abs(cy) + jnp.abs(cz)] + [zero] * 10
    for r, a in enumerate(rows):
        table[pl.ds(r, 1), :] = a
    turned = table[...].T.astype(BF16)
    phi_ref[...] = turned[:NSLOT]
    row = lax.broadcasted_iota(jnp.int32, (128, 768), 0)
    lane = lax.broadcasted_iota(jnp.int32, (128, 768), 1)
    kind, z = lane >> 7, lane & 7
    drop = ((kind == 3) & (z == 0)) | ((kind == 4) & (z == 7))
    pick = ((row == 112 + kind) & jnp.logical_not(drop)).astype(F32).astype(BF16)
    coef_ref[...] = jnp.dot(turned, pick, preferred_element_type=F32)[:NSLOT] * KD


def velocities(order):
    return pl.pallas_call(
        velocity_kernel,
        in_specs=[spec()],
        out_specs=[spec()] * 2,
        out_shape=[shape(NSLOT, 128, dtype=BF16), shape(NSLOT, 768)],
        scratch_shapes=[pltpu.VMEM((128, NPAD), F32), pltpu.VMEM((1, NPAD), jnp.int32)],
        compiler_params=params(),
        name="velocities",
    )(order)


def clear_tail(high_ref, low_ref):
    tail = jnp.zeros((NPAD - NSLOT, high_ref.shape[1]), BF16)
    high_ref[pl.ds(NSLOT, NPAD - NSLOT), :] = tail
    low_ref[pl.ds(NSLOT, NPAD - NSLOT), :] = tail


def sums_of(left, high, low):
    total = jnp.dot(left, high, preferred_element_type=F32) + jnp.dot(left, low, preferred_element_type=F32)
    total = total[:24] + total[24:]
    sub = lax.broadcasted_iota(jnp.int32, (8, 128), 0)
    lane = lax.broadcasted_iota(jnp.int32, (8, 128), 1)
    top = (sub >= 5) & ((lane & 7) >= 4)
    out = []
    for half in range(2):
        part = total[:, half * 128 : half * 128 + 128]
        out.append((part[0:8], jnp.where(top, part[16:24], part[8:16])))
    return out


def put_moments(forward, left_ref, high_ref, low_ref, out_ref):
    left = left_ref[...]
    for i in range(4):
        cols = pl.ds(i * COL, COL)
        row = column_of(forward, i) * 2
        for half, (low, mid) in enumerate(sums_of(left, high_ref[:, cols], low_ref[:, cols])):
            out_ref[pl.ds(row + half, 8, stride=8), :] = low
            out_ref[pl.ds(64 + row + half, 8, stride=8), :] = mid


def split_into(value, rows, cols, high_ref, low_ref):
    high = value.astype(BF16)
    high_ref[rows, cols] = high
    low_ref[rows, cols] = (value - high.astype(F32)).astype(BF16)


PARTS = 3


def unpack_kernel(dir_ref, in_ref, order_ref, near_ref, m_ref, left_ref, whole, high_ref, low_ref, table, padded, sems):
    forward = dir_ref[0]
    size = NSLOT // PARTS
    spans = [pl.ds(p * size * 8, size * 8) for p in range(PARTS)]
    copies = fetch(sems, *[(in_ref.at[a], whole.at[a]) for a in spans])
    put_left(order_ref, padded, table, left_ref)
    clear_tail(high_ref, low_ref)
    step = 96

    for p in range(PARTS):
        copies[p].wait()

        def body(k, carry):
            first = pl.multiple_of(p * size + k * step, 16)
            rows = pl.ds(first, step)
            for i in range(4):
                for half in range(2):
                    start = first * 8 + half * 4 + column_of(forward, i)
                    part = whole[pl.ds(start, step, stride=8), :]
                    if i == 3:
                        near_ref[rows, pl.ds(half * 128, 128)] = part
                    split_into(part, rows, pl.ds(i * COL + half * 128, 128), high_ref, low_ref)
            return carry

        lax.fori_loop(0, size // step, body, 0)
    put_moments(forward, left_ref, high_ref, low_ref, m_ref)


def unpack(forward, flat, order):
    return pl.pallas_call(
        unpack_kernel,
        in_specs=[smem(), anywhere(), spec()],
        out_specs=[spec()] * 3,
        out_shape=[shape(NSLOT, COL), shape(128, 128), shape(48, NPAD, dtype=BF16)],
        scratch_shapes=[
            pltpu.VMEM((NSLOT * 8, 128), F32),
            pltpu.VMEM((NPAD, CELLS), BF16),
            pltpu.VMEM((NPAD, CELLS), BF16),
            pltpu.VMEM((48, NPAD), F32),
            pltpu.VMEM((1, NPAD), jnp.int32),
            pltpu.SemaphoreType.DMA((PARTS,)),
        ],
        compiler_params=params(16),
        name="unpack",
    )(forward, flat, order)


def tag_kernel(at_ref, tag_ref, out_ref):
    row = lax.broadcasted_iota(jnp.int32, (8, 64), 0)
    x = lax.broadcasted_iota(jnp.int32, (8, 64), 1)
    strip = (x == at_ref[0] * 4 + (row >> 1)).astype(F32).astype(BF16)
    picked = lax.dot_general(
        strip, tag_ref[...].astype(F32).astype(BF16), (((1,), (1,)), ((), ())), preferred_element_type=F32
    )
    row = lax.broadcasted_iota(jnp.int32, (64, COL), 0)
    lane = lax.broadcasted_iota(jnp.int32, (64, COL), 1)
    spread = row == ((lane >> 2) & 1) * 32 + (lane >> 3)
    spread = jnp.dot(picked.astype(BF16), spread.astype(F32).astype(BF16), preferred_element_type=F32)
    odd = (lax.broadcasted_iota(jnp.int32, (8, 128), 0) & 1) == 1
    out_ref[...] = jnp.where(odd, spread[:, 128:], spread[:, :128]).astype(jnp.int32)


def strip_tags(at, tags):
    return pl.pallas_call(
        tag_kernel,
        in_specs=[smem(), spec()],
        out_specs=spec(),
        out_shape=shape(8, 128, dtype=jnp.int32),
        compiler_params=params(),
        name="strip_tags",
    )(at, tags)


def put_fields(forward, m_ref, tag_ref, right_ref, keep_ref, table):
    m = [m_ref[pl.ds(f * 8, 8), :] * WEIGHT for f in range(15)]
    rho = m[0]
    inv = 1.0 / rho
    u = [a * inv for a in m[1:4]]
    energy = m[4] + m[5] + m[6]
    usq = u[0] * u[0] + u[1] * u[1] + u[2] * u[2]
    temp = (energy * inv - usq) * (1.0 / 3.0)
    stress = [[m[4], m[7], m[8]], [m[7], m[5], m[9]], [m[8], m[9], m[6]]]
    q = []
    for i in range(3):
        pu = stress[i][0] * u[0] + stress[i][1] * u[1] + stress[i][2] * u[2]
        q.append(0.5 * (m[10 + i] - 2.0 * pu - u[i] * energy + 2.0 * rho * usq * u[i]))
    log_t = jnp.log(temp)
    inv_t = 1.0 / temp
    rate = (DT / 0.05) * rho * jnp.exp(0.19 * log_t)
    amp = rate * rho * jnp.exp(-1.5 * log_t)
    half = (0.5 * LOG2E) * inv_t
    zero = jnp.zeros_like(rho)
    expo = [-half * usq] + [2.0 * half * a for a in u] + [-half] * 3 + [zero] * 9
    scale = inv * inv_t * inv_t * (1.0 / 15.0)
    a = [b * scale for b in q]
    s0 = u[0] * a[0] + u[1] * a[1] + u[2] * a[2]
    s1 = usq * inv_t - 5.0
    poly = [amp * (1.0 - s0 * s1)]
    poly += [amp * (a[i] * s1 + 2.0 * s0 * u[i] * inv_t) for i in range(3)]
    front = amp * inv_t
    poly += [-front * (2.0 * a[i] * u[i] + s0) for i in range(3)]
    poly += [-2.0 * front * (a[i] * u[j] + a[j] * u[i]) for i, j in ((0, 1), (0, 2), (1, 2))]
    poly += [front * a[i] for i in range(3)] + [zero] * 3
    z = lax.broadcasted_iota(jnp.int32, (8, 128), 1) & 7
    tag = tag_ref[...]
    density, heat = zero, zero
    walls = []
    for side, at in ((0, 0), (1, 7)):
        for level in range(3):
            here = (z == at) & (tag == level)
            n = jnp.where(here, m[13] * (1.0 / MASS[side][level]), 0.0)
            heat = jnp.where(here, n * ENERGY[side][level] - m[14], heat)
            walls.append(n * WALL_T[side][level] ** -1.5)
    for r, c in enumerate(expo + poly + walls + [zero] * 10):
        table[pl.ds(r * 8, 8), :] = c
    keep = 1.0 - rate
    table[pl.ds(384, 8), :] = keep
    n = 4
    right_ref[...] = jnp.zeros(right_ref.shape, BF16)

    def pieces(value, count):
        out = []
        for _ in range(count):
            piece = value.astype(BF16)
            out.append(piece)
            value = value - piece.astype(F32)
        return out

    for k in range(n):
        col = column_of(forward, k)
        for hf in range(2):
            j = col * 2 + hf
            at = k * COL + hf * 128
            keep_ref[pl.ds(k * 2 + hf, 1), :] = table[pl.ds(384 + j, 1), :]
            for kind in range(2):
                lanes = pl.ds(kind * n * COL + at, 128)
                first, second, third = pieces(table[pl.ds(kind * 128 + j, 16, stride=8), :], 3)
                for g, piece in enumerate((first, second, third, first, second)):
                    right_ref[pl.ds(g * 16, 16), lanes] = piece
            wall = table[pl.ds(256 + j, 16, stride=8), :]
            twice = table[pl.ds(256 + j, 6, stride=8), :]
            twice = jnp.concatenate([twice, twice, jnp.zeros((4, 128), F32)], axis=0)
            lanes = pl.ds(2 * n * COL + at, 128)
            right_ref[pl.ds(80, 16), lanes] = pieces(twice, 1)[0]
            right_ref[pl.ds(96, 16), lanes] = pieces(wall, 2)[1]
    return heat


def field_scratch():
    return [pltpu.VMEM((128, 3 * CELLS), BF16), pltpu.VMEM((8, 128), F32), pltpu.VMEM((392, 128), F32)]


def put_heat(heat, table, out_ref):
    lane = lax.broadcasted_iota(jnp.int32, (128, 64), 0)
    to = lax.broadcasted_iota(jnp.int32, (128, 64), 1)
    pick = (lane == (to & 15) * 8 + 7 * (to >> 5)).astype(F32).astype(BF16)
    total = jnp.zeros((8, 64), F32)
    for _ in range(3):
        piece = heat.astype(BF16)
        total = total + jnp.dot(piece, pick, preferred_element_type=F32)
        heat = heat - piece.astype(F32)
    odd = lax.broadcasted_iota(jnp.int32, (8, 64), 0) & 1
    half = (lax.broadcasted_iota(jnp.int32, (8, 64), 1) >> 4) & 1
    total = jnp.where(odd == half, total, 0.0)
    table[pl.ds(0, 8), pl.ds(0, 64)] = total
    for x in range(4):
        for side in range(2):
            lanes = pl.ds(side * 32, 32)
            out_ref[x, pl.ds(side, 1), :] = table[pl.ds(2 * x, 1), lanes] + table[pl.ds(2 * x + 1, 1), lanes]


def products(n, phi_ref, right_ref, prod):
    phi = phi_ref[...]
    for k in range(3 * n):
        cols = pl.ds(k * COL, COL)
        prod[:, cols] = jnp.dot(phi, right_ref[:, cols], preferred_element_type=F32)


def updated(n, i, rows, coefs, h, upwind, keep, prod):
    cx, cyp, cym, czp, czm, spill = coefs
    lane = lax.broadcasted_iota(jnp.int32, (1, 128), 1)
    plus = [pltpu.roll(a, 8, 1) for a in h]
    minus = [pltpu.roll(a, 120, 1) for a in h]
    out = []
    for hf in range(2):
        at = i * COL + hf * 128
        before = jnp.where(lane < 8, plus[1 - hf], plus[hf])
        after = jnp.where(lane >= 120, minus[1 - hf], minus[hf])
        expo = prod[rows, pl.ds(at, 128)]
        poly = prod[rows, pl.ds(n * COL + at, 128)]
        ghost = prod[rows, pl.ds(2 * n * COL + at, 128)]
        new = jnp.exp2(expo) * poly + ghost
        new = new + h[hf] * (keep[2 * i + hf] - spill)
        new = new + (cyp * before + cym * after)
        new = new + (czp * pltpu.roll(h[hf], 1, 1) + czm * pltpu.roll(h[hf], 127, 1))
        if upwind is not None:
            new = new + cx * upwind[hf]
        out.append(new)
    return out


def read_coefs(coef_ref, rows):
    return [coef_ref[rows, pl.ds(c * 128, 128)] for c in range(6)]


def sweep(column, coef_ref, keep_ref, prod, put):
    step = 32

    def body(k, carry):
        first = pl.multiple_of(k * step, step)
        rows = pl.ds(first, step)
        coefs = read_coefs(coef_ref, rows)
        keep = [keep_ref[pl.ds(b, 1), :] for b in range(8)]
        upwind = None
        for i in range(4):
            h = [column(i, hf, first, step) for hf in range(2)]
            new = updated(4, i, rows, coefs, h, upwind, keep, prod)
            for hf in range(2):
                put(i, hf, first, step, new[hf])
            upwind = h
        return carry

    lax.fori_loop(0, NSLOT // step, body, 0)


def first_kernel(
    dir_ref, in_ref, m0_ref, tag_ref, phi_ref, coef_ref, left_ref, c0_ref, rest_ref, edge_ref, m_ref,
    right, keep, table, prod, whole, coef, high_ref, low_ref, sems,
):
    forward = dir_ref[0]
    copies = fetch(sems, (in_ref, whole), (coef_ref, coef))
    clear_tail(high_ref, low_ref)
    put_fields(forward, m0_ref, tag_ref, right, keep, table)
    products(4, phi_ref, right, prod)
    for copy in copies:
        copy.wait()

    def column(i, hf, first, step):
        return whole[pl.ds(first * 8 + hf * 4 + column_of(forward, i), step, stride=8), :]

    def put(i, hf, first, step, new):
        rows = pl.ds(first, step)
        side = pl.ds(hf * 128, 128)
        if i == 0:
            c0_ref[rows, side] = new
        else:
            rest_ref[rows, pl.ds((i - 1) * COL + hf * 128, 128)] = new
        if i == 3:
            edge_ref[rows, side] = new
        split_into(new, rows, pl.ds(i * COL + hf * 128, 128), high_ref, low_ref)

    sweep(column, coef, keep, prod, put)
    put_moments(forward, left_ref, high_ref, low_ref, m_ref)


def first_step(forward, flat, m, tags, phi, coef, left):
    return pl.pallas_call(
        first_kernel,
        in_specs=[smem(), anywhere(), spec(), spec(), spec(), anywhere(), spec()],
        out_specs=[spec()] * 4,
        out_shape=[shape(NSLOT, COL), shape(NSLOT, 3 * COL), shape(NSLOT, COL), shape(128, 128)],
        scratch_shapes=field_scratch()
        + [
            pltpu.VMEM((NSLOT, 3 * CELLS), F32),
            pltpu.VMEM((NSLOT * 8, 128), F32),
            pltpu.VMEM((NSLOT, 768), F32),
            pltpu.VMEM((NPAD, CELLS), BF16),
            pltpu.VMEM((NPAD, CELLS), BF16),
            pltpu.SemaphoreType.DMA((2,)),
        ],
        compiler_params=params(32),
        name="first_step",
    )(forward, flat, m, tags, phi, coef, left)


def inflow_kernel(
    dir_ref, c0_any, halo_any, coef_any, left_any, m_ref, c1_ref, out_ref, c0, halo, coef, left, high_ref, low_ref, sems
):
    copies = fetch(sems, (halo_any, halo), (c0_any, c0), (coef_any.at[:, pl.ds(0, 128)], coef), (left_any, left))
    clear_tail(high_ref, low_ref)
    out_ref[...] = m_ref[...]
    for copy in copies:
        copy.wait()
    step = 48

    def body(k, carry):
        rows = pl.ds(pl.multiple_of(k * step, 16), step)
        cx = coef[rows, :]
        for half in range(2):
            cols = pl.ds(half * 128, 128)
            share = cx * halo[rows, cols]
            c1_ref[rows, cols] = c0[rows, cols] + share
            split_into(share, rows, cols, high_ref, low_ref)
        return carry

    lax.fori_loop(0, NSLOT // step, body, 0)
    row = column_of(dir_ref[0], 0) * 2
    for half, parts in enumerate(sums_of(left[...], high_ref[...], low_ref[...])):
        for k, part in enumerate(parts):
            at = pl.ds(64 * k + row + half, 8, stride=8)
            out_ref[at, :] = m_ref[at, :] + part


def inflow(forward, c0, halo, coef, left, m):
    return pl.pallas_call(
        inflow_kernel,
        in_specs=[smem()] + [anywhere()] * 4 + [spec()],
        out_specs=[spec()] * 2,
        out_shape=[shape(NSLOT, COL), shape(128, 128)],
        scratch_shapes=[
            pltpu.VMEM((NSLOT, COL), F32),
            pltpu.VMEM((NSLOT, COL), F32),
            pltpu.VMEM((NSLOT, 128), F32),
            pltpu.VMEM((48, NPAD), BF16),
            pltpu.VMEM((NPAD, COL), BF16),
            pltpu.VMEM((NPAD, COL), BF16),
            pltpu.SemaphoreType.DMA((4,)),
        ],
        compiler_params=params(),
        name="inflow",
    )(forward, c0, halo, coef, left, m)


def second_kernel(
    dir_ref, c1_any, rest_any, m0_ref, tag_ref, phi_ref, coef_any, out_ref, heat_ref,
    right, keep, table, prod, c1, rest, coef, sems,
):
    forward = dir_ref[0]
    copies = fetch(sems, (c1_any, c1), (rest_any, rest), (coef_any, coef))
    heat = put_fields(forward, m0_ref, tag_ref, right, keep, table)
    put_heat(heat, table, heat_ref)
    products(4, phi_ref, right, prod)
    for copy in copies:
        copy.wait()

    def column(i, hf, first, step):
        if i == 0:
            return c1[pl.ds(first, step), pl.ds(hf * 128, 128)]
        return rest[pl.ds(first, step), pl.ds((i - 1) * COL + hf * 128, 128)]

    def put(i, hf, first, step, new):
        out_ref[pl.ds(first * 8 + hf * 4 + column_of(forward, i), step, stride=8), :] = new

    sweep(column, coef, keep, prod, put)


def second_step(forward, c1, rest, m, tags, phi, coef):
    return pl.pallas_call(
        second_kernel,
        in_specs=[smem(), anywhere(), anywhere(), spec(), spec(), spec(), anywhere()],
        out_specs=[spec()] * 2,
        out_shape=[shape(NSLOT * 8, 128), shape(4, 2, 32)],
        scratch_shapes=field_scratch()
        + [
            pltpu.VMEM((NSLOT, 3 * CELLS), F32),
            pltpu.VMEM((NSLOT, COL), F32),
            pltpu.VMEM((NSLOT, 3 * COL), F32),
            pltpu.VMEM((NSLOT, 768), F32),
            pltpu.SemaphoreType.DMA((3,)),
        ],
        compiler_params=params(32),
        name="second_step",
    )(forward, c1, rest, m, tags, phi, coef)


def last_kernel(dir_ref, h_ref, halo_ref, cx_ref, out_ref):
    step = halo_ref.shape[0]
    col = column_of(dir_ref[0], 0)
    out_ref[...] = h_ref[...]
    cx = cx_ref[...]
    for half in range(2):
        at = pl.ds(half * 4 + col, step, stride=8)
        out_ref[at, :] = h_ref[at, :] + cx * halo_ref[:, pl.ds(half * 128, 128)]


def last(forward, h, halo, coef):
    step = 144
    return pl.pallas_call(
        last_kernel,
        grid=(NSLOT // step,),
        in_specs=[
            smem(),
            pl.BlockSpec((step * 8, 128), lambda i: (i, 0)),
            pl.BlockSpec((step, COL), lambda i: (i, 0)),
            pl.BlockSpec((step, 128), lambda i: (i, 0)),
        ],
        out_specs=pl.BlockSpec((step * 8, 128), lambda i: (i, 0)),
        out_shape=shape(NSLOT * 8, 128),
        compiler_params=params(),
        name="last",
    )(forward, h, halo, coef)


def body(state, velocity_order, wall_tag):
    forward = upstream_first().reshape(1)
    at = lax.axis_index("space").astype(jnp.int32).reshape(1)
    flat = state.reshape(NSLOT, 4, 2, 128).transpose(0, 2, 1, 3).reshape(NSLOT * 8, 128)
    near, m1, left = unpack(forward, flat, velocity_order)
    m1 = over_near(m1)
    near, m1 = lax.optimization_barrier((near, m1))
    halo = downstream(near)
    phi, coef = velocities(velocity_order)
    tags = strip_tags(at, jnp.transpose(wall_tag, (1, 2, 0)).reshape(64, 64))
    m1 = over_rest(m1)
    c0, rest, edge, m2 = first_step(forward, flat, m1, tags, phi, coef, left)
    c1, m2 = inflow(forward, c0, halo, coef, left, m2)
    m2 = over_near(m2)
    edge, m2 = lax.optimization_barrier((edge, m2))
    halo = downstream(edge)
    m2 = over_rest(m2)
    out, wall_heat = second_step(forward, c1, rest, m2, tags, phi, coef)
    out = last(forward, out, halo, coef)
    state_next = out.reshape(NSLOT, 2, 4, 128).transpose(0, 2, 1, 3).reshape(NSLOT, 4, 256)
    return state_next, wall_heat


def solution(mesh):
    return jax.shard_map(
        body,
        mesh=mesh,
        in_specs=(P("vel", "space", None), P("vel"), P()),
        out_specs=(P("vel", "space", None), P("space", None, None)),
        check_vma=False,
    )
```

time: 117 us -> 92.2 us (0.79)
  the two profiles are of different devices: /device:TPU:4 before, /device:TPU:2 now
where the time goes in v2:
time: 92.2 us; the launch traced here: 91.8 us
  waiting for transfers between devices  37.7 us (41%)
  Pallas kernels  26 us (28%)
  starting transfers between devices  17.7 us (19%)
  local copies, waits for them, and re-layouts  7.94 us (9%)
  other arithmetic  1.62 us (2%)
    ppermute x12, waiting for transfers between devices, permute(): lax.ppermute(value, AXES, [(i, index_of(*move(*device_of(i)))) for i in r...  37.7 us
    ppermute x12, starting transfers between devices, permute(): lax.ppermute(value, AXES, [(i, index_of(*move(*device_of(i)))) for i in r...  17.7 us
    pallas_call x1, Pallas kernels, first_step(): pl.pallas_call(first_kernel, in_specs=[smem(), anywhere(), spec(), spec()...  9.01 us
    pallas_call x1, Pallas kernels, second_step(): pl.pallas_call(second_kernel, in_specs=[smem(), anywhere(), anywhere(), s...  8.67 us
    unnamed x18, local copies, waits for them, and re-layouts  7.94 us
    pallas_call x1, Pallas kernels, unpack(): pl.pallas_call(unpack_kernel, in_specs=[smem(), anywhere(), spec()], out_...  3.3 us
    pallas_call x1, Pallas kernels, last(): pl.pallas_call(last_kernel, grid=(NSLOT // step,), in_specs=[smem(), pl.B...  2.92 us
  transfers between devices with their start and end apart: 12, of which 10 were waited for; matrix products, arithmetic and copies ran while one was open for 2% of the time, Pallas kernels for 20%

profile of v2, /device:TPU:2, one launch (start us, length us, event | category | flops | bytes accessed | tf_op | source)
XLA Modules:
  0.0 91.8 jit_solution(8149732498213331032)
XLA Ops:
  0.7 2.0 %copy-done = f32[864,4,256]{2,1,0:T(4,128)S(1)} copy-done((f32[864,4,256]{2,1,0:T(4,128)S(1)}, f32[864,4,256]{2,1,0:T(4,128)}, u32[]{:S(2)}) %copy-start) | copy-done | bytes 3538968
  2.7 0.7 copy-done.7
  3.3 3.3 %unpack.1 = (f32[864,256]{1,0:T(8,128)}, f32[128,128]{1,0:T(8,128)S(1)}, bf16[48,896]{1,0:T(8,128)(2,1)S(1)}) custom-call(s32[1]{0:T(128)} %bitcast.dir_ref, f32[6912,128]{1,0:T(8,128)S(1)} %bitcast.15, s32[864]{0:T(1024)S(1)} %copy-done.7), custom_call_target="tpu_custom_call" | custom-call | tf_op jit(solution)/shard_map/unpack/pallas_call | solution.py:250
  6.7 1.7 %collective-permute-start = (f32[128,128]{1,0:T(8,128)S(1)}, f32[128,128]{1,0:T(8,128)S(1)}, u32[]{:S(2)}, u32[]{:S(2)}) collective-permute-start(f32[128,128]{1,0:T(8,128)S(1)} %get-tuple-element.20), channel_id=1, source_target_pairs={{0,32},{1,33},{2,34},{3,35},{4,36},{5,37},{6,38},{7,39},{8,40},{9,... | collective-permute-start | bytes 196616 | tf_op jit(solution)/shard_map/ppermute | solution.py:55
  8.3 2.7 %collective-permute-done = f32[128,128]{1,0:T(8,128)S(1)} collective-permute-done((f32[128,128]{1,0:T(8,128)S(1)}, f32[128,128]{1,0:T(8,128)S(1)}, u32[]{:S(2)}, u32[]{:S(2)}) %collective-permute-start) | collective-permute-done | bytes 65568 | tf_op jit(solution)/shard_map/ppermute | solution.py:55
  11.0 8.6 %collective-permute-start.5 = (f32[864,256]{1,0:T(8,128)}, f32[864,256]{1,0:T(8,128)S(1)}, u32[]{:S(2)}, u32[]{:S(2)}) collective-permute-start(f32[864,256]{1,0:T(8,128)} %get-tuple-element.26), channel_id=1, source_target_pairs={{0,15},{1,0},{2,1},{3,2},{4,3},{5,4},{6,5},{7,6},{8,7},{9,8},{10,9... | collective-permute-start | bytes 2654216 | tf_op jit(solution)/shard_map/ppermute | solution.py:55
  19.6 1.3 %collective-permute-done.1 = f32[128,128]{1,0:T(8,128)S(1)} collective-permute-done((f32[128,128]{1,0:T(8,128)S(1)}, f32[128,128]{1,0:T(8,128)S(1)}, u32[]{:S(2)}, u32[]{:S(2)}) %collective-permute-start.1) | collective-permute-done | bytes 65568 | tf_op jit(solution)/shard_map/ppermute | solution.py:55
  20.9 0.6 add.31
  21.5 0.5 collective-permute-start.4
  22.0 1.5 %collective-permute-start.3 = (f32[128,128]{1,0:T(8,128)}, f32[128,128]{1,0:T(8,128)}, u32[]{:S(2)}, u32[]{:S(2)}) collective-permute-start(f32[128,128]{1,0:T(8,128)} %add.31), channel_id=1, source_target_pairs={{0,64},{1,65},{2,66},{3,67},{4,68},{5,69},{6,70},{7,71},{8,72},{9,... | collective-permute-start | bytes 196616 | tf_op jit(solution)/shard_map/ppermute | solution.py:55
  23.5 0.6 collective-permute-start.2
  24.1 0.7 velocities.1
  24.8 0.7 copy-done.2
  25.5 0.8 copy-done.6
  26.5 0.4 collective-permute-done.3
  26.9 2.7 %collective-permute-done.2 = f32[128,128]{1,0:T(8,128)} collective-permute-done((f32[128,128]{1,0:T(8,128)}, f32[128,128]{1,0:T(8,128)}, u32[]{:S(2)}, u32[]{:S(2)}) %collective-permute-start.2) | collective-permute-done | bytes 65568 | tf_op jit(solution)/shard_map/ppermute | solution.py:55
  29.6 1.0 %add_add_fusion.1.m0_ref = f32[128,128]{1,0:T(8,128)S(1)} fusion(f32[128,128]{1,0:T(8,128)} %collective-permute-done.3, f32[128,128]{1,0:T(8,128)} %collective-permute-done.4, f32[128,128]{1,0:T(8,128)} %add.31, f32[128,128]{1,0:T(8,128)} %collective-permute-done.2), kind=kLoop, calls=%fused_computation.1 | loop fusion | flops 49152 | bytes 327680 | tf_op jit(solution)/shard_map/add | solution.py:71
  30.6 2.0 %copy-done.1 = f32[864,4,256]{2,1,0:T(4,128)S(1)} copy-done((f32[864,4,256]{2,1,0:T(4,128)S(1)}, f32[864,4,256]{2,1,0:T(4,128)}, u32[]{:S(2)}) %copy-start.1) | copy-done | bytes 3538968
  32.5 0.9 %copy-done.3 = bf16[864,128]{1,0:T(8,128)(2,1)S(1)} copy-done((bf16[864,128]{1,0:T(8,128)(2,1)S(1)}, bf16[864,128]{1,0:T(8,128)(2,1)}, u32[]{:S(2)}) %copy-start.3) | copy-done | bytes 221208
  33.5 0.9 copy-done.5
  34.4 9.0 %first_step.1 = (f32[864,256]{1,0:T(8,128)S(1)}, f32[864,768]{1,0:T(8,128)S(1)}, f32[864,256]{1,0:T(8,128)S(1)}, f32[128,128]{1,0:T(8,128)S(1)}) custom-call(s32[1]{0:T(128)} %bitcast.dir_ref, f32[6912,128]{1,0:T(8,128)S(1)} %bitcast.16, f32[128,128]{1,0:T(8,128)S(1)} %add_add_fusion.1.m0_ref, s32[8,128]{1,0:T(8,128)S(1)} %strip_tags.1.tag_ref, ...), custom_call_target="tpu_custom_call" | custom-call | tf_op jit(solution)/shard_map/first_step/pallas_call | solution.py:477
  43.4 1.1 %inflow.1 = (f32[864,256]{1,0:T(8,128)S(1)}, f32[128,128]{1,0:T(8,128)S(1)}) custom-call(s32[1]{0:T(128)} %bitcast.dir_ref, f32[864,256]{1,0:T(8,128)S(1)} %get-tuple-element.25.c0_any, f32[864,256]{1,0:T(8,128)S(1)} %collective-permute-done.5.halo_any, f32[864,768]{1,0:T(8,128)S(1)} %get-tuple-element.23.coef_ref.coef_any.cx_ref, ...), custom_call_target="tpu_custom_call" | custom-call | tf_op jit(solution)/shard_map/inflow/pallas_call | solution.py:525
  44.6 0.8 collective-permute-start.6
  45.3 20.9 %collective-permute-done.6 = f32[128,128]{1,0:T(8,128)S(1)} collective-permute-done((f32[128,128]{1,0:T(8,128)S(1)}, f32[128,128]{1,0:T(8,128)S(1)}, u32[]{:S(2)}, u32[]{:S(2)}) %collective-permute-start.6) | collective-permute-done | bytes 65568 | tf_op jit(solution)/shard_map/ppermute | solution.py:55
  66.4 1.2 %collective-permute-done.7 = f32[128,128]{1,0:T(8,128)S(1)} collective-permute-done((f32[128,128]{1,0:T(8,128)S(1)}, f32[128,128]{1,0:T(8,128)S(1)}, u32[]{:S(2)}, u32[]{:S(2)}) %collective-permute-start.7) | collective-permute-done | bytes 65568 | tf_op jit(solution)/shard_map/ppermute | solution.py:55
  67.7 1.8 %collective-permute-start.10 = (f32[128,128]{1,0:T(8,128)S(1)}, f32[128,128]{1,0:T(8,128)S(1)}, u32[]{:S(2)}, u32[]{:S(2)}) collective-permute-start(f32[128,128]{1,0:T(8,128)S(1)} %add.36), channel_id=1, source_target_pairs={{0,192},{1,193},{2,194},{3,195},{4,196},{5,197},{6,198},{7,199},{8... | collective-permute-start | bytes 196616 | tf_op jit(solution)/shard_map/ppermute | solution.py:55
  69.8 1.8 %collective-permute-start.8 = (f32[128,128]{1,0:T(8,128)S(1)}, f32[128,128]{1,0:T(8,128)S(1)}, u32[]{:S(2)}, u32[]{:S(2)}) collective-permute-start(f32[128,128]{1,0:T(8,128)S(1)} %add.36), channel_id=1, source_target_pairs={{0,128},{1,129},{2,130},{3,131},{4,132},{5,133},{6,134},{7,135},{8... | collective-permute-start | bytes 196616 | tf_op jit(solution)/shard_map/ppermute | solution.py:55
  72.0 2.0 %collective-permute-done.9 = f32[128,128]{1,0:T(8,128)S(1)} collective-permute-done((f32[128,128]{1,0:T(8,128)S(1)}, f32[128,128]{1,0:T(8,128)S(1)}, u32[]{:S(2)}, u32[]{:S(2)}) %collective-permute-start.9) | collective-permute-done | bytes 65568 | tf_op jit(solution)/shard_map/ppermute | solution.py:55
  74.1 1.5 %collective-permute-done.8 = f32[128,128]{1,0:T(8,128)S(1)} collective-permute-done((f32[128,128]{1,0:T(8,128)S(1)}, f32[128,128]{1,0:T(8,128)S(1)}, u32[]{:S(2)}, u32[]{:S(2)}) %collective-permute-start.8) | collective-permute-done | bytes 65568 | tf_op jit(solution)/shard_map/ppermute | solution.py:55
  75.6 8.7 %second_step.1 = (f32[6912,128]{1,0:T(8,128)S(1)}, f32[4,2,32]{2,1,0:T(2,128)}) custom-call(s32[1]{0:T(128)} %bitcast.dir_ref, f32[864,256]{1,0:T(8,128)S(1)} %get-tuple-element.28.c1_any, f32[864,768]{1,0:T(8,128)S(1)} %get-tuple-element.29.rest_any, f32[128,128]{1,0:T(8,128)S(1)} %add_add_fusion.m0_ref, s32[8,128]{1,0:T(8,128)S(1)} %strip_tags.1.tag_ref, ...), custom_call_target="tpu_custom_call" | custom-call | tf_op jit(solution)/shard_map/second_step/pallas_call | solution.py:568
  84.3 4.6 %collective-permute-done.11.halo_ref = f32[864,256]{1,0:T(8,128)S(1)} collective-permute-done((f32[864,256]{1,0:T(8,128)S(1)}, f32[864,256]{1,0:T(8,128)S(1)}, u32[]{:S(2)}, u32[]{:S(2)}) %collective-permute-start.11) | collective-permute-done | bytes 884768 | tf_op jit(solution)/shard_map/ppermute | solution.py:55
  88.9 2.9 %last.1 = f32[6912,128]{1,0:T(8,128)} custom-call(s32[1]{0:T(128)} %bitcast.dir_ref, f32[6912,128]{1,0:T(8,128)S(1)} %get-tuple-element.33.h_ref, f32[864,256]{1,0:T(8,128)S(1)} %collective-permute-done.11.halo_ref, f32[864,768]{1,0:T(8,128)S(1)} %get-tuple-element.23.coef_ref.coef_any.cx_ref), custom_call_target="tpu_custom_call" | custom-call | tf_op jit(solution)/shard_map/last/pallas_call | solution.py:598
  (23 shorter events, 1.2 us)
Async XLA Ops:
  0.6 23.5 %copy-start.8 = (s32[864]{0:T(1024)S(1)}, s32[864]{0:T(1024)}, u32[]{:S(2)}) copy-start(s32[864]{0:T(1024)} %order_ref.3) | copy-start | bytes 10372
  0.6 2.0 %copy-start = (f32[864,4,256]{2,1,0:T(4,128)S(1)}, f32[864,4,256]{2,1,0:T(4,128)}, u32[]{:S(2)}) copy-start(f32[864,4,256]{2,1,0:T(4,128)} %param.3) | copy-start | bytes 10616836
  2.7 0.7 copy-start.7
  6.6 4.4 %copy-start.4 = (bf16[48,896]{1,0:T(8,128)(2,1)}, bf16[48,896]{1,0:T(8,128)(2,1)S(1)}, u32[]{:S(2)}) copy-start(bf16[48,896]{1,0:T(8,128)(2,1)S(1)} %get-tuple-element.24.left_ref.left_any) | copy-start | bytes 258052
  6.7 4.4 %collective-permute-start = (f32[128,128]{1,0:T(8,128)S(1)}, f32[128,128]{1,0:T(8,128)S(1)}, u32[]{:S(2)}, u32[]{:S(2)}) collective-permute-start(f32[128,128]{1,0:T(8,128)S(1)} %get-tuple-element.20), channel_id=1, source_target_pairs={{0,32},{1,33},{2,34},{3,35},{4,36},{5,37},{6,38},{7,39},{8,40},{9,... | collective-permute-start | bytes 196616 | tf_op jit(solution)/shard_map/ppermute | solution.py:55
  11.0 32.4 %collective-permute-start.5 = (f32[864,256]{1,0:T(8,128)}, f32[864,256]{1,0:T(8,128)S(1)}, u32[]{:S(2)}, u32[]{:S(2)}) collective-permute-start(f32[864,256]{1,0:T(8,128)} %get-tuple-element.26), channel_id=1, source_target_pairs={{0,15},{1,0},{2,1},{3,2},{4,3},{5,4},{6,5},{7,6},{8,7},{9,8},{10,9... | collective-permute-start | bytes 2654216 | tf_op jit(solution)/shard_map/ppermute | solution.py:55
  19.6 1.3 %collective-permute-start.1 = (f32[128,128]{1,0:T(8,128)S(1)}, f32[128,128]{1,0:T(8,128)S(1)}, u32[]{:S(2)}, u32[]{:S(2)}) collective-permute-start(f32[128,128]{1,0:T(8,128)S(1)} %add.30), channel_id=1, source_target_pairs={{0,16},{1,17},{2,18},{3,19},{4,20},{5,21},{6,22},{7,23},{8,24},{9,... | collective-permute-start | bytes 196616 | tf_op jit(solution)/shard_map/ppermute | solution.py:55
  21.5 5.0 %collective-permute-start.4 = (f32[128,128]{1,0:T(8,128)}, f32[128,128]{1,0:T(8,128)}, u32[]{:S(2)}, u32[]{:S(2)}) collective-permute-start(f32[128,128]{1,0:T(8,128)} %add.31), channel_id=1, source_target_pairs={{0,192},{1,193},{2,194},{3,195},{4,196},{5,197},{6,198},{7,199},{8... | collective-permute-start | bytes 196616 | tf_op jit(solution)/shard_map/ppermute | solution.py:55
  22.0 4.9 %collective-permute-start.3 = (f32[128,128]{1,0:T(8,128)}, f32[128,128]{1,0:T(8,128)}, u32[]{:S(2)}, u32[]{:S(2)}) collective-permute-start(f32[128,128]{1,0:T(8,128)} %add.31), channel_id=1, source_target_pairs={{0,64},{1,65},{2,66},{3,67},{4,68},{5,69},{6,70},{7,71},{8,72},{9,... | collective-permute-start | bytes 196616 | tf_op jit(solution)/shard_map/ppermute | solution.py:55
  23.5 6.1 %collective-permute-start.2 = (f32[128,128]{1,0:T(8,128)}, f32[128,128]{1,0:T(8,128)}, u32[]{:S(2)}, u32[]{:S(2)}) collective-permute-start(f32[128,128]{1,0:T(8,128)} %add.31), channel_id=1, source_target_pairs={{0,128},{1,129},{2,130},{3,131},{4,132},{5,133},{6,134},{7,135},{8... | collective-permute-start | bytes 196616 | tf_op jit(solution)/shard_map/ppermute | solution.py:55
  24.8 0.7 copy-start.2
  25.5 0.8 copy-start.6
  30.5 2.0 %copy-start.1 = (f32[864,4,256]{2,1,0:T(4,128)S(1)}, f32[864,4,256]{2,1,0:T(4,128)}, u32[]{:S(2)}) copy-start(f32[864,4,256]{2,1,0:T(4,128)} %param.3) | copy-start | bytes 10616836
  32.5 0.9 %copy-start.3 = (bf16[864,128]{1,0:T(8,128)(2,1)S(1)}, bf16[864,128]{1,0:T(8,128)(2,1)}, u32[]{:S(2)}) copy-start(bf16[864,128]{1,0:T(8,128)(2,1)} %copy-done.2) | copy-start | bytes 663556
  33.5 0.9 copy-start.5
  44.6 21.7 %collective-permute-start.6 = (f32[128,128]{1,0:T(8,128)S(1)}, f32[128,128]{1,0:T(8,128)S(1)}, u32[]{:S(2)}, u32[]{:S(2)}) collective-permute-start(f32[128,128]{1,0:T(8,128)S(1)} %get-tuple-element.31), channel_id=1, source_target_pairs={{0,32},{1,33},{2,34},{3,35},{4,36},{5,37},{6,38},{7,39},{8,40},{9,... | collective-permute-start | bytes 196616 | tf_op jit(solution)/shard_map/ppermute | solution.py:55
  66.3 22.6 %collective-permute-start.11 = (f32[864,256]{1,0:T(8,128)S(1)}, f32[864,256]{1,0:T(8,128)S(1)}, u32[]{:S(2)}, u32[]{:S(2)}) collective-permute-start(f32[864,256]{1,0:T(8,128)S(1)} %get-tuple-element.34), channel_id=1, source_target_pairs={{0,15},{1,0},{2,1},{3,2},{4,3},{5,4},{6,5},{7,6},{8,7},{9,8},{10,9... | collective-permute-start | bytes 2654216 | tf_op jit(solution)/shard_map/ppermute | solution.py:55
  66.3 1.3 %collective-permute-start.7 = (f32[128,128]{1,0:T(8,128)S(1)}, f32[128,128]{1,0:T(8,128)S(1)}, u32[]{:S(2)}, u32[]{:S(2)}) collective-permute-start(f32[128,128]{1,0:T(8,128)S(1)} %add.35), channel_id=1, source_target_pairs={{0,16},{1,17},{2,18},{3,19},{4,20},{5,21},{6,22},{7,23},{8,24},{9,... | collective-permute-start | bytes 196616 | tf_op jit(solution)/shard_map/ppermute | solution.py:55
  67.7 4.3 %collective-permute-start.10 = (f32[128,128]{1,0:T(8,128)S(1)}, f32[128,128]{1,0:T(8,128)S(1)}, u32[]{:S(2)}, u32[]{:S(2)}) collective-permute-start(f32[128,128]{1,0:T(8,128)S(1)} %add.36), channel_id=1, source_target_pairs={{0,192},{1,193},{2,194},{3,195},{4,196},{5,197},{6,198},{7,199},{8... | collective-permute-start | bytes 196616 | tf_op jit(solution)/shard_map/ppermute | solution.py:55
  69.5 4.6 %collective-permute-start.9 = (f32[128,128]{1,0:T(8,128)S(1)}, f32[128,128]{1,0:T(8,128)S(1)}, u32[]{:S(2)}, u32[]{:S(2)}) collective-permute-start(f32[128,128]{1,0:T(8,128)S(1)} %add.36), channel_id=1, source_target_pairs={{0,64},{1,65},{2,66},{3,67},{4,68},{5,69},{6,70},{7,71},{8,72},{9,... | collective-permute-start | bytes 196616 | tf_op jit(solution)/shard_map/ppermute | solution.py:55
  69.8 5.8 %collective-permute-start.8 = (f32[128,128]{1,0:T(8,128)S(1)}, f32[128,128]{1,0:T(8,128)S(1)}, u32[]{:S(2)}, u32[]{:S(2)}) collective-permute-start(f32[128,128]{1,0:T(8,128)S(1)} %add.36), channel_id=1, source_target_pairs={{0,128},{1,129},{2,130},{3,131},{4,132},{5,133},{6,134},{7,135},{8... | collective-permute-start | bytes 196616 | tf_op jit(solution)/shard_map/ppermute | solution.py:55

commit v3 on v2

--- a/solution.py
+++ b/solution.py
@@ -59,16 +59,33 @@
     return permute(value, lambda x, y, c, s: (x, y, c, s - 1 if x < 2 else s + 1))
 
 
-def over_near(part):
+def over_y(part):
     return part + permute(part, lambda x, y, c, s: (x, y ^ 1, c, s))
 
 
+def over_x(part):
+    return part + permute(part, lambda x, y, c, s: (x ^ 1, y, c, s))
+
+
 def over_rest(part):
-    part = part + permute(part, lambda x, y, c, s: (x, y, c ^ 1, s))
-    one = permute(part, lambda x, y, c, s: (x + 1, y, c, s))
-    three = permute(part, lambda x, y, c, s: (x - 1, y, c, s))
-    two = permute(part, lambda x, y, c, s: (x + 2, y, c, s))
-    return (part + two) + (one + three)
+    part = part + permute(part, lambda x, y, c, s: (x ^ 2, y, c, s))
+    return part + permute(part, lambda x, y, c, s: (x, y, c ^ 1, s))
+
+
+def hold(token, *values):
+    def kernel(*refs):
+        del refs
+
+    place = pl.BlockSpec(memory_space=pl.ANY)
+    return pl.pallas_call(
+        kernel,
+        in_specs=[spec()] + [place] * len(values),
+        out_specs=[place] * len(values),
+        out_shape=[shape(*v.shape) for v in values],
+        input_output_aliases={k + 1: k for k in range(len(values))},
+        cost_estimate=cost(HOLD_COST),
+        name="hold",
+    )(token, *values)
 
 
 def upstream_first():
@@ -84,19 +101,28 @@
 
 
 def anywhere():
-    return pl.BlockSpec(memory_space=pl.ANY)
+    return pl.BlockSpec(memory_space=pltpu.HBM)
 
 
 def smem():
     return pl.BlockSpec(memory_space=pltpu.SMEM)
 
 
-def params(mib=8):
-    return pltpu.CompilerParams(vmem_limit_bytes=mib * 2**20)
+def params(mib=63.5):
+    return pltpu.CompilerParams(vmem_limit_bytes=int(mib * 2**20))
+
+
+def cost(us):
+    return pl.CostEstimate(flops=int(us * 1.15e9), bytes_accessed=10_000, transcendentals=0)
 
 
 def shape(*dims, dtype=F32):
     return jax.ShapeDtypeStruct(dims, dtype)
+
+
+def settle(copies):
+    for copy in copies:
+        copy.wait()
 
 
 def fetch(sems, *pairs):
@@ -137,10 +163,10 @@
     for r, a in enumerate(sums):
         table[pl.ds(r, 1), :] = high(a)
         table[pl.ds(24 + r, 1), :] = a - high(a)
-    left_ref[...] = table[...].astype(BF16)
-
-
-def velocity_kernel(order_ref, phi_ref, coef_ref, table, padded):
+    left_ref[...] = table[pl.ds(0, 48), :].astype(BF16)
+
+
+def put_phi(order_ref, padded, table, phi_ref):
     cx, cy, cz, sq, phi = velocity_rows(order_ref, padded)
     zero = jnp.zeros_like(cx)
     down, up = jnp.maximum(-cz, 0.0), jnp.maximum(cz, 0.0)
@@ -160,24 +186,15 @@
         table[pl.ds(r, 1), :] = a
     turned = table[...].T.astype(BF16)
     phi_ref[...] = turned[:NSLOT]
-    row = lax.broadcasted_iota(jnp.int32, (128, 768), 0)
-    lane = lax.broadcasted_iota(jnp.int32, (128, 768), 1)
+
+
+def coefs_of(phi, kinds):
+    row = lax.broadcasted_iota(jnp.int32, (128, 128 * kinds), 0)
+    lane = lax.broadcasted_iota(jnp.int32, (128, 128 * kinds), 1)
     kind, z = lane >> 7, lane & 7
     drop = ((kind == 3) & (z == 0)) | ((kind == 4) & (z == 7))
     pick = ((row == 112 + kind) & jnp.logical_not(drop)).astype(F32).astype(BF16)
-    coef_ref[...] = jnp.dot(turned, pick, preferred_element_type=F32)[:NSLOT] * KD
-
-
-def velocities(order):
-    return pl.pallas_call(
-        velocity_kernel,
-        in_specs=[spec()],
-        out_specs=[spec()] * 2,
-        out_shape=[shape(NSLOT, 128, dtype=BF16), shape(NSLOT, 768)],
-        scratch_shapes=[pltpu.VMEM((128, NPAD), F32), pltpu.VMEM((1, NPAD), jnp.int32)],
-        compiler_params=params(),
-        name="velocities",
-    )(order)
+    return jnp.dot(phi, pick, preferred_element_type=F32) * KD
 
 
 def clear_tail(high_ref, low_ref):
@@ -216,13 +233,22 @@
 
 
 PARTS = 3
-
-
-def unpack_kernel(dir_ref, in_ref, order_ref, near_ref, m_ref, left_ref, whole, high_ref, low_ref, table, padded, sems):
+FIRST_COST, SECOND_COST, HOLD_COST = 6, 2, 3
+
+
+def column_rows(ref, col):
+    return ref.reshape(NSLOT * 2, 4, 128).at[:, col, :]
+
+
+def unpack_kernel(
+    dir_ref, in_ref, order_ref, near_any, m_ref, left_any, phi_any,
+    left_ref, phi_ref, whole, high_ref, low_ref, table, padded, sems, out_sems,
+):
     forward = dir_ref[0]
     size = NSLOT // PARTS
     spans = [pl.ds(p * size * 8, size * 8) for p in range(PARTS)]
     copies = fetch(sems, *[(in_ref.at[a], whole.at[a]) for a in spans])
+    put_phi(order_ref, padded, table, phi_ref)
     put_left(order_ref, padded, table, left_ref)
     clear_tail(high_ref, low_ref)
     step = 96
@@ -237,30 +263,36 @@
                 for half in range(2):
                     start = first * 8 + half * 4 + column_of(forward, i)
                     part = whole[pl.ds(start, step, stride=8), :]
-                    if i == 3:
-                        near_ref[rows, pl.ds(half * 128, 128)] = part
                     split_into(part, rows, pl.ds(i * COL + half * 128, 128), high_ref, low_ref)
             return carry
 
         lax.fori_loop(0, size // step, body, 0)
+    near = column_rows(whole, column_of(forward, 3))
+    outs = fetch(out_sems, (near, near_any), (left_ref, left_any), (phi_ref, phi_any))
     put_moments(forward, left_ref, high_ref, low_ref, m_ref)
+    settle(outs)
 
 
 def unpack(forward, flat, order):
     return pl.pallas_call(
         unpack_kernel,
         in_specs=[smem(), anywhere(), spec()],
-        out_specs=[spec()] * 3,
-        out_shape=[shape(NSLOT, COL), shape(128, 128), shape(48, NPAD, dtype=BF16)],
+        out_specs=[anywhere(), spec(), anywhere(), anywhere()],
+        out_shape=[
+            shape(NSLOT * 2, 128), shape(128, 128), shape(48, NPAD, dtype=BF16), shape(NSLOT, 128, dtype=BF16)
+        ],
         scratch_shapes=[
+            pltpu.VMEM((48, NPAD), BF16),
+            pltpu.VMEM((NSLOT, 128), BF16),
             pltpu.VMEM((NSLOT * 8, 128), F32),
             pltpu.VMEM((NPAD, CELLS), BF16),
             pltpu.VMEM((NPAD, CELLS), BF16),
-            pltpu.VMEM((48, NPAD), F32),
+            pltpu.VMEM((128, NPAD), F32),
             pltpu.VMEM((1, NPAD), jnp.int32),
             pltpu.SemaphoreType.DMA((PARTS,)),
+            pltpu.SemaphoreType.DMA((3,)),
         ],
-        compiler_params=params(16),
+        compiler_params=params(),
         name="unpack",
     )(forward, flat, order)
 
@@ -423,7 +455,7 @@
     return [coef_ref[rows, pl.ds(c * 128, 128)] for c in range(6)]
 
 
-def sweep(column, coef_ref, keep_ref, prod, put):
+def sweep(column, coef_ref, keep_ref, prod, put, start=0, stop=NSLOT):
     step = 32
 
     def body(k, carry):
@@ -440,80 +472,82 @@
             upwind = h
         return carry
 
-    lax.fori_loop(0, NSLOT // step, body, 0)
+    lax.fori_loop(start // step, stop // step, body, 0)
 
 
 def first_kernel(
-    dir_ref, in_ref, m0_ref, tag_ref, phi_ref, coef_ref, left_ref, c0_ref, rest_ref, edge_ref, m_ref,
-    right, keep, table, prod, whole, coef, high_ref, low_ref, sems,
+    dir_ref, in_ref, m0_ref, tag_ref, phi_ref, left_ref, h1_any, edge_any, m_ref,
+    right, keep, table, prod, whole, phi, coef, left, h1, edge, high_ref, low_ref, sems, out_sems,
 ):
     forward = dir_ref[0]
-    copies = fetch(sems, (in_ref, whole), (coef_ref, coef))
+    copies = fetch(sems, (phi_ref, phi), (in_ref, whole), (left_ref, left))
     clear_tail(high_ref, low_ref)
     put_fields(forward, m0_ref, tag_ref, right, keep, table)
-    products(4, phi_ref, right, prod)
-    for copy in copies:
-        copy.wait()
+    copies[0].wait()
+    products(4, phi, right, prod)
+    coef[...] = coefs_of(phi[...], 6)
+    settle(copies[1:])
 
     def column(i, hf, first, step):
         return whole[pl.ds(first * 8 + hf * 4 + column_of(forward, i), step, stride=8), :]
 
     def put(i, hf, first, step, new):
         rows = pl.ds(first, step)
-        side = pl.ds(hf * 128, 128)
-        if i == 0:
-            c0_ref[rows, side] = new
-        else:
-            rest_ref[rows, pl.ds((i - 1) * COL + hf * 128, 128)] = new
+        cols = pl.ds(i * COL + hf * 128, 128)
+        h1[rows, cols] = new
         if i == 3:
-            edge_ref[rows, side] = new
-        split_into(new, rows, pl.ds(i * COL + hf * 128, 128), high_ref, low_ref)
-
-    sweep(column, coef, keep, prod, put)
-    put_moments(forward, left_ref, high_ref, low_ref, m_ref)
-
-
-def first_step(forward, flat, m, tags, phi, coef, left):
+            edge[pl.ds(first * 2 + hf, step, stride=2), :] = new
+        split_into(new, rows, cols, high_ref, low_ref)
+
+    size = NSLOT // PARTS
+    outs = []
+    for p in range(PARTS):
+        sweep(column, coef, keep, prod, put, p * size, p * size + size)
+        rows = pl.ds(p * size, size)
+        outs.append(pltpu.make_async_copy(h1.at[rows], h1_any.at[rows], out_sems.at[p]))
+        outs[-1].start()
+    outs.append(pltpu.make_async_copy(edge, edge_any, out_sems.at[PARTS]))
+    outs[-1].start()
+    put_moments(forward, left, high_ref, low_ref, m_ref)
+    settle(outs)
+
+
+def first_step(forward, flat, m, tags, phi, left):
     return pl.pallas_call(
         first_kernel,
-        in_specs=[smem(), anywhere(), spec(), spec(), spec(), anywhere(), spec()],
-        out_specs=[spec()] * 4,
-        out_shape=[shape(NSLOT, COL), shape(NSLOT, 3 * COL), shape(NSLOT, COL), shape(128, 128)],
+        in_specs=[smem(), anywhere(), spec(), spec(), anywhere(), anywhere()],
+        out_specs=[anywhere(), anywhere(), spec()],
+        out_shape=[shape(NSLOT, CELLS), shape(NSLOT * 2, 128), shape(128, 128)],
         scratch_shapes=field_scratch()
         + [
             pltpu.VMEM((NSLOT, 3 * CELLS), F32),
             pltpu.VMEM((NSLOT * 8, 128), F32),
+            pltpu.VMEM((NSLOT, 128), BF16),
             pltpu.VMEM((NSLOT, 768), F32),
+            pltpu.VMEM((48, NPAD), BF16),
+            pltpu.VMEM((NSLOT, CELLS), F32),
+            pltpu.VMEM((NSLOT * 2, 128), F32),
             pltpu.VMEM((NPAD, CELLS), BF16),
             pltpu.VMEM((NPAD, CELLS), BF16),
-            pltpu.SemaphoreType.DMA((2,)),
+            pltpu.SemaphoreType.DMA((3,)),
+            pltpu.SemaphoreType.DMA((PARTS + 1,)),
         ],
-        compiler_params=params(32),
+        compiler_params=params(),
+        cost_estimate=cost(FIRST_COST),
         name="first_step",
-    )(forward, flat, m, tags, phi, coef, left)
-
-
-def inflow_kernel(
-    dir_ref, c0_any, halo_any, coef_any, left_any, m_ref, c1_ref, out_ref, c0, halo, coef, left, high_ref, low_ref, sems
-):
-    copies = fetch(sems, (halo_any, halo), (c0_any, c0), (coef_any.at[:, pl.ds(0, 128)], coef), (left_any, left))
+    )(forward, flat, m, tags, phi, left)
+
+
+def inflow_kernel(dir_ref, halo_any, phi_any, left_any, m_ref, out_ref, halo, phi, left, high_ref, low_ref, sems):
+    copies = fetch(sems, (phi_any, phi), (halo_any, halo), (left_any, left))
     clear_tail(high_ref, low_ref)
     out_ref[...] = m_ref[...]
-    for copy in copies:
-        copy.wait()
-    step = 48
-
-    def body(k, carry):
-        rows = pl.ds(pl.multiple_of(k * step, 16), step)
-        cx = coef[rows, :]
-        for half in range(2):
-            cols = pl.ds(half * 128, 128)
-            share = cx * halo[rows, cols]
-            c1_ref[rows, cols] = c0[rows, cols] + share
-            split_into(share, rows, cols, high_ref, low_ref)
-        return carry
-
-    lax.fori_loop(0, NSLOT // step, body, 0)
+    copies[0].wait()
+    cx = coefs_of(phi[...], 1)
+    settle(copies[1:])
+    for half in range(2):
+        share = cx * halo[pl.ds(half, NSLOT, stride=2), :]
+        split_into(share, pl.ds(0, NSLOT), pl.ds(half * 128, 128), high_ref, low_ref)
     row = column_of(dir_ref[0], 0) * 2
     for half, parts in enumerate(sums_of(left[...], high_ref[...], low_ref[...])):
         for k, part in enumerate(parts):
@@ -521,115 +555,134 @@
             out_ref[at, :] = m_ref[at, :] + part
 
 
-def inflow(forward, c0, halo, coef, left, m):
+def inflow(forward, halo, phi, left, m):
     return pl.pallas_call(
         inflow_kernel,
-        in_specs=[smem()] + [anywhere()] * 4 + [spec()],
-        out_specs=[spec()] * 2,
-        out_shape=[shape(NSLOT, COL), shape(128, 128)],
+        in_specs=[smem()] + [anywhere()] * 3 + [spec()],
+        out_specs=spec(),
+        out_shape=shape(128, 128),
         scratch_shapes=[
-            pltpu.VMEM((NSLOT, COL), F32),
-            pltpu.VMEM((NSLOT, COL), F32),
-            pltpu.VMEM((NSLOT, 128), F32),
+            pltpu.VMEM((NSLOT * 2, 128), F32),
+            pltpu.VMEM((NSLOT, 128), BF16),
             pltpu.VMEM((48, NPAD), BF16),
             pltpu.VMEM((NPAD, COL), BF16),
             pltpu.VMEM((NPAD, COL), BF16),
-            pltpu.SemaphoreType.DMA((4,)),
+            pltpu.SemaphoreType.DMA((3,)),
         ],
         compiler_params=params(),
         name="inflow",
-    )(forward, c0, halo, coef, left, m)
+    )(forward, halo, phi, left, m)
 
 
 def second_kernel(
-    dir_ref, c1_any, rest_any, m0_ref, tag_ref, phi_ref, coef_any, out_ref, heat_ref,
-    right, keep, table, prod, c1, rest, coef, sems,
+    dir_ref, h_any, halo_any, m0_ref, tag_ref, phi_any, out_any, pre_any, heat_ref,
+    right, keep, table, prod, h, halo, phi, coef, out_ref, pre_ref, sems, out_sems,
 ):
     forward = dir_ref[0]
-    copies = fetch(sems, (c1_any, c1), (rest_any, rest), (coef_any, coef))
+    copies = fetch(sems, (phi_any, phi), (h_any, h), (halo_any, halo))
     heat = put_fields(forward, m0_ref, tag_ref, right, keep, table)
     put_heat(heat, table, heat_ref)
-    products(4, phi_ref, right, prod)
-    for copy in copies:
-        copy.wait()
+    copies[0].wait()
+    products(4, phi, right, prod)
+    coef[...] = coefs_of(phi[...], 6)
+    settle(copies[1:])
 
     def column(i, hf, first, step):
+        rows = pl.ds(first, step)
+        state = h[rows, pl.ds(i * COL + hf * 128, 128)]
         if i == 0:
-            return c1[pl.ds(first, step), pl.ds(hf * 128, 128)]
-        return rest[pl.ds(first, step), pl.ds((i - 1) * COL + hf * 128, 128)]
+            state = state + coef[rows, pl.ds(0, 128)] * halo[pl.ds(first * 2 + hf, step, stride=2), :]
+        return state
 
     def put(i, hf, first, step, new):
         out_ref[pl.ds(first * 8 + hf * 4 + column_of(forward, i), step, stride=8), :] = new
-
-    sweep(column, coef, keep, prod, put)
-
-
-def second_step(forward, c1, rest, m, tags, phi, coef):
+        if i == 0:
+            pre_ref[pl.ds(first * 2 + hf, step, stride=2), :] = new
+
+    size = NSLOT // PARTS
+    outs = []
+    for p in range(PARTS):
+        sweep(column, coef, keep, prod, put, p * size, p * size + size)
+        rows = pl.ds(p * size * 8, size * 8)
+        outs.append(pltpu.make_async_copy(out_ref.at[rows], out_any.at[rows], out_sems.at[p]))
+        outs[-1].start()
+    outs.append(pltpu.make_async_copy(pre_ref, pre_any, out_sems.at[PARTS]))
+    outs[-1].start()
+    settle(outs)
+
+
+def second_step(forward, h, halo, m, tags, phi):
     return pl.pallas_call(
         second_kernel,
-        in_specs=[smem(), anywhere(), anywhere(), spec(), spec(), spec(), anywhere()],
-        out_specs=[spec()] * 2,
-        out_shape=[shape(NSLOT * 8, 128), shape(4, 2, 32)],
+        in_specs=[smem(), anywhere(), anywhere(), spec(), spec(), anywhere()],
+        out_specs=[anywhere(), anywhere(), spec()],
+        out_shape=[shape(NSLOT * 8, 128), shape(NSLOT * 2, 128), shape(4, 2, 32)],
         scratch_shapes=field_scratch()
         + [
             pltpu.VMEM((NSLOT, 3 * CELLS), F32),
-            pltpu.VMEM((NSLOT, COL), F32),
-            pltpu.VMEM((NSLOT, 3 * COL), F32),
+            pltpu.VMEM((NSLOT, CELLS), F32),
+            pltpu.VMEM((NSLOT * 2, 128), F32),
+            pltpu.VMEM((NSLOT, 128), BF16),
             pltpu.VMEM((NSLOT, 768), F32),
+            pltpu.VMEM((NSLOT * 8, 128), F32),
+            pltpu.VMEM((NSLOT * 2, 128), F32),
             pltpu.SemaphoreType.DMA((3,)),
+            pltpu.SemaphoreType.DMA((PARTS + 1,)),
         ],
-        compiler_params=params(32),
+        compiler_params=params(),
+        cost_estimate=cost(SECOND_COST),
         name="second_step",
-    )(forward, c1, rest, m, tags, phi, coef)
-
-
-def last_kernel(dir_ref, h_ref, halo_ref, cx_ref, out_ref):
-    step = halo_ref.shape[0]
-    col = column_of(dir_ref[0], 0)
-    out_ref[...] = h_ref[...]
-    cx = cx_ref[...]
+    )(forward, h, halo, m, tags, phi)
+
+
+def last_kernel(dir_ref, h_any, pre_any, halo_any, phi_any, out_any, pre, halo, phi, sems, out_sems):
+    del h_any
+    copies = fetch(sems, (phi_any, phi), (pre_any, pre), (halo_any, halo))
+    copies[0].wait()
+    cx = coefs_of(phi[...], 1)
+    settle(copies[1:])
     for half in range(2):
-        at = pl.ds(half * 4 + col, step, stride=8)
-        out_ref[at, :] = h_ref[at, :] + cx * halo_ref[:, pl.ds(half * 128, 128)]
-
-
-def last(forward, h, halo, coef):
-    step = 144
+        at = pl.ds(half, NSLOT, stride=2)
+        pre[at, :] = pre[at, :] + cx * halo[at, :]
+    settle(fetch(out_sems, (pre, column_rows(out_any, column_of(dir_ref[0], 0)))))
+
+
+def last(forward, h, pre, halo, phi):
     return pl.pallas_call(
         last_kernel,
-        grid=(NSLOT // step,),
-        in_specs=[
-            smem(),
-            pl.BlockSpec((step * 8, 128), lambda i: (i, 0)),
-            pl.BlockSpec((step, COL), lambda i: (i, 0)),
-            pl.BlockSpec((step, 128), lambda i: (i, 0)),
+        in_specs=[smem()] + [anywhere()] * 4,
+        out_specs=anywhere(),
+        out_shape=shape(NSLOT * 8, 128),
+        input_output_aliases={1: 0},
+        scratch_shapes=[
+            pltpu.VMEM((NSLOT * 2, 128), F32),
+            pltpu.VMEM((NSLOT * 2, 128), F32),
+            pltpu.VMEM((NSLOT, 128), BF16),
+            pltpu.SemaphoreType.DMA((3,)),
+            pltpu.SemaphoreType.DMA((1,)),
         ],
-        out_specs=pl.BlockSpec((step * 8, 128), lambda i: (i, 0)),
-        out_shape=shape(NSLOT * 8, 128),
         compiler_params=params(),
         name="last",
-    )(forward, h, halo, coef)
+    )(forward, h, pre, halo, phi)
 
 
 def body(state, velocity_order, wall_tag):
     forward = upstream_first().reshape(1)
     at = lax.axis_index("space").astype(jnp.int32).reshape(1)
     flat = state.reshape(NSLOT, 4, 2, 128).transpose(0, 2, 1, 3).reshape(NSLOT * 8, 128)
-    near, m1, left = unpack(forward, flat, velocity_order)
-    m1 = over_near(m1)
-    near, m1 = lax.optimization_barrier((near, m1))
-    halo = downstream(near)
-    phi, coef = velocities(velocity_order)
+    near, m, left, phi = unpack(forward, flat, velocity_order)
+    m = over_y(m)
+    (near,) = hold(m, near)
+    near = downstream(near)
     tags = strip_tags(at, jnp.transpose(wall_tag, (1, 2, 0)).reshape(64, 64))
-    m1 = over_rest(m1)
-    c0, rest, edge, m2 = first_step(forward, flat, m1, tags, phi, coef, left)
-    c1, m2 = inflow(forward, c0, halo, coef, left, m2)
-    m2 = over_near(m2)
-    edge, m2 = lax.optimization_barrier((edge, m2))
-    halo = downstream(edge)
-    m2 = over_rest(m2)
-    out, wall_heat = second_step(forward, c1, rest, m2, tags, phi, coef)
-    out = last(forward, out, halo, coef)
+    m = over_rest(over_x(m))
+    h1, edge, m = first_step(forward, flat, m, tags, phi, left)
+    m = over_x(over_y(inflow(forward, near, phi, left, m)))
+    (edge,) = hold(m, edge)
+    edge = downstream(edge)
+    m = over_rest(m)
+    out, pre, wall_heat = second_step(forward, h1, near, m, tags, phi)
+    out = last(forward, out, pre, edge, phi)
     state_next = out.reshape(NSLOT, 2, 4, 128).transpose(0, 2, 1, 3).reshape(NSLOT, 4, 256)
     return state_next, wall_heat
 

time: 92.2 us -> 85.5 us (0.927)
  the two profiles are of different devices: /device:TPU:2 before, /device:TPU:4 now
where the time goes in v3:
time: 85.5 us; the launch traced here: 84.4 us
  Pallas kernels  37.3 us (44%)
  waiting for transfers between devices  22.5 us (26%)
  starting transfers between devices  19.5 us (23%)
  other arithmetic  4.27 us (5%)
  between operations  0.88 us (1%)
    ppermute x10, waiting for transfers between devices, permute(): lax.ppermute(value, AXES, [(i, index_of(*move(*device_of(i)))) for i in r...  22.5 us
    ppermute x10, starting transfers between devices, permute(): lax.ppermute(value, AXES, [(i, index_of(*move(*device_of(i)))) for i in r...  19.5 us
    pallas_call x1, Pallas kernels, second_step(): pl.pallas_call(second_kernel, in_specs=[smem(), anywhere(), anywhere(), s...  11.7 us
    pallas_call x1, Pallas kernels, first_step(): pl.pallas_call(first_kernel, in_specs=[smem(), anywhere(), spec(), spec()...  11.6 us
    pallas_call x1, Pallas kernels, unpack(): pl.pallas_call(unpack_kernel, in_specs=[smem(), anywhere(), spec()], out_...  4.67 us
    pallas_call x1, Pallas kernels, inflow(): pl.pallas_call(inflow_kernel, in_specs=[smem()] + [anywhere()] * 3 + [spe...  3.2 us
    pallas_call x1, Pallas kernels, last(): pl.pallas_call(last_kernel, in_specs=[smem()] + [anywhere()] * 4, out_spe...  2.67 us
    add x2, other arithmetic, over_y(): return part + permute(part, lambda x, y, c, s: (x, y ^ 1, c, s))  2.33 us
  transfers between devices with their start and end apart: 10, of which 8 were waited for; matrix products, arithmetic and copies ran while one was open for 2% of the time, Pallas kernels for 30%

profile of v3, /device:TPU:4, one launch (start us, length us, event | category | flops | bytes accessed | tf_op | source)
XLA Modules:
  0.0 84.4 jit_solution(1711121525926955618)
XLA Ops:
  0.6 4.7 %unpack.1 = (f32[1728,128]{1,0:T(8,128)}, f32[128,128]{1,0:T(8,128)}, bf16[48,896]{1,0:T(8,128)(2,1)}, bf16[864,128]{1,0:T(8,128)(2,1)}) custom-call(s32[1]{0:T(128)} %bitcast.dir_ref, f32[6912,128]{1,0:T(8,128)} %bitcast.15, s32[864]{0:T(1024)} %order_ref.1), custom_call_target="tpu_custom_call" | custom-call | tf_op jit(solution)/shard_map/unpack/pallas_call | solution.py:277
  5.3 1.7 %collective-permute-start = (f32[128,128]{1,0:T(8,128)}, f32[128,128]{1,0:T(8,128)S(1)}, u32[]{:S(2)}, u32[]{:S(2)}) collective-permute-start(f32[128,128]{1,0:T(8,128)} %get-tuple-element.12), channel_id=1, source_target_pairs={{0,32},{1,33},{2,34},{3,35},{4,36},{5,37},{6,38},{7,39},{8,40},{9,... | collective-permute-start | bytes 196616 | tf_op jit(solution)/shard_map/ppermute | solution.py:55
  7.0 2.9 %collective-permute-done = f32[128,128]{1,0:T(8,128)S(1)} collective-permute-done((f32[128,128]{1,0:T(8,128)}, f32[128,128]{1,0:T(8,128)S(1)}, u32[]{:S(2)}, u32[]{:S(2)}) %collective-permute-start) | collective-permute-done | bytes 65568 | tf_op jit(solution)/shard_map/ppermute | solution.py:55
  9.9 1.5 %add.24.refs_0_ = f32[128,128]{1,0:T(8,128)} add(f32[128,128]{1,0:T(8,128)} %get-tuple-element.12, f32[128,128]{1,0:T(8,128)S(1)} %collective-permute-done) | non-fusion elementwise | flops 16384 | bytes 196608 | tf_op jit(solution)/shard_map/add | solution.py:63
  11.4 0.9 %hold.2 = f32[1728,128]{1,0:T(8,128)} custom-call(f32[128,128]{1,0:T(8,128)} %add.24.refs_0_, f32[1728,128]{1,0:T(8,128)} %get-tuple-element.16.refs_1_), custom_call_target="tpu_custom_call", output_to_operand_aliasing={{}: (1, {})} | custom-call | flops 3449999872 | bytes 10000 | tf_op jit(solution)/shard_map/hold/pallas_call | solution.py:80
  12.3 3.2 %collective-permute-start.4 = (f32[1728,128]{1,0:T(8,128)}, f32[1728,128]{1,0:T(8,128)}, u32[]{:S(2)}, u32[]{:S(2)}) collective-permute-start(f32[1728,128]{1,0:T(8,128)} %hold.2), channel_id=1, source_target_pairs={{0,15},{1,0},{2,1},{3,2},{4,3},{5,4},{6,5},{7,6},{8,7},{9,8},{10,9... | collective-permute-start | bytes 2654216 | tf_op jit(solution)/shard_map/ppermute | solution.py:55
  15.5 1.2 %collective-permute-start.1 = (f32[128,128]{1,0:T(8,128)S(1)}, f32[128,128]{1,0:T(8,128)S(1)}, u32[]{:S(2)}, u32[]{:S(2)}) collective-permute-start(f32[128,128]{1,0:T(8,128)S(1)} %copy-done), channel_id=1, source_target_pairs={{0,64},{1,65},{2,66},{3,67},{4,68},{5,69},{6,70},{7,71},{8,72},{9,... | collective-permute-start | bytes 196616 | tf_op jit(solution)/shard_map/ppermute | solution.py:55
  16.7 3.1 %collective-permute-done.1 = f32[128,128]{1,0:T(8,128)S(1)} collective-permute-done((f32[128,128]{1,0:T(8,128)S(1)}, f32[128,128]{1,0:T(8,128)S(1)}, u32[]{:S(2)}, u32[]{:S(2)}) %collective-permute-start.1) | collective-permute-done | bytes 65568 | tf_op jit(solution)/shard_map/ppermute | solution.py:55
  19.8 5.9 %collective-permute-start.2 = (f32[128,128]{1,0:T(8,128)S(1)}, f32[128,128]{1,0:T(8,128)S(1)}, u32[]{:S(2)}, u32[]{:S(2)}) collective-permute-start(f32[128,128]{1,0:T(8,128)S(1)} %add.25), channel_id=1, source_target_pairs={{0,128},{1,129},{2,130},{3,131},{4,132},{5,133},{6,134},{7,135},{8... | collective-permute-start | bytes 196616 | tf_op jit(solution)/shard_map/ppermute | solution.py:55
  25.6 2.2 %collective-permute-done.2 = f32[128,128]{1,0:T(8,128)S(1)} collective-permute-done((f32[128,128]{1,0:T(8,128)S(1)}, f32[128,128]{1,0:T(8,128)S(1)}, u32[]{:S(2)}, u32[]{:S(2)}) %collective-permute-start.2) | collective-permute-done | bytes 65568 | tf_op jit(solution)/shard_map/ppermute | solution.py:55
  27.9 0.1 collective-permute-start.3
  28.0 1.6 %strip_tags.1.tag_ref = s32[8,128]{1,0:T(8,128)} custom-call(s32[1]{0:T(128)} %bitcast.6.at_ref, s32[64,64]{1,0:T(8,128)} %bitcast.18), custom_call_target="tpu_custom_call" | custom-call | tf_op jit(solution)/shard_map/strip_tags/pallas_call | solution.py:316
  29.6 0.0 collective-permute-done.3
  29.6 0.6 add.27.m0_ref
  30.2 11.6 %first_step.1 = (f32[864,1024]{1,0:T(8,128)}, f32[1728,128]{1,0:T(8,128)}, f32[128,128]{1,0:T(8,128)}) custom-call(s32[1]{0:T(128)} %bitcast.dir_ref, f32[6912,128]{1,0:T(8,128)} %bitcast.16, f32[128,128]{1,0:T(8,128)} %add.27.m0_ref, s32[8,128]{1,0:T(8,128)} %strip_tags.1.tag_ref, bf16[864,128]{1,0:T(8,128)(2,1)} %get-tuple-element.13.phi_ref.phi_any, ...), custom_call_target="tpu_custom_call" | custom-call | flops 6899999744 | bytes 10000 | tf_op jit(solution)/shard_map/first_step/pallas_call | solution.py:516
  41.9 3.2 %inflow.1 = f32[128,128]{1,0:T(8,128)} custom-call(s32[1]{0:T(128)} %bitcast.dir_ref, f32[1728,128]{1,0:T(8,128)} %collective-permute-done.4.halo_any, bf16[864,128]{1,0:T(8,128)(2,1)} %get-tuple-element.13.phi_ref.phi_any, bf16[48,896]{1,0:T(8,128)(2,1)} %get-tuple-element.14.left_ref.left_any, f32[128,128]{1,0:T(8,128)} %get-tuple-element.17.m_ref), custom_call_target="tpu_custom_call" | custom-call | tf_op jit(solution)/shard_map/inflow/pallas_call | solution.py:559
  45.1 0.8 collective-permute-start.5
  45.9 4.0 %collective-permute-done.5 = f32[128,128]{1,0:T(8,128)S(1)} collective-permute-done((f32[128,128]{1,0:T(8,128)}, f32[128,128]{1,0:T(8,128)S(1)}, u32[]{:S(2)}, u32[]{:S(2)}) %collective-permute-start.5) | collective-permute-done | bytes 65568 | tf_op jit(solution)/shard_map/ppermute | solution.py:55
  49.9 0.9 %add.28 = f32[128,128]{1,0:T(8,128)S(1)} add(f32[128,128]{1,0:T(8,128)} %inflow.1, f32[128,128]{1,0:T(8,128)S(1)} %collective-permute-done.5) | non-fusion elementwise | flops 16384 | bytes 196608 | tf_op jit(solution)/shard_map/add | solution.py:63
  50.7 2.7 %collective-permute-start.6 = (f32[128,128]{1,0:T(8,128)S(1)}, f32[128,128]{1,0:T(8,128)S(1)}, u32[]{:S(2)}, u32[]{:S(2)}) collective-permute-start(f32[128,128]{1,0:T(8,128)S(1)} %add.28), channel_id=1, source_target_pairs={{0,64},{1,65},{2,66},{3,67},{4,68},{5,69},{6,70},{7,71},{8,72},{9,... | collective-permute-start | bytes 196616 | tf_op jit(solution)/shard_map/ppermute | solution.py:55
  53.5 2.2 %collective-permute-done.6 = f32[128,128]{1,0:T(8,128)S(1)} collective-permute-done((f32[128,128]{1,0:T(8,128)S(1)}, f32[128,128]{1,0:T(8,128)S(1)}, u32[]{:S(2)}, u32[]{:S(2)}) %collective-permute-start.6) | collective-permute-done | bytes 65568 | tf_op jit(solution)/shard_map/ppermute | solution.py:55
  55.7 0.6 add.29.refs_0_
  56.3 0.9 %hold.3 = f32[1728,128]{1,0:T(8,128)} custom-call(f32[128,128]{1,0:T(8,128)} %add.29.refs_0_, f32[1728,128]{1,0:T(8,128)} %get-tuple-element.20.refs_1_), custom_call_target="tpu_custom_call", output_to_operand_aliasing={{}: (1, {})} | custom-call | flops 3449999872 | bytes 10000 | tf_op jit(solution)/shard_map/hold/pallas_call | solution.py:80
  57.3 0.0 collective-permute-start.9
  57.3 3.7 %collective-permute-start.7 = (f32[128,128]{1,0:T(8,128)S(1)}, f32[128,128]{1,0:T(8,128)S(1)}, u32[]{:S(2)}, u32[]{:S(2)}) collective-permute-start(f32[128,128]{1,0:T(8,128)S(1)} %copy-done.1), channel_id=1, source_target_pairs={{0,128},{1,129},{2,130},{3,131},{4,132},{5,133},{6,134},{7,135},{8... | collective-permute-start | bytes 196616 | tf_op jit(solution)/shard_map/ppermute | solution.py:55
  60.9 2.2 %collective-permute-done.7 = f32[128,128]{1,0:T(8,128)S(1)} collective-permute-done((f32[128,128]{1,0:T(8,128)S(1)}, f32[128,128]{1,0:T(8,128)S(1)}, u32[]{:S(2)}, u32[]{:S(2)}) %collective-permute-start.7) | collective-permute-done | bytes 65568 | tf_op jit(solution)/shard_map/ppermute | solution.py:55
  63.2 0.3 collective-permute-start.8
  63.5 1.2 %collective-permute-done.8 = f32[128,128]{1,0:T(8,128)S(1)} collective-permute-done((f32[128,128]{1,0:T(8,128)S(1)}, f32[128,128]{1,0:T(8,128)S(1)}, u32[]{:S(2)}, u32[]{:S(2)}) %collective-permute-start.8) | collective-permute-done | bytes 65568 | tf_op jit(solution)/shard_map/ppermute | solution.py:55
  64.7 0.6 add.31.m0_ref
  65.4 11.7 %second_step.1 = (f32[6912,128]{1,0:T(8,128)}, f32[1728,128]{1,0:T(8,128)}, f32[4,2,32]{2,1,0:T(2,128)}) custom-call(s32[1]{0:T(128)} %bitcast.dir_ref, f32[864,1024]{1,0:T(8,128)} %get-tuple-element.15.h_any, f32[1728,128]{1,0:T(8,128)} %collective-permute-done.4.halo_any, f32[128,128]{1,0:T(8,128)} %add.31.m0_ref, s32[8,128]{1,0:T(8,128)} %strip_tags.1.tag_ref, ...), custom_call_target="tpu_custom_call" | custom-call | flops 2300000000 | bytes 10000 | tf_op jit(solution)/shard_map/second_step/pallas_call | solution.py:615
  77.1 4.5 %collective-permute-done.9.halo_any = f32[1728,128]{1,0:T(8,128)} collective-permute-done((f32[1728,128]{1,0:T(8,128)}, f32[1728,128]{1,0:T(8,128)}, u32[]{:S(2)}, u32[]{:S(2)}) %collective-permute-start.9) | collective-permute-done | bytes 884768 | tf_op jit(solution)/shard_map/ppermute | solution.py:55
  81.6 2.7 %last.1 = f32[6912,128]{1,0:T(8,128)} custom-call(s32[1]{0:T(128)} %bitcast.dir_ref, f32[6912,128]{1,0:T(8,128)} %get-tuple-element.18.h_any, f32[1728,128]{1,0:T(8,128)} %get-tuple-element.19.pre_any, f32[1728,128]{1,0:T(8,128)} %collective-permute-done.9.halo_any, bf16[864,128]{1,0:T(8,128)(2,1)} %get-tuple-element.13.phi_ref.phi_any), custom_call_target="tpu_custom_call", output_to_operand_aliasing={{}: (1, {})} | custom-call | tf_op jit(solution)/shard_map/last/pallas_call | solution.py:651
  (8 shorter events, 0.0 us)
Async XLA Ops:
  5.3 4.6 %collective-permute-start = (f32[128,128]{1,0:T(8,128)}, f32[128,128]{1,0:T(8,128)S(1)}, u32[]{:S(2)}, u32[]{:S(2)}) collective-permute-start(f32[128,128]{1,0:T(8,128)} %get-tuple-element.12), channel_id=1, source_target_pairs={{0,32},{1,33},{2,34},{3,35},{4,36},{5,37},{6,38},{7,39},{8,40},{9,... | collective-permute-start | bytes 196616 | tf_op jit(solution)/shard_map/ppermute | solution.py:55
  11.4 4.1 %copy-start = (f32[128,128]{1,0:T(8,128)S(1)}, f32[128,128]{1,0:T(8,128)}, u32[]{:S(2)}) copy-start(f32[128,128]{1,0:T(8,128)} %add.24.refs_0_) | copy-start | bytes 196612
  12.3 29.6 %collective-permute-start.4 = (f32[1728,128]{1,0:T(8,128)}, f32[1728,128]{1,0:T(8,128)}, u32[]{:S(2)}, u32[]{:S(2)}) collective-permute-start(f32[1728,128]{1,0:T(8,128)} %hold.2), channel_id=1, source_target_pairs={{0,15},{1,0},{2,1},{3,2},{4,3},{5,4},{6,5},{7,6},{8,7},{9,8},{10,9... | collective-permute-start | bytes 2654216 | tf_op jit(solution)/shard_map/ppermute | solution.py:55
  15.5 4.3 %collective-permute-start.1 = (f32[128,128]{1,0:T(8,128)S(1)}, f32[128,128]{1,0:T(8,128)S(1)}, u32[]{:S(2)}, u32[]{:S(2)}) collective-permute-start(f32[128,128]{1,0:T(8,128)S(1)} %copy-done), channel_id=1, source_target_pairs={{0,64},{1,65},{2,66},{3,67},{4,68},{5,69},{6,70},{7,71},{8,72},{9,... | collective-permute-start | bytes 196616 | tf_op jit(solution)/shard_map/ppermute | solution.py:55
  19.8 8.1 %collective-permute-start.2 = (f32[128,128]{1,0:T(8,128)S(1)}, f32[128,128]{1,0:T(8,128)S(1)}, u32[]{:S(2)}, u32[]{:S(2)}) collective-permute-start(f32[128,128]{1,0:T(8,128)S(1)} %add.25), channel_id=1, source_target_pairs={{0,128},{1,129},{2,130},{3,131},{4,132},{5,133},{6,134},{7,135},{8... | collective-permute-start | bytes 196616 | tf_op jit(solution)/shard_map/ppermute | solution.py:55
  27.9 1.7 %collective-permute-start.3 = (f32[128,128]{1,0:T(8,128)S(1)}, f32[128,128]{1,0:T(8,128)S(1)}, u32[]{:S(2)}, u32[]{:S(2)}) collective-permute-start(f32[128,128]{1,0:T(8,128)S(1)} %add.26), channel_id=1, source_target_pairs={{0,16},{1,17},{2,18},{3,19},{4,20},{5,21},{6,22},{7,23},{8,24},{9,... | collective-permute-start | bytes 196616 | tf_op jit(solution)/shard_map/ppermute | solution.py:55
  45.1 4.8 %collective-permute-start.5 = (f32[128,128]{1,0:T(8,128)}, f32[128,128]{1,0:T(8,128)S(1)}, u32[]{:S(2)}, u32[]{:S(2)}) collective-permute-start(f32[128,128]{1,0:T(8,128)} %inflow.1), channel_id=1, source_target_pairs={{0,32},{1,33},{2,34},{3,35},{4,36},{5,37},{6,38},{7,39},{8,40},{9,... | collective-permute-start | bytes 196616 | tf_op jit(solution)/shard_map/ppermute | solution.py:55
  50.7 5.0 %collective-permute-start.6 = (f32[128,128]{1,0:T(8,128)S(1)}, f32[128,128]{1,0:T(8,128)S(1)}, u32[]{:S(2)}, u32[]{:S(2)}) collective-permute-start(f32[128,128]{1,0:T(8,128)S(1)} %add.28), channel_id=1, source_target_pairs={{0,64},{1,65},{2,66},{3,67},{4,68},{5,69},{6,70},{7,71},{8,72},{9,... | collective-permute-start | bytes 196616 | tf_op jit(solution)/shard_map/ppermute | solution.py:55
  56.3 0.9 %copy-start.1 = (f32[128,128]{1,0:T(8,128)S(1)}, f32[128,128]{1,0:T(8,128)}, u32[]{:S(2)}) copy-start(f32[128,128]{1,0:T(8,128)} %add.29.refs_0_) | copy-start | bytes 196612
  57.3 24.3 %collective-permute-start.9 = (f32[1728,128]{1,0:T(8,128)}, f32[1728,128]{1,0:T(8,128)}, u32[]{:S(2)}, u32[]{:S(2)}) collective-permute-start(f32[1728,128]{1,0:T(8,128)} %hold.3), channel_id=1, source_target_pairs={{0,15},{1,0},{2,1},{3,2},{4,3},{5,4},{6,5},{7,6},{8,7},{9,8},{10,9... | collective-permute-start | bytes 2654216 | tf_op jit(solution)/shard_map/ppermute | solution.py:55
  57.3 5.9 %collective-permute-start.7 = (f32[128,128]{1,0:T(8,128)S(1)}, f32[128,128]{1,0:T(8,128)S(1)}, u32[]{:S(2)}, u32[]{:S(2)}) collective-permute-start(f32[128,128]{1,0:T(8,128)S(1)} %copy-done.1), channel_id=1, source_target_pairs={{0,128},{1,129},{2,130},{3,131},{4,132},{5,133},{6,134},{7,135},{8... | collective-permute-start | bytes 196616 | tf_op jit(solution)/shard_map/ppermute | solution.py:55
  63.2 1.5 %collective-permute-start.8 = (f32[128,128]{1,0:T(8,128)S(1)}, f32[128,128]{1,0:T(8,128)S(1)}, u32[]{:S(2)}, u32[]{:S(2)}) collective-permute-start(f32[128,128]{1,0:T(8,128)S(1)} %add.30), channel_id=1, source_target_pairs={{0,16},{1,17},{2,18},{3,19},{4,20},{5,21},{6,22},{7,23},{8,24},{9,... | collective-permute-start | bytes 196616 | tf_op jit(solution)/shard_map/ppermute | solution.py:55

commit v4 on v3

--- a/solution.py
+++ b/solution.py
@@ -67,9 +67,10 @@
     return part + permute(part, lambda x, y, c, s: (x ^ 1, y, c, s))
 
 
-def over_rest(part):
+def over_rest(part, *work):
     part = part + permute(part, lambda x, y, c, s: (x ^ 2, y, c, s))
-    return part + permute(part, lambda x, y, c, s: (x, y, c ^ 1, s))
+    part, *work = lax.optimization_barrier((part, *work))
+    return part + permute(part, lambda x, y, c, s: (x, y, c ^ 1, s)), work
 
 
 def hold(token, *values):
@@ -83,6 +84,7 @@
         out_specs=[place] * len(values),
         out_shape=[shape(*v.shape) for v in values],
         input_output_aliases={k + 1: k for k in range(len(values))},
+        compiler_params=params(53),
         cost_estimate=cost(HOLD_COST),
         name="hold",
     )(token, *values)
@@ -233,7 +235,10 @@
 
 
 PARTS = 3
-FIRST_COST, SECOND_COST, HOLD_COST = 6, 2, 3
+HALO = 2 * NSLOT
+PIECES = (((0, 288), (288, 288), (576, 288)), ((0, 192), (192, 192), (384, 480)))
+FIRST_COST, SECOND_COST, HOLD_COST = 4, 2, 3
+DRIFT_COST = 2
 
 
 def column_rows(ref, col):
@@ -242,7 +247,7 @@
 
 def unpack_kernel(
     dir_ref, in_ref, order_ref, near_any, m_ref, left_any, phi_any,
-    left_ref, phi_ref, whole, high_ref, low_ref, table, padded, sems, out_sems,
+    left_ref, phi_ref, flux, whole, high_ref, low_ref, table, padded, sems, out_sems,
 ):
     forward = dir_ref[0]
     size = NSLOT // PARTS
@@ -267,9 +272,20 @@
             return carry
 
         lax.fori_loop(0, size // step, body, 0)
-    near = column_rows(whole, column_of(forward, 3))
-    outs = fetch(out_sems, (near, near_any), (left_ref, left_any), (phi_ref, phi_any))
+    col = column_of(forward, 3)
+    near = column_rows(whole, col)
+    outs = fetch(out_sems, (near, near_any.at[pl.ds(0, HALO)]), (left_ref, left_any), (phi_ref, phi_any))
     put_moments(forward, left_ref, high_ref, low_ref, m_ref)
+    cx = coefs_of(phi_ref[...], 1)
+    for half in range(2):
+        share = cx * whole[pl.ds(half * 4 + col, NSLOT, stride=8), :]
+        split_into(share, pl.ds(0, NSLOT), pl.ds(half * 128, 128), high_ref, low_ref)
+    cols = pl.ds(0, COL)
+    for half, parts in enumerate(sums_of(left_ref[...], high_ref[:, cols], low_ref[:, cols])):
+        for k, part in enumerate(parts):
+            flux[pl.ds((half * 2 + k) * 8, 8), :] = part
+    outs += [pltpu.make_async_copy(flux, near_any.at[pl.ds(HALO, 32)], out_sems.at[3])]
+    outs[-1].start()
     settle(outs)
 
 
@@ -279,18 +295,19 @@
         in_specs=[smem(), anywhere(), spec()],
         out_specs=[anywhere(), spec(), anywhere(), anywhere()],
         out_shape=[
-            shape(NSLOT * 2, 128), shape(128, 128), shape(48, NPAD, dtype=BF16), shape(NSLOT, 128, dtype=BF16)
+            shape(HALO + 32, 128), shape(128, 128), shape(48, NPAD, dtype=BF16), shape(NSLOT, 128, dtype=BF16)
         ],
         scratch_shapes=[
             pltpu.VMEM((48, NPAD), BF16),
             pltpu.VMEM((NSLOT, 128), BF16),
+            pltpu.VMEM((32, 128), F32),
             pltpu.VMEM((NSLOT * 8, 128), F32),
             pltpu.VMEM((NPAD, CELLS), BF16),
             pltpu.VMEM((NPAD, CELLS), BF16),
             pltpu.VMEM((128, NPAD), F32),
             pltpu.VMEM((1, NPAD), jnp.int32),
             pltpu.SemaphoreType.DMA((PARTS,)),
-            pltpu.SemaphoreType.DMA((3,)),
+            pltpu.SemaphoreType.DMA((4,)),
         ],
         compiler_params=params(),
         name="unpack",
@@ -365,8 +382,7 @@
             walls.append(n * WALL_T[side][level] ** -1.5)
     for r, c in enumerate(expo + poly + walls + [zero] * 10):
         table[pl.ds(r * 8, 8), :] = c
-    keep = 1.0 - rate
-    table[pl.ds(384, 8), :] = keep
+    table[pl.ds(384, 8), :] = rate
     n = 4
     right_ref[...] = jnp.zeros(right_ref.shape, BF16)
 
@@ -428,21 +444,16 @@
         prod[:, cols] = jnp.dot(phi, right_ref[:, cols], preferred_element_type=F32)
 
 
-def updated(n, i, rows, coefs, h, upwind, keep, prod):
+def drift_of(coefs, h, upwind):
     cx, cyp, cym, czp, czm, spill = coefs
     lane = lax.broadcasted_iota(jnp.int32, (1, 128), 1)
     plus = [pltpu.roll(a, 8, 1) for a in h]
     minus = [pltpu.roll(a, 120, 1) for a in h]
     out = []
     for hf in range(2):
-        at = i * COL + hf * 128
         before = jnp.where(lane < 8, plus[1 - hf], plus[hf])
         after = jnp.where(lane >= 120, minus[1 - hf], minus[hf])
-        expo = prod[rows, pl.ds(at, 128)]
-        poly = prod[rows, pl.ds(n * COL + at, 128)]
-        ghost = prod[rows, pl.ds(2 * n * COL + at, 128)]
-        new = jnp.exp2(expo) * poly + ghost
-        new = new + h[hf] * (keep[2 * i + hf] - spill)
+        new = h[hf] - spill * h[hf]
         new = new + (cyp * before + cym * after)
         new = new + (czp * pltpu.roll(h[hf], 1, 1) + czm * pltpu.roll(h[hf], 127, 1))
         if upwind is not None:
@@ -455,38 +466,132 @@
     return [coef_ref[rows, pl.ds(c * 128, 128)] for c in range(6)]
 
 
-def sweep(column, coef_ref, keep_ref, prod, put, start=0, stop=NSLOT):
+def drift_kernel(dir_ref, phi_any, *refs, start, size, first_step):
+    steps = size // 3
+    if first_step:
+        state_any, out_any, phi, state, out, coef, sems, out_sems = refs
+        spans = [(pl.ds((start + q * steps) * 8, steps * 8), pl.ds(q * steps * 8, steps * 8)) for q in range(3)]
+        pairs = [[(state_any.at[a], state.at[b])] for a, b in spans]
+    else:
+        state_any, halo_any, out_any, phi, state, halo, out, coef, sems, out_sems = refs
+        spans = [(pl.ds(start + q * steps, steps), pl.ds(q * steps, steps)) for q in range(3)]
+        pairs = [[(state_any.at[a], state.at[b])] for a, b in spans]
+        pairs[0].append((halo_any.at[pl.ds(start * 2, size * 2)], halo))
+    flat_pairs = [(phi_any.at[pl.ds(start, size)], phi)] + [pair for group in pairs for pair in group]
+    copies = fetch(sems, *flat_pairs)
+    forward = dir_ref[0]
+    copies[0].wait()
+    coef[...] = coefs_of(phi[...], 6)
+    step = 32
+    at = 1
+    outs = []
+    for q in range(3):
+        settle(copies[at : at + len(pairs[q])])
+        at += len(pairs[q])
+
+        def body(k, carry):
+            first = pl.multiple_of(q * steps + k * step, step)
+            rows = pl.ds(first, step)
+            coefs = read_coefs(coef, rows)
+            upwind = None
+            for i in range(4):
+                if first_step:
+                    col = column_of(forward, i)
+                    h = [state[pl.ds(first * 8 + hf * 4 + col, step, stride=8), :] for hf in range(2)]
+                else:
+                    h = [state[rows, pl.ds(i * COL + hf * 128, 128)] for hf in range(2)]
+                    if i == 0:
+                        h = [a + coefs[0] * halo[pl.ds(first * 2 + hf, step, stride=2), :] for hf, a in enumerate(h)]
+                for hf, new in enumerate(drift_of(coefs, h, upwind)):
+                    out[rows, pl.ds(i * COL + hf * 128, 128)] = new
+                upwind = h
+            return carry
+
+        lax.fori_loop(0, steps // step, body, 0)
+        rows = pl.ds(q * steps, steps)
+        outs.append(pltpu.make_async_copy(out.at[rows], out_any.at[rows], out_sems.at[q]))
+        outs[-1].start()
+    settle(outs)
+
+
+def drift(forward, phi, piece, *states):
+    first_step = len(states) == 1
+    start, size = piece
+
+    def kernel(*refs):
+        drift_kernel(*refs, start=start, size=size, first_step=first_step)
+
+    if first_step:
+        held = [pltpu.VMEM((size * 8, 128), F32)]
+    else:
+        held = [pltpu.VMEM((size, CELLS), F32), pltpu.VMEM((size * 2, 128), F32)]
+    return pl.pallas_call(
+        kernel,
+        in_specs=[smem()] + [anywhere()] * (1 + len(states)),
+        out_specs=anywhere(),
+        out_shape=shape(size, CELLS),
+        scratch_shapes=[pltpu.VMEM((size, 128), BF16)]
+        + held
+        + [
+            pltpu.VMEM((size, CELLS), F32),
+            pltpu.VMEM((size, 768), F32),
+            pltpu.SemaphoreType.DMA((5,)),
+            pltpu.SemaphoreType.DMA((3,)),
+        ],
+        compiler_params=params(),
+        cost_estimate=cost(DRIFT_COST),
+        name="drift",
+    )(forward, phi, *states)
+
+
+def sweep(column, drifted, rate_ref, prod, put, start, stop):
     step = 32
 
     def body(k, carry):
         first = pl.multiple_of(k * step, step)
         rows = pl.ds(first, step)
-        coefs = read_coefs(coef_ref, rows)
-        keep = [keep_ref[pl.ds(b, 1), :] for b in range(8)]
-        upwind = None
         for i in range(4):
-            h = [column(i, hf, first, step) for hf in range(2)]
-            new = updated(4, i, rows, coefs, h, upwind, keep, prod)
             for hf in range(2):
-                put(i, hf, first, step, new[hf])
-            upwind = h
+                at = i * COL + hf * 128
+                expo = prod[rows, pl.ds(at, 128)]
+                poly = prod[rows, pl.ds(CELLS + at, 128)]
+                ghost = prod[rows, pl.ds(2 * CELLS + at, 128)]
+                new = jnp.exp2(expo) * poly + ghost
+                new = new + drifted[rows, pl.ds(at, 128)]
+                new = new - rate_ref[pl.ds(2 * i + hf, 1), :] * column(i, hf, first, step)
+                put(i, hf, first, step, new)
         return carry
 
     lax.fori_loop(start // step, stop // step, body, 0)
 
 
+def fetch_parts(sems, pieces, drifted_any, drifted, state_any, state, scale):
+    size = NSLOT // PARTS
+    pairs, counts = [], []
+    left = list(zip(pieces, drifted_any, strict=True))
+    for p in range(PARTS):
+        rows = pl.ds(p * size * scale, size * scale)
+        group = [(state_any.at[rows], state.at[rows])]
+        while left and left[0][0][0] < (p + 1) * size:
+            (start, count), ref = left.pop(0)
+            group.append((ref, drifted.at[pl.ds(start, count)]))
+        pairs += group
+        counts.append(len(group))
+    copies = fetch(sems, *pairs)
+    return [copies[sum(counts[:p]) : sum(counts[: p + 1])] for p in range(PARTS)]
+
+
 def first_kernel(
-    dir_ref, in_ref, m0_ref, tag_ref, phi_ref, left_ref, h1_any, edge_any, m_ref,
-    right, keep, table, prod, whole, phi, coef, left, h1, edge, high_ref, low_ref, sems, out_sems,
+    dir_ref, in_ref, d0_any, d1_any, d2_any, m0_ref, tag_ref, phi_ref, left_ref, h1_any, edge_any, m_ref,
+    right, keep, table, prod, whole, drifted, phi, left, h1, edge, high_ref, low_ref, sems, part_sems, out_sems,
 ):
     forward = dir_ref[0]
-    copies = fetch(sems, (phi_ref, phi), (in_ref, whole), (left_ref, left))
+    copies = fetch(sems, (phi_ref, phi), (left_ref, left))
+    parts = fetch_parts(part_sems, PIECES[0], (d0_any, d1_any, d2_any), drifted, in_ref, whole, 8)
     clear_tail(high_ref, low_ref)
     put_fields(forward, m0_ref, tag_ref, right, keep, table)
-    copies[0].wait()
+    settle(copies)
     products(4, phi, right, prod)
-    coef[...] = coefs_of(phi[...], 6)
-    settle(copies[1:])
 
     def column(i, hf, first, step):
         return whole[pl.ds(first * 8 + hf * 4 + column_of(forward, i), step, stride=8), :]
@@ -502,7 +607,8 @@
     size = NSLOT // PARTS
     outs = []
     for p in range(PARTS):
-        sweep(column, coef, keep, prod, put, p * size, p * size + size)
+        settle(parts[p])
+        sweep(column, drifted, keep, prod, put, p * size, p * size + size)
         rows = pl.ds(p * size, size)
         outs.append(pltpu.make_async_copy(h1.at[rows], h1_any.at[rows], out_sems.at[p]))
         outs[-1].start()
@@ -512,86 +618,75 @@
     settle(outs)
 
 
-def first_step(forward, flat, m, tags, phi, left):
+def first_step(forward, flat, drifted, m, tags, phi, left):
     return pl.pallas_call(
         first_kernel,
-        in_specs=[smem(), anywhere(), spec(), spec(), anywhere(), anywhere()],
+        in_specs=[smem()] + [anywhere()] * 4 + [spec(), spec(), anywhere(), anywhere()],
         out_specs=[anywhere(), anywhere(), spec()],
         out_shape=[shape(NSLOT, CELLS), shape(NSLOT * 2, 128), shape(128, 128)],
         scratch_shapes=field_scratch()
         + [
             pltpu.VMEM((NSLOT, 3 * CELLS), F32),
             pltpu.VMEM((NSLOT * 8, 128), F32),
+            pltpu.VMEM((NSLOT, CELLS), F32),
             pltpu.VMEM((NSLOT, 128), BF16),
-            pltpu.VMEM((NSLOT, 768), F32),
             pltpu.VMEM((48, NPAD), BF16),
             pltpu.VMEM((NSLOT, CELLS), F32),
             pltpu.VMEM((NSLOT * 2, 128), F32),
             pltpu.VMEM((NPAD, CELLS), BF16),
             pltpu.VMEM((NPAD, CELLS), BF16),
-            pltpu.SemaphoreType.DMA((3,)),
+            pltpu.SemaphoreType.DMA((2,)),
+            pltpu.SemaphoreType.DMA((2 * PARTS,)),
             pltpu.SemaphoreType.DMA((PARTS + 1,)),
         ],
         compiler_params=params(),
         cost_estimate=cost(FIRST_COST),
         name="first_step",
-    )(forward, flat, m, tags, phi, left)
-
-
-def inflow_kernel(dir_ref, halo_any, phi_any, left_any, m_ref, out_ref, halo, phi, left, high_ref, low_ref, sems):
-    copies = fetch(sems, (phi_any, phi), (halo_any, halo), (left_any, left))
-    clear_tail(high_ref, low_ref)
+    )(forward, flat, *drifted, m, tags, phi, left)
+
+
+def inflow_kernel(dir_ref, halo_any, m_ref, out_ref, flux, sems):
+    copies = fetch(sems, (halo_any.at[pl.ds(HALO, 32)], flux))
     out_ref[...] = m_ref[...]
-    copies[0].wait()
-    cx = coefs_of(phi[...], 1)
-    settle(copies[1:])
+    row = column_of(dir_ref[0], 0) * 2
+    settle(copies)
     for half in range(2):
-        share = cx * halo[pl.ds(half, NSLOT, stride=2), :]
-        split_into(share, pl.ds(0, NSLOT), pl.ds(half * 128, 128), high_ref, low_ref)
-    row = column_of(dir_ref[0], 0) * 2
-    for half, parts in enumerate(sums_of(left[...], high_ref[...], low_ref[...])):
-        for k, part in enumerate(parts):
+        for k in range(2):
             at = pl.ds(64 * k + row + half, 8, stride=8)
-            out_ref[at, :] = m_ref[at, :] + part
-
-
-def inflow(forward, halo, phi, left, m):
+            out_ref[at, :] = m_ref[at, :] + flux[pl.ds((half * 2 + k) * 8, 8), :]
+
+
+def inflow(forward, halo, m):
     return pl.pallas_call(
         inflow_kernel,
-        in_specs=[smem()] + [anywhere()] * 3 + [spec()],
+        in_specs=[smem(), anywhere(), spec()],
         out_specs=spec(),
         out_shape=shape(128, 128),
-        scratch_shapes=[
-            pltpu.VMEM((NSLOT * 2, 128), F32),
-            pltpu.VMEM((NSLOT, 128), BF16),
-            pltpu.VMEM((48, NPAD), BF16),
-            pltpu.VMEM((NPAD, COL), BF16),
-            pltpu.VMEM((NPAD, COL), BF16),
-            pltpu.SemaphoreType.DMA((3,)),
-        ],
-        compiler_params=params(),
+        scratch_shapes=[pltpu.VMEM((32, 128), F32), pltpu.SemaphoreType.DMA((1,))],
+        compiler_params=params(53),
         name="inflow",
-    )(forward, halo, phi, left, m)
+    )(forward, halo, m)
 
 
 def second_kernel(
-    dir_ref, h_any, halo_any, m0_ref, tag_ref, phi_any, out_any, pre_any, heat_ref,
-    right, keep, table, prod, h, halo, phi, coef, out_ref, pre_ref, sems, out_sems,
+    dir_ref, h_any, halo_any, d0_any, d1_any, d2_any, m0_ref, tag_ref, phi_any, out_any, pre_any, heat_ref,
+    right, keep, table, prod, h, halo, drifted, phi, cx, out_ref, pre_ref, sems, part_sems, out_sems,
 ):
     forward = dir_ref[0]
-    copies = fetch(sems, (phi_any, phi), (h_any, h), (halo_any, halo))
+    copies = fetch(sems, (phi_any, phi), (halo_any.at[pl.ds(0, HALO)], halo))
+    parts = fetch_parts(part_sems, PIECES[1], (d0_any, d1_any, d2_any), drifted, h_any, h, 1)
     heat = put_fields(forward, m0_ref, tag_ref, right, keep, table)
     put_heat(heat, table, heat_ref)
     copies[0].wait()
     products(4, phi, right, prod)
-    coef[...] = coefs_of(phi[...], 6)
-    settle(copies[1:])
+    cx[...] = coefs_of(phi[...], 1)
+    copies[1].wait()
 
     def column(i, hf, first, step):
         rows = pl.ds(first, step)
         state = h[rows, pl.ds(i * COL + hf * 128, 128)]
         if i == 0:
-            state = state + coef[rows, pl.ds(0, 128)] * halo[pl.ds(first * 2 + hf, step, stride=2), :]
+            state = state + cx[rows, :] * halo[pl.ds(first * 2 + hf, step, stride=2), :]
         return state
 
     def put(i, hf, first, step, new):
@@ -602,7 +697,8 @@
     size = NSLOT // PARTS
     outs = []
     for p in range(PARTS):
-        sweep(column, coef, keep, prod, put, p * size, p * size + size)
+        settle(parts[p])
+        sweep(column, drifted, keep, prod, put, p * size, p * size + size)
         rows = pl.ds(p * size * 8, size * 8)
         outs.append(pltpu.make_async_copy(out_ref.at[rows], out_any.at[rows], out_sems.at[p]))
         outs[-1].start()
@@ -611,10 +707,10 @@
     settle(outs)
 
 
-def second_step(forward, h, halo, m, tags, phi):
+def second_step(forward, h, halo, drifted, m, tags, phi):
     return pl.pallas_call(
         second_kernel,
-        in_specs=[smem(), anywhere(), anywhere(), spec(), spec(), anywhere()],
+        in_specs=[smem()] + [anywhere()] * 5 + [spec(), spec(), anywhere()],
         out_specs=[anywhere(), anywhere(), spec()],
         out_shape=[shape(NSLOT * 8, 128), shape(NSLOT * 2, 128), shape(4, 2, 32)],
         scratch_shapes=field_scratch()
@@ -622,29 +718,42 @@
             pltpu.VMEM((NSLOT, 3 * CELLS), F32),
             pltpu.VMEM((NSLOT, CELLS), F32),
             pltpu.VMEM((NSLOT * 2, 128), F32),
+            pltpu.VMEM((NSLOT, CELLS), F32),
             pltpu.VMEM((NSLOT, 128), BF16),
-            pltpu.VMEM((NSLOT, 768), F32),
+            pltpu.VMEM((NSLOT, 128), F32),
             pltpu.VMEM((NSLOT * 8, 128), F32),
             pltpu.VMEM((NSLOT * 2, 128), F32),
-            pltpu.SemaphoreType.DMA((3,)),
+            pltpu.SemaphoreType.DMA((2,)),
+            pltpu.SemaphoreType.DMA((2 * PARTS,)),
             pltpu.SemaphoreType.DMA((PARTS + 1,)),
         ],
         compiler_params=params(),
         cost_estimate=cost(SECOND_COST),
         name="second_step",
-    )(forward, h, halo, m, tags, phi)
+    )(forward, h, halo, *drifted, m, tags, phi)
 
 
 def last_kernel(dir_ref, h_any, pre_any, halo_any, phi_any, out_any, pre, halo, phi, sems, out_sems):
     del h_any
-    copies = fetch(sems, (phi_any, phi), (pre_any, pre), (halo_any, halo))
+    size = HALO // PARTS
+    spans = [pl.ds(p * size, size) for p in range(PARTS)]
+    pairs = [(phi_any, phi)]
+    for rows in spans:
+        pairs += [(pre_any.at[rows], pre.at[rows]), (halo_any.at[rows], halo.at[rows])]
+    copies = fetch(sems, *pairs)
     copies[0].wait()
     cx = coefs_of(phi[...], 1)
-    settle(copies[1:])
-    for half in range(2):
-        at = pl.ds(half, NSLOT, stride=2)
-        pre[at, :] = pre[at, :] + cx * halo[at, :]
-    settle(fetch(out_sems, (pre, column_rows(out_any, column_of(dir_ref[0], 0)))))
+    column = column_rows(out_any, column_of(dir_ref[0], 0))
+    outs = []
+    for p, rows in enumerate(spans):
+        settle(copies[1 + 2 * p : 3 + 2 * p])
+        part = cx[p * (size // 2) : (p + 1) * (size // 2)]
+        for half in range(2):
+            at = pl.ds(p * size + half, size // 2, stride=2)
+            pre[at, :] = pre[at, :] + part * halo[at, :]
+        outs.append(pltpu.make_async_copy(pre.at[rows], column.at[rows], out_sems.at[p]))
+        outs[-1].start()
+    settle(outs)
 
 
 def last(forward, h, pre, halo, phi):
@@ -658,8 +767,8 @@
             pltpu.VMEM((NSLOT * 2, 128), F32),
             pltpu.VMEM((NSLOT * 2, 128), F32),
             pltpu.VMEM((NSLOT, 128), BF16),
-            pltpu.SemaphoreType.DMA((3,)),
-            pltpu.SemaphoreType.DMA((1,)),
+            pltpu.SemaphoreType.DMA((1 + 2 * PARTS,)),
+            pltpu.SemaphoreType.DMA((PARTS,)),
         ],
         compiler_params=params(),
         name="last",
@@ -671,17 +780,20 @@
     at = lax.axis_index("space").astype(jnp.int32).reshape(1)
     flat = state.reshape(NSLOT, 4, 2, 128).transpose(0, 2, 1, 3).reshape(NSLOT * 8, 128)
     near, m, left, phi = unpack(forward, flat, velocity_order)
-    m = over_y(m)
+    drifted = [drift(forward, phi, piece, flat) for piece in PIECES[0]]
+    m, drifted[0] = lax.optimization_barrier((over_y(m), drifted[0]))
     (near,) = hold(m, near)
     near = downstream(near)
     tags = strip_tags(at, jnp.transpose(wall_tag, (1, 2, 0)).reshape(64, 64))
-    m = over_rest(over_x(m))
-    h1, edge, m = first_step(forward, flat, m, tags, phi, left)
-    m = over_x(over_y(inflow(forward, near, phi, left, m)))
+    m, drifted = over_rest(over_x(m), *drifted)
+    h1, edge, m = first_step(forward, flat, drifted, m, tags, phi, left)
+    drifted = [drift(forward, phi, piece, h1, near) for piece in PIECES[1]]
+    m, drifted[0] = lax.optimization_barrier((over_y(inflow(forward, near, m)), drifted[0]))
+    m, drifted[1] = lax.optimization_barrier((over_x(m), drifted[1]))
     (edge,) = hold(m, edge)
     edge = downstream(edge)
-    m = over_rest(m)
-    out, pre, wall_heat = second_step(forward, h1, near, m, tags, phi)
+    m, drifted = over_rest(m, *drifted)
+    out, pre, wall_heat = second_step(forward, h1, near, drifted, m, tags, phi)
     out = last(forward, out, pre, edge, phi)
     state_next = out.reshape(NSLOT, 2, 4, 128).transpose(0, 2, 1, 3).reshape(NSLOT, 4, 256)
     return state_next, wall_heat

time: 85.5 us -> 80.2 us (0.938)
  waiting for transfers between devices: 22.5 us -> 6.92 us
  Pallas kernels: 37.3 us -> 50.2 us
  other arithmetic: 4.27 us -> 1.33 us
    ppermute x10, waiting for transfers between devices: 22.5 us -> 6.92 us  [permute(): lax.ppermute(value, AXES, [(i, index_of(*move(*device_of(i)))) for i in r...]
    pallas_call x3 -> x9, Pallas kernels: 26.5 us -> 40.7 us  [the longest x6 23.3 us: drift(): pl.pallas_call(kernel, in_specs=[smem()] + [anywhere()] * (1 + len(states...]
    add x2, other arithmetic: 2.33 us -> 0.02 us  [over_y(): return part + permute(part, lambda x, y, c, s: (x, y ^ 1, c, s))]
    pallas_call x2, Pallas kernels: 1.82 us -> 0.01 us  [hold(): pl.pallas_call(kernel, in_specs=[spec()] + [place] * len(values), out_spe...]
  transfers between devices with their start and end apart: 10 -> 10, of which waited for: 8 -> 3; matrix products, arithmetic and copies ran while one was open for 2% -> 2% of each run, Pallas kernels for 30% -> 52%
where the time goes in v4:
time: 80.2 us; the launch traced here: 79.7 us
  Pallas kernels  50.2 us (63%)
  starting transfers between devices  19.4 us (24%)
  waiting for transfers between devices  6.92 us (9%)
  other arithmetic  1.33 us (2%)
  between operations  1.02 us (1%)
  local copies, waits for them, and re-layouts  0.84 us (1%)
    pallas_call x6, Pallas kernels, drift(): pl.pallas_call(kernel, in_specs=[smem()] + [anywhere()] * (1 + len(states...  23.3 us
    ppermute x10, starting transfers between devices, permute(): lax.ppermute(value, AXES, [(i, index_of(*move(*device_of(i)))) for i in r...  19.4 us
    pallas_call x1, Pallas kernels, first_step(): pl.pallas_call(first_kernel, in_specs=[smem()] + [anywhere()] * 4 + [spec...  9.08 us
    pallas_call x1, Pallas kernels, second_step(): pl.pallas_call(second_kernel, in_specs=[smem()] + [anywhere()] * 5 + [spe...  7.6 us
    ppermute x10, waiting for transfers between devices, permute(): lax.ppermute(value, AXES, [(i, index_of(*move(*device_of(i)))) for i in r...  6.92 us
    pallas_call x1, Pallas kernels, unpack(): pl.pallas_call(unpack_kernel, in_specs=[smem(), anywhere(), spec()], out_...  5.51 us
    pallas_call x1, Pallas kernels, last(): pl.pallas_call(last_kernel, in_specs=[smem()] + [anywhere()] * 4, out_spe...  2.38 us
  transfers between devices with their start and end apart: 10, of which 3 were waited for; matrix products, arithmetic and copies ran while one was open for 2% of the time, Pallas kernels for 52%

profile of v4, /device:TPU:4, one launch (start us, length us, event | category | flops | bytes accessed | tf_op | source)
XLA Modules:
  0.0 79.7 jit_solution(2927449563446444812)
XLA Ops:
  0.6 5.5 %unpack.1 = (f32[1760,128]{1,0:T(8,128)}, f32[128,128]{1,0:T(8,128)}, bf16[48,896]{1,0:T(8,128)(2,1)}, bf16[864,128]{1,0:T(8,128)(2,1)}) custom-call(s32[1]{0:T(128)} %bitcast.dir_ref.refs_0_, f32[6912,128]{1,0:T(8,128)} %bitcast.15, s32[864]{0:T(1024)} %order_ref.1), custom_call_target="tpu_custom_call" | custom-call | tf_op jit(solution)/shard_map/unpack/pallas_call | solution.py:293
  6.2 1.7 %collective-permute-start = (f32[128,128]{1,0:T(8,128)}, f32[128,128]{1,0:T(8,128)S(1)}, u32[]{:S(2)}, u32[]{:S(2)}) collective-permute-start(f32[128,128]{1,0:T(8,128)} %get-tuple-element.26), channel_id=1, source_target_pairs={{0,32},{1,33},{2,34},{3,35},{4,36},{5,37},{6,38},{7,39},{8,40},{9,... | collective-permute-start | bytes 196616 | tf_op jit(solution)/shard_map/ppermute | solution.py:55
  7.8 3.9 %drift.6.d0_any = f32[288,1024]{1,0:T(8,128)} custom-call(s32[1]{0:T(128)} %bitcast.dir_ref.refs_0_, bf16[864,128]{1,0:T(8,128)(2,1)} %get-tuple-element.27.refs_1_.phi_ref.phi_any, f32[6912,128]{1,0:T(8,128)} %bitcast.16), custom_call_target="tpu_custom_call" | custom-call | flops 2300000000 | bytes 10000 | tf_op jit(solution)/shard_map/drift/pallas_call | solution.py:528
  11.8 1.3 %collective-permute-start.1 = (f32[128,128]{1,0:T(8,128)S(1)}, f32[128,128]{1,0:T(8,128)S(1)}, u32[]{:S(2)}, u32[]{:S(2)}) collective-permute-start(f32[128,128]{1,0:T(8,128)S(1)} %add.24.refs_0_), channel_id=1, source_target_pairs={{0,64},{1,65},{2,66},{3,67},{4,68},{5,69},{6,70},{7,71},{8,72},{9,... | collective-permute-start | bytes 196616 | tf_op jit(solution)/shard_map/ppermute | solution.py:55
  13.1 2.9 %collective-permute-start.4 = (f32[1760,128]{1,0:T(8,128)}, f32[1760,128]{1,0:T(8,128)}, u32[]{:S(2)}, u32[]{:S(2)}) collective-permute-start(f32[1760,128]{1,0:T(8,128)} %hold.2), channel_id=1, source_target_pairs={{0,15},{1,0},{2,1},{3,2},{4,3},{5,4},{6,5},{7,6},{8,7},{9,8},{10,9... | collective-permute-start | bytes 2703368 | tf_op jit(solution)/shard_map/ppermute | solution.py:55
  16.0 3.9 %drift.8.d2_any = f32[288,1024]{1,0:T(8,128)} custom-call(s32[1]{0:T(128)} %bitcast.dir_ref.refs_0_, bf16[864,128]{1,0:T(8,128)(2,1)} %get-tuple-element.27.refs_1_.phi_ref.phi_any, f32[6912,128]{1,0:T(8,128)} %bitcast.17), custom_call_target="tpu_custom_call" | custom-call | flops 2300000000 | bytes 10000 | tf_op jit(solution)/shard_map/drift/pallas_call | solution.py:528
  19.9 0.0 collective-permute-done.1
  19.9 6.2 %collective-permute-start.2 = (f32[128,128]{1,0:T(8,128)S(1)}, f32[128,128]{1,0:T(8,128)S(1)}, u32[]{:S(2)}, u32[]{:S(2)}) collective-permute-start(f32[128,128]{1,0:T(8,128)S(1)} %add.25), channel_id=1, source_target_pairs={{0,128},{1,129},{2,130},{3,131},{4,132},{5,133},{6,134},{7,135},{8... | collective-permute-start | bytes 196616 | tf_op jit(solution)/shard_map/ppermute | solution.py:55
  26.1 3.9 %drift.7.d1_any = f32[288,1024]{1,0:T(8,128)} custom-call(s32[1]{0:T(128)} %bitcast.dir_ref.refs_0_, bf16[864,128]{1,0:T(8,128)(2,1)} %get-tuple-element.27.refs_1_.phi_ref.phi_any, f32[6912,128]{1,0:T(8,128)} %bitcast.18), custom_call_target="tpu_custom_call" | custom-call | flops 2300000000 | bytes 10000 | tf_op jit(solution)/shard_map/drift/pallas_call | solution.py:528
  30.0 0.1 collective-permute-start.3
  30.1 1.6 %strip_tags.1.tag_ref = s32[8,128]{1,0:T(8,128)} custom-call(s32[1]{0:T(128)} %bitcast.6.at_ref, s32[64,64]{1,0:T(8,128)} %bitcast.21), custom_call_target="tpu_custom_call" | custom-call | tf_op jit(solution)/shard_map/strip_tags/pallas_call | solution.py:333
  31.7 0.0 collective-permute-done.3
  31.7 0.6 add.27.m0_ref
  32.4 9.1 %first_step.1 = (f32[864,1024]{1,0:T(8,128)}, f32[1728,128]{1,0:T(8,128)}, f32[128,128]{1,0:T(8,128)}) custom-call(s32[1]{0:T(128)} %bitcast.dir_ref.refs_0_, f32[6912,128]{1,0:T(8,128)} %bitcast.19, f32[288,1024]{1,0:T(8,128)} %drift.6.d0_any, f32[288,1024]{1,0:T(8,128)} %drift.7.d1_any, f32[288,1024]{1,0:T(8,128)} %drift.8.d2_any, f32[128,128]{1,0:T(8,128)} %add.27.m0_ref, ...), custom_call_target="tpu_custom_call" | custom-call | flops 4600000000 | bytes 10000 | tf_op jit(solution)/shard_map/first_step/pallas_call | solution.py:622
  41.4 0.0 collective-permute-done.4.halo_any.refs_3_
  41.5 0.8 %copy-done = f32[128,128]{1,0:T(8,128)S(1)} copy-done((f32[128,128]{1,0:T(8,128)S(1)}, f32[128,128]{1,0:T(8,128)}, u32[]{:S(2)}) %copy-start) | copy-done | bytes 65560
  42.3 0.7 inflow.1
  43.0 0.2 collective-permute-start.5
  43.3 3.1 %drift.9.d0_any = f32[192,1024]{1,0:T(8,128)} custom-call(s32[1]{0:T(128)} %bitcast.dir_ref.refs_0_, bf16[864,128]{1,0:T(8,128)(2,1)} %get-tuple-element.27.refs_1_.phi_ref.phi_any, f32[864,1024]{1,0:T(8,128)} %get-tuple-element.35.refs_2_.h_any, f32[1760,128]{1,0:T(8,128)} %collective-permute-done.4.halo_any.refs_3_), custom_call_target="tpu_custom_call" | custom-call | flops 2300000000 | bytes 10000 | tf_op jit(solution)/shard_map/drift/pallas_call | solution.py:528
  46.4 1.2 %collective-permute-done.5 = f32[128,128]{1,0:T(8,128)S(1)} collective-permute-done((f32[128,128]{1,0:T(8,128)S(1)}, f32[128,128]{1,0:T(8,128)S(1)}, u32[]{:S(2)}, u32[]{:S(2)}) %collective-permute-start.5) | collective-permute-done | bytes 65568 | tf_op jit(solution)/shard_map/ppermute | solution.py:55
  47.6 1.4 %collective-permute-start.6 = (f32[128,128]{1,0:T(8,128)S(1)}, f32[128,128]{1,0:T(8,128)S(1)}, u32[]{:S(2)}, u32[]{:S(2)}) collective-permute-start(f32[128,128]{1,0:T(8,128)S(1)} %add.28), channel_id=1, source_target_pairs={{0,64},{1,65},{2,66},{3,67},{4,68},{5,69},{6,70},{7,71},{8,72},{9,... | collective-permute-start | bytes 196616 | tf_op jit(solution)/shard_map/ppermute | solution.py:55
  49.0 3.1 %drift.10.d1_any = f32[192,1024]{1,0:T(8,128)} custom-call(s32[1]{0:T(128)} %bitcast.dir_ref.refs_0_, bf16[864,128]{1,0:T(8,128)(2,1)} %get-tuple-element.27.refs_1_.phi_ref.phi_any, f32[864,1024]{1,0:T(8,128)} %get-tuple-element.35.refs_2_.h_any, f32[1760,128]{1,0:T(8,128)} %collective-permute-done.4.halo_any.refs_3_), custom_call_target="tpu_custom_call" | custom-call | flops 2300000000 | bytes 10000 | tf_op jit(solution)/shard_map/drift/pallas_call | solution.py:528
  52.1 0.0 collective-permute-done.6
  52.2 0.1 collective-permute-start.9
  52.3 5.5 %collective-permute-start.7 = (f32[128,128]{1,0:T(8,128)S(1)}, f32[128,128]{1,0:T(8,128)S(1)}, u32[]{:S(2)}, u32[]{:S(2)}) collective-permute-start(f32[128,128]{1,0:T(8,128)S(1)} %add.29.refs_0_), channel_id=1, source_target_pairs={{0,128},{1,129},{2,130},{3,131},{4,132},{5,133},{6,134},{7,135},{8... | collective-permute-start | bytes 196616 | tf_op jit(solution)/shard_map/ppermute | solution.py:55
  57.7 5.4 %drift.11.d2_any = f32[480,1024]{1,0:T(8,128)} custom-call(s32[1]{0:T(128)} %bitcast.dir_ref.refs_0_, bf16[864,128]{1,0:T(8,128)(2,1)} %get-tuple-element.27.refs_1_.phi_ref.phi_any, f32[864,1024]{1,0:T(8,128)} %get-tuple-element.35.refs_2_.h_any, f32[1760,128]{1,0:T(8,128)} %collective-permute-done.4.halo_any.refs_3_), custom_call_target="tpu_custom_call" | custom-call | flops 2300000000 | bytes 10000 | tf_op jit(solution)/shard_map/drift/pallas_call | solution.py:528
  63.2 0.1 collective-permute-start.8
  63.3 1.2 %collective-permute-done.8 = f32[128,128]{1,0:T(8,128)S(1)} collective-permute-done((f32[128,128]{1,0:T(8,128)S(1)}, f32[128,128]{1,0:T(8,128)S(1)}, u32[]{:S(2)}, u32[]{:S(2)}) %collective-permute-start.8) | collective-permute-done | bytes 65568 | tf_op jit(solution)/shard_map/ppermute | solution.py:55
  64.5 0.6 add.31.m0_ref
  65.2 7.6 %second_step.1 = (f32[6912,128]{1,0:T(8,128)}, f32[1728,128]{1,0:T(8,128)}, f32[4,2,32]{2,1,0:T(2,128)}) custom-call(s32[1]{0:T(128)} %bitcast.dir_ref.refs_0_, f32[864,1024]{1,0:T(8,128)} %get-tuple-element.35.refs_2_.h_any, f32[1760,128]{1,0:T(8,128)} %collective-permute-done.4.halo_any.refs_3_, f32[192,1024]{1,0:T(8,128)} %drift.9.d0_any, ...), custom_call_target="tpu_custom_call" | custom-call | flops 2300000000 | bytes 10000 | tf_op jit(solution)/shard_map/second_step/pallas_call | solution.py:711
  72.8 4.4 %collective-permute-done.9.halo_any = f32[1728,128]{1,0:T(8,128)} collective-permute-done((f32[1728,128]{1,0:T(8,128)}, f32[1728,128]{1,0:T(8,128)}, u32[]{:S(2)}, u32[]{:S(2)}) %collective-permute-start.9) | collective-permute-done | bytes 884768 | tf_op jit(solution)/shard_map/ppermute | solution.py:55
  77.2 2.4 %last.1 = f32[6912,128]{1,0:T(8,128)} custom-call(s32[1]{0:T(128)} %bitcast.dir_ref.refs_0_, f32[6912,128]{1,0:T(8,128)} %get-tuple-element.46.h_any, f32[1728,128]{1,0:T(8,128)} %get-tuple-element.47.pre_any, f32[1728,128]{1,0:T(8,128)} %collective-permute-done.9.halo_any, ...), custom_call_target="tpu_custom_call", output_to_operand_aliasing={{}: (1, {})} | custom-call | tf_op jit(solution)/shard_map/last/pallas_call | solution.py:760
  (14 shorter events, 0.1 us)
Async XLA Ops:
  6.2 5.6 %collective-permute-start = (f32[128,128]{1,0:T(8,128)}, f32[128,128]{1,0:T(8,128)S(1)}, u32[]{:S(2)}, u32[]{:S(2)}) collective-permute-start(f32[128,128]{1,0:T(8,128)} %get-tuple-element.26), channel_id=1, source_target_pairs={{0,32},{1,33},{2,34},{3,35},{4,36},{5,37},{6,38},{7,39},{8,40},{9,... | collective-permute-start | bytes 196616 | tf_op jit(solution)/shard_map/ppermute | solution.py:55
  7.8 3.9 %copy-start.1 = (f32[128,128]{1,0:T(8,128)S(1)}, f32[128,128]{1,0:T(8,128)}, u32[]{:S(2)}) copy-start(f32[128,128]{1,0:T(8,128)} %get-tuple-element.26) | copy-start | bytes 196612
  11.8 8.1 %collective-permute-start.1 = (f32[128,128]{1,0:T(8,128)S(1)}, f32[128,128]{1,0:T(8,128)S(1)}, u32[]{:S(2)}, u32[]{:S(2)}) collective-permute-start(f32[128,128]{1,0:T(8,128)S(1)} %add.24.refs_0_), channel_id=1, source_target_pairs={{0,64},{1,65},{2,66},{3,67},{4,68},{5,69},{6,70},{7,71},{8,72},{9,... | collective-permute-start | bytes 196616 | tf_op jit(solution)/shard_map/ppermute | solution.py:55
  13.1 28.4 %collective-permute-start.4 = (f32[1760,128]{1,0:T(8,128)}, f32[1760,128]{1,0:T(8,128)}, u32[]{:S(2)}, u32[]{:S(2)}) collective-permute-start(f32[1760,128]{1,0:T(8,128)} %hold.2), channel_id=1, source_target_pairs={{0,15},{1,0},{2,1},{3,2},{4,3},{5,4},{6,5},{7,6},{8,7},{9,8},{10,9... | collective-permute-start | bytes 2703368 | tf_op jit(solution)/shard_map/ppermute | solution.py:55
  19.9 10.1 %collective-permute-start.2 = (f32[128,128]{1,0:T(8,128)S(1)}, f32[128,128]{1,0:T(8,128)S(1)}, u32[]{:S(2)}, u32[]{:S(2)}) collective-permute-start(f32[128,128]{1,0:T(8,128)S(1)} %add.25), channel_id=1, source_target_pairs={{0,128},{1,129},{2,130},{3,131},{4,132},{5,133},{6,134},{7,135},{8... | collective-permute-start | bytes 196616 | tf_op jit(solution)/shard_map/ppermute | solution.py:55
  30.0 1.7 %collective-permute-start.3 = (f32[128,128]{1,0:T(8,128)S(1)}, f32[128,128]{1,0:T(8,128)S(1)}, u32[]{:S(2)}, u32[]{:S(2)}) collective-permute-start(f32[128,128]{1,0:T(8,128)S(1)} %add.26), channel_id=1, source_target_pairs={{0,16},{1,17},{2,18},{3,19},{4,20},{5,21},{6,22},{7,23},{8,24},{9,... | collective-permute-start | bytes 196616 | tf_op jit(solution)/shard_map/ppermute | solution.py:55
  41.5 0.8 %copy-start = (f32[128,128]{1,0:T(8,128)S(1)}, f32[128,128]{1,0:T(8,128)}, u32[]{:S(2)}) copy-start(f32[128,128]{1,0:T(8,128)} %get-tuple-element.37.m_ref) | copy-start | bytes 196612
  43.0 4.6 %collective-permute-start.5 = (f32[128,128]{1,0:T(8,128)S(1)}, f32[128,128]{1,0:T(8,128)S(1)}, u32[]{:S(2)}, u32[]{:S(2)}) collective-permute-start(f32[128,128]{1,0:T(8,128)S(1)} %inflow.1), channel_id=1, source_target_pairs={{0,32},{1,33},{2,34},{3,35},{4,36},{5,37},{6,38},{7,39},{8,40},{9,... | collective-permute-start | bytes 196616 | tf_op jit(solution)/shard_map/ppermute | solution.py:55
  47.6 4.5 %collective-permute-start.6 = (f32[128,128]{1,0:T(8,128)S(1)}, f32[128,128]{1,0:T(8,128)S(1)}, u32[]{:S(2)}, u32[]{:S(2)}) collective-permute-start(f32[128,128]{1,0:T(8,128)S(1)} %add.28), channel_id=1, source_target_pairs={{0,64},{1,65},{2,66},{3,67},{4,68},{5,69},{6,70},{7,71},{8,72},{9,... | collective-permute-start | bytes 196616 | tf_op jit(solution)/shard_map/ppermute | solution.py:55
  52.2 25.0 %collective-permute-start.9 = (f32[1728,128]{1,0:T(8,128)}, f32[1728,128]{1,0:T(8,128)}, u32[]{:S(2)}, u32[]{:S(2)}) collective-permute-start(f32[1728,128]{1,0:T(8,128)} %hold.3), channel_id=1, source_target_pairs={{0,15},{1,0},{2,1},{3,2},{4,3},{5,4},{6,5},{7,6},{8,7},{9,8},{10,9... | collective-permute-start | bytes 2654216 | tf_op jit(solution)/shard_map/ppermute | solution.py:55
  52.3 10.9 %collective-permute-start.7 = (f32[128,128]{1,0:T(8,128)S(1)}, f32[128,128]{1,0:T(8,128)S(1)}, u32[]{:S(2)}, u32[]{:S(2)}) collective-permute-start(f32[128,128]{1,0:T(8,128)S(1)} %add.29.refs_0_), channel_id=1, source_target_pairs={{0,128},{1,129},{2,130},{3,131},{4,132},{5,133},{6,134},{7,135},{8... | collective-permute-start | bytes 196616 | tf_op jit(solution)/shard_map/ppermute | solution.py:55
  63.2 1.3 %collective-permute-start.8 = (f32[128,128]{1,0:T(8,128)S(1)}, f32[128,128]{1,0:T(8,128)S(1)}, u32[]{:S(2)}, u32[]{:S(2)}) collective-permute-start(f32[128,128]{1,0:T(8,128)S(1)} %add.30), channel_id=1, source_target_pairs={{0,16},{1,17},{2,18},{3,19},{4,20},{5,21},{6,22},{7,23},{8,24},{9,... | collective-permute-start | bytes 196616 | tf_op jit(solution)/shard_map/ppermute | solution.py:55

commit v5 on v4

--- a/solution.py
+++ b/solution.py
@@ -236,9 +236,9 @@
 
 PARTS = 3
 HALO = 2 * NSLOT
-PIECES = (((0, 288), (288, 288), (576, 288)), ((0, 192), (192, 192), (384, 480)))
-FIRST_COST, SECOND_COST, HOLD_COST = 4, 2, 3
-DRIFT_COST = 2
+PIECES = (((0, 288), (288, 576)), ((0, 192), (192, 192), (384, 480)))
+FIRST_COST, SECOND_COST, HOLD_COST = 5, 2, 3
+DRIFT_COST = 3
 
 
 def column_rows(ref, col):
@@ -314,7 +314,7 @@
     )(forward, flat, order)
 
 
-def tag_kernel(at_ref, tag_ref, out_ref):
+def strip_tags(at_ref, tag_ref):
     row = lax.broadcasted_iota(jnp.int32, (8, 64), 0)
     x = lax.broadcasted_iota(jnp.int32, (8, 64), 1)
     strip = (x == at_ref[0] * 4 + (row >> 1)).astype(F32).astype(BF16)
@@ -326,21 +326,10 @@
     spread = row == ((lane >> 2) & 1) * 32 + (lane >> 3)
     spread = jnp.dot(picked.astype(BF16), spread.astype(F32).astype(BF16), preferred_element_type=F32)
     odd = (lax.broadcasted_iota(jnp.int32, (8, 128), 0) & 1) == 1
-    out_ref[...] = jnp.where(odd, spread[:, 128:], spread[:, :128]).astype(jnp.int32)
-
-
-def strip_tags(at, tags):
-    return pl.pallas_call(
-        tag_kernel,
-        in_specs=[smem(), spec()],
-        out_specs=spec(),
-        out_shape=shape(8, 128, dtype=jnp.int32),
-        compiler_params=params(),
-        name="strip_tags",
-    )(at, tags)
-
-
-def put_fields(forward, m_ref, tag_ref, right_ref, keep_ref, table):
+    return jnp.where(odd, spread[:, 128:], spread[:, :128]).astype(jnp.int32)
+
+
+def put_fields(forward, m_ref, at_ref, tag_ref, right_ref, keep_ref, table):
     m = [m_ref[pl.ds(f * 8, 8), :] * WEIGHT for f in range(15)]
     rho = m[0]
     inv = 1.0 / rho
@@ -371,7 +360,7 @@
     poly += [-2.0 * front * (a[i] * u[j] + a[j] * u[i]) for i, j in ((0, 1), (0, 2), (1, 2))]
     poly += [front * a[i] for i in range(3)] + [zero] * 3
     z = lax.broadcasted_iota(jnp.int32, (8, 128), 1) & 7
-    tag = tag_ref[...]
+    tag = strip_tags(at_ref, tag_ref)
     density, heat = zero, zero
     walls = []
     for side, at in ((0, 0), (1, 7)):
@@ -582,14 +571,14 @@
 
 
 def first_kernel(
-    dir_ref, in_ref, d0_any, d1_any, d2_any, m0_ref, tag_ref, phi_ref, left_ref, h1_any, edge_any, m_ref,
+    drifted_any, dir_ref, at_ref, in_ref, m0_ref, tag_ref, phi_ref, left_ref, h1_any, edge_any, m_ref,
     right, keep, table, prod, whole, drifted, phi, left, h1, edge, high_ref, low_ref, sems, part_sems, out_sems,
 ):
     forward = dir_ref[0]
     copies = fetch(sems, (phi_ref, phi), (left_ref, left))
-    parts = fetch_parts(part_sems, PIECES[0], (d0_any, d1_any, d2_any), drifted, in_ref, whole, 8)
+    parts = fetch_parts(part_sems, PIECES[0], drifted_any, drifted, in_ref, whole, 8)
     clear_tail(high_ref, low_ref)
-    put_fields(forward, m0_ref, tag_ref, right, keep, table)
+    put_fields(forward, m0_ref, at_ref, tag_ref, right, keep, table)
     settle(copies)
     products(4, phi, right, prod)
 
@@ -618,10 +607,15 @@
     settle(outs)
 
 
-def first_step(forward, flat, drifted, m, tags, phi, left):
+def first_step(forward, at, flat, drifted, m, tags, phi, left):
+    n = len(drifted)
+
+    def kernel(*refs):
+        first_kernel(refs[3 : 3 + n], *refs[:3], *refs[3 + n :])
+
     return pl.pallas_call(
-        first_kernel,
-        in_specs=[smem()] + [anywhere()] * 4 + [spec(), spec(), anywhere(), anywhere()],
+        kernel,
+        in_specs=[smem(), smem()] + [anywhere()] * (1 + n) + [spec(), spec(), anywhere(), anywhere()],
         out_specs=[anywhere(), anywhere(), spec()],
         out_shape=[shape(NSLOT, CELLS), shape(NSLOT * 2, 128), shape(128, 128)],
         scratch_shapes=field_scratch()
@@ -636,20 +630,20 @@
             pltpu.VMEM((NPAD, CELLS), BF16),
             pltpu.VMEM((NPAD, CELLS), BF16),
             pltpu.SemaphoreType.DMA((2,)),
-            pltpu.SemaphoreType.DMA((2 * PARTS,)),
+            pltpu.SemaphoreType.DMA((PARTS + n,)),
             pltpu.SemaphoreType.DMA((PARTS + 1,)),
         ],
-        compiler_params=params(),
+        compiler_params=params(53.7),
         cost_estimate=cost(FIRST_COST),
         name="first_step",
-    )(forward, flat, *drifted, m, tags, phi, left)
-
-
-def inflow_kernel(dir_ref, halo_any, m_ref, out_ref, flux, sems):
-    copies = fetch(sems, (halo_any.at[pl.ds(HALO, 32)], flux))
-    out_ref[...] = m_ref[...]
+    )(forward, at, flat, *drifted, m, tags, phi, left)
+
+
+def inflow_kernel(dir_ref, halo_any, m_any, out_ref, m_ref, flux, sems):
+    copies = fetch(sems, (halo_any.at[pl.ds(HALO, 32)], flux), (m_any, m_ref))
     row = column_of(dir_ref[0], 0) * 2
     settle(copies)
+    out_ref[...] = m_ref[...]
     for half in range(2):
         for k in range(2):
             at = pl.ds(64 * k + row + half, 8, stride=8)
@@ -659,23 +653,23 @@
 def inflow(forward, halo, m):
     return pl.pallas_call(
         inflow_kernel,
-        in_specs=[smem(), anywhere(), spec()],
+        in_specs=[smem(), anywhere(), anywhere()],
         out_specs=spec(),
         out_shape=shape(128, 128),
-        scratch_shapes=[pltpu.VMEM((32, 128), F32), pltpu.SemaphoreType.DMA((1,))],
+        scratch_shapes=[pltpu.VMEM((128, 128), F32), pltpu.VMEM((32, 128), F32), pltpu.SemaphoreType.DMA((2,))],
         compiler_params=params(53),
         name="inflow",
     )(forward, halo, m)
 
 
 def second_kernel(
-    dir_ref, h_any, halo_any, d0_any, d1_any, d2_any, m0_ref, tag_ref, phi_any, out_any, pre_any, heat_ref,
+    drifted_any, dir_ref, at_ref, h_any, halo_any, m0_ref, tag_ref, phi_any, out_any, pre_any, heat_ref,
     right, keep, table, prod, h, halo, drifted, phi, cx, out_ref, pre_ref, sems, part_sems, out_sems,
 ):
     forward = dir_ref[0]
     copies = fetch(sems, (phi_any, phi), (halo_any.at[pl.ds(0, HALO)], halo))
-    parts = fetch_parts(part_sems, PIECES[1], (d0_any, d1_any, d2_any), drifted, h_any, h, 1)
-    heat = put_fields(forward, m0_ref, tag_ref, right, keep, table)
+    parts = fetch_parts(part_sems, PIECES[1], drifted_any, drifted, h_any, h, 1)
+    heat = put_fields(forward, m0_ref, at_ref, tag_ref, right, keep, table)
     put_heat(heat, table, heat_ref)
     copies[0].wait()
     products(4, phi, right, prod)
@@ -707,10 +701,15 @@
     settle(outs)
 
 
-def second_step(forward, h, halo, drifted, m, tags, phi):
+def second_step(forward, at, h, halo, drifted, m, tags, phi):
+    n = len(drifted)
+
+    def kernel(*refs):
+        second_kernel(refs[4 : 4 + n], *refs[:4], *refs[4 + n :])
+
     return pl.pallas_call(
-        second_kernel,
-        in_specs=[smem()] + [anywhere()] * 5 + [spec(), spec(), anywhere()],
+        kernel,
+        in_specs=[smem(), smem()] + [anywhere()] * (2 + n) + [spec(), spec(), anywhere()],
         out_specs=[anywhere(), anywhere(), spec()],
         out_shape=[shape(NSLOT * 8, 128), shape(NSLOT * 2, 128), shape(4, 2, 32)],
         scratch_shapes=field_scratch()
@@ -724,13 +723,13 @@
             pltpu.VMEM((NSLOT * 8, 128), F32),
             pltpu.VMEM((NSLOT * 2, 128), F32),
             pltpu.SemaphoreType.DMA((2,)),
-            pltpu.SemaphoreType.DMA((2 * PARTS,)),
+            pltpu.SemaphoreType.DMA((PARTS + n,)),
             pltpu.SemaphoreType.DMA((PARTS + 1,)),
         ],
-        compiler_params=params(),
+        compiler_params=params(53.7),
         cost_estimate=cost(SECOND_COST),
         name="second_step",
-    )(forward, h, halo, *drifted, m, tags, phi)
+    )(forward, at, h, halo, *drifted, m, tags, phi)
 
 
 def last_kernel(dir_ref, h_any, pre_any, halo_any, phi_any, out_any, pre, halo, phi, sems, out_sems):
@@ -784,16 +783,16 @@
     m, drifted[0] = lax.optimization_barrier((over_y(m), drifted[0]))
     (near,) = hold(m, near)
     near = downstream(near)
-    tags = strip_tags(at, jnp.transpose(wall_tag, (1, 2, 0)).reshape(64, 64))
+    tags = jnp.transpose(wall_tag, (1, 2, 0)).reshape(64, 64)
     m, drifted = over_rest(over_x(m), *drifted)
-    h1, edge, m = first_step(forward, flat, drifted, m, tags, phi, left)
+    h1, edge, m = first_step(forward, at, flat, drifted, m, tags, phi, left)
     drifted = [drift(forward, phi, piece, h1, near) for piece in PIECES[1]]
     m, drifted[0] = lax.optimization_barrier((over_y(inflow(forward, near, m)), drifted[0]))
     m, drifted[1] = lax.optimization_barrier((over_x(m), drifted[1]))
     (edge,) = hold(m, edge)
     edge = downstream(edge)
     m, drifted = over_rest(m, *drifted)
-    out, pre, wall_heat = second_step(forward, h1, near, drifted, m, tags, phi)
+    out, pre, wall_heat = second_step(forward, at, h1, near, drifted, m, tags, phi)
     out = last(forward, out, pre, edge, phi)
     state_next = out.reshape(NSLOT, 2, 4, 128).transpose(0, 2, 1, 3).reshape(NSLOT, 4, 256)
     return state_next, wall_heat

time: 80.2 us -> 76.2 us (0.950)
  Pallas kernels: 50.2 us -> 46.1 us
  waiting for transfers between devices: 6.92 us -> 8.91 us
  other arithmetic: 1.33 us -> 0.08 us
  local copies, waits for them, and re-layouts: 0.84 us -> 0.01 us
    pallas_call x4 -> x3, Pallas kernels: 19 us -> 16.7 us  [the longest x1 8.34 us: second_step(): pl.pallas_call(kernel, in_specs=[smem(), smem()] + [anywhere()] * (2 + n)...]
    ppermute x10, waiting for transfers between devices: 6.92 us -> 8.91 us  [permute(): lax.ppermute(value, AXES, [(i, index_of(*move(*device_of(i)))) for i in r...]
    pallas_call x6 -> x5, Pallas kernels: 23.3 us -> 21.5 us  [drift(): pl.pallas_call(kernel, in_specs=[smem()] + [anywhere()] * (1 + len(states...]
    add x2, other arithmetic: 1.27 us -> 0.02 us  [over_rest(): return (part + permute(part, lambda x, y, c, s: (x, y, c ^ 1, s)), work)]
    unnamed x4, local copies, waits for them, and re-layouts: 0.84 us -> 0.01 us
  transfers between devices with their start and end apart: 10 -> 10, of which waited for: 3 -> 7; matrix products, arithmetic and copies ran while one was open for 2% -> 0% of each run, Pallas kernels for 52% -> 50%
where the time goes in v5:
time: 76.2 us; the launch traced here: 75.7 us
  Pallas kernels  46.1 us (60%)
  starting transfers between devices  19.6 us (26%)
  waiting for transfers between devices  8.91 us (12%)
  between operations  1 us (1%)
    pallas_call x5, Pallas kernels, drift(): pl.pallas_call(kernel, in_specs=[smem()] + [anywhere()] * (1 + len(states...  21.5 us
    ppermute x10, starting transfers between devices, permute(): lax.ppermute(value, AXES, [(i, index_of(*move(*device_of(i)))) for i in r...  19.6 us
    ppermute x10, waiting for transfers between devices, permute(): lax.ppermute(value, AXES, [(i, index_of(*move(*device_of(i)))) for i in r...  8.91 us
    pallas_call x1, Pallas kernels, second_step(): pl.pallas_call(kernel, in_specs=[smem(), smem()] + [anywhere()] * (2 + n)...  8.34 us
    pallas_call x1, Pallas kernels, first_step(): pl.pallas_call(kernel, in_specs=[smem(), smem()] + [anywhere()] * (1 + n)...  7.64 us
    pallas_call x1, Pallas kernels, unpack(): pl.pallas_call(unpack_kernel, in_specs=[smem(), anywhere(), spec()], out_...  5.53 us
    pallas_call x1, Pallas kernels, last(): pl.pallas_call(last_kernel, in_specs=[smem()] + [anywhere()] * 4, out_spe...  2.38 us
  transfers between devices with their start and end apart: 10, of which 7 were waited for; matrix products, arithmetic and copies ran while one was open for 0% of the time, Pallas kernels for 50%

profile of v5, /device:TPU:4, one launch (start us, length us, event | category | flops | bytes accessed | tf_op | source)
XLA Modules:
  0.0 75.7 jit_solution(10095450987150611687)
XLA Ops:
  0.6 5.5 %unpack.1 = (f32[1760,128]{1,0:T(8,128)}, f32[128,128]{1,0:T(8,128)}, bf16[48,896]{1,0:T(8,128)(2,1)}, bf16[864,128]{1,0:T(8,128)(2,1)}) custom-call(s32[1]{0:T(128)} %bitcast.dir_ref.refs_0_, f32[6912,128]{1,0:T(8,128)} %bitcast.17, s32[864]{0:T(1024)} %order_ref.1), custom_call_target="tpu_custom_call" | custom-call | tf_op jit(solution)/shard_map/unpack/pallas_call | solution.py:293
  6.2 1.7 %collective-permute-start = (f32[128,128]{1,0:T(8,128)}, f32[128,128]{1,0:T(8,128)S(1)}, u32[]{:S(2)}, u32[]{:S(2)}) collective-permute-start(f32[128,128]{1,0:T(8,128)} %get-tuple-element.25), channel_id=1, source_target_pairs={{0,32},{1,33},{2,34},{3,35},{4,36},{5,37},{6,38},{7,39},{8,40},{9,... | collective-permute-start | bytes 196616 | tf_op jit(solution)/shard_map/ppermute | solution.py:55
  7.8 3.9 %drift.5.refs_3_ = f32[288,1024]{1,0:T(8,128)} custom-call(s32[1]{0:T(128)} %bitcast.dir_ref.refs_0_, bf16[864,128]{1,0:T(8,128)(2,1)} %get-tuple-element.26.refs_1_.refs_7_.refs_9_.phi_any, f32[6912,128]{1,0:T(8,128)} %bitcast.18), custom_call_target="tpu_custom_call" | custom-call | flops 3449999872 | bytes 10000 | tf_op jit(solution)/shard_map/drift/pallas_call | solution.py:517
  11.8 0.0 collective-permute-done
  11.8 0.0 copy-done.1
  11.8 1.3 %collective-permute-start.1 = (f32[128,128]{1,0:T(8,128)S(1)}, f32[128,128]{1,0:T(8,128)S(1)}, u32[]{:S(2)}, u32[]{:S(2)}) collective-permute-start(f32[128,128]{1,0:T(8,128)S(1)} %add.24.refs_0_), channel_id=1, source_target_pairs={{0,64},{1,65},{2,66},{3,67},{4,68},{5,69},{6,70},{7,71},{8,72},{9,... | collective-permute-start | bytes 196616 | tf_op jit(solution)/shard_map/ppermute | solution.py:55
  13.1 2.9 %collective-permute-start.4 = (f32[1760,128]{1,0:T(8,128)}, f32[1760,128]{1,0:T(8,128)}, u32[]{:S(2)}, u32[]{:S(2)}) collective-permute-start(f32[1760,128]{1,0:T(8,128)} %hold.2), channel_id=1, source_target_pairs={{0,15},{1,0},{2,1},{3,2},{4,3},{5,4},{6,5},{7,6},{8,7},{9,8},{10,9... | collective-permute-start | bytes 2703368 | tf_op jit(solution)/shard_map/ppermute | solution.py:55
  16.0 0.2 collective-permute-done.1
  16.2 0.0 copy-start
  16.2 6.0 %collective-permute-start.2 = (f32[128,128]{1,0:T(8,128)S(1)}, f32[128,128]{1,0:T(8,128)S(1)}, u32[]{:S(2)}, u32[]{:S(2)}) collective-permute-start(f32[128,128]{1,0:T(8,128)S(1)} %add.25), channel_id=1, source_target_pairs={{0,128},{1,129},{2,130},{3,131},{4,132},{5,133},{6,134},{7,135},{8... | collective-permute-start | bytes 196616 | tf_op jit(solution)/shard_map/ppermute | solution.py:55
  22.2 6.0 %drift.6.refs_4_ = f32[576,1024]{1,0:T(8,128)} custom-call(s32[1]{0:T(128)} %bitcast.dir_ref.refs_0_, bf16[864,128]{1,0:T(8,128)(2,1)} %get-tuple-element.26.refs_1_.refs_7_.refs_9_.phi_any, f32[6912,128]{1,0:T(8,128)} %bitcast.19), custom_call_target="tpu_custom_call" | custom-call | flops 3449999872 | bytes 10000 | tf_op jit(solution)/shard_map/drift/pallas_call | solution.py:517
  28.2 0.0 collective-permute-done.2
  28.2 0.1 collective-permute-start.3
  28.3 1.2 %collective-permute-done.3 = f32[128,128]{1,0:T(8,128)S(1)} collective-permute-done((f32[128,128]{1,0:T(8,128)S(1)}, f32[128,128]{1,0:T(8,128)S(1)}, u32[]{:S(2)}, u32[]{:S(2)}) %collective-permute-start.3) | collective-permute-done | bytes 65568 | tf_op jit(solution)/shard_map/ppermute | solution.py:55
  29.6 7.6 %first_step.1 = (f32[864,1024]{1,0:T(8,128)}, f32[1728,128]{1,0:T(8,128)}, f32[128,128]{1,0:T(8,128)S(1)}) custom-call(s32[1]{0:T(128)} %bitcast.dir_ref.refs_0_, s32[1]{0:T(128)} %bitcast.1.refs_1_, f32[6912,128]{1,0:T(8,128)} %bitcast.20, f32[288,1024]{1,0:T(8,128)} %drift.5.refs_3_, f32[576,1024]{1,0:T(8,128)} %drift.6.refs_4_, ...), custom_call_target="tpu_custom_call" | custom-call | flops 5750000128 | bytes 10000 | tf_op jit(solution)/shard_map/first_step/pallas_call | solution.py:616
  37.3 3.9 %collective-permute-done.4.halo_any.refs_3_ = f32[1760,128]{1,0:T(8,128)} collective-permute-done((f32[1760,128]{1,0:T(8,128)}, f32[1760,128]{1,0:T(8,128)}, u32[]{:S(2)}, u32[]{:S(2)}) %collective-permute-start.4) | collective-permute-done | bytes 901152 | tf_op jit(solution)/shard_map/ppermute | solution.py:55
  41.1 0.7 inflow.1
  41.9 0.2 collective-permute-start.5
  42.1 3.1 %drift.7.refs_4_ = f32[192,1024]{1,0:T(8,128)} custom-call(s32[1]{0:T(128)} %bitcast.dir_ref.refs_0_, bf16[864,128]{1,0:T(8,128)(2,1)} %get-tuple-element.26.refs_1_.refs_7_.refs_9_.phi_any, f32[864,1024]{1,0:T(8,128)} %get-tuple-element.33.refs_2_, f32[1760,128]{1,0:T(8,128)} %collective-permute-done.4.halo_any.refs_3_), custom_call_target="tpu_custom_call" | custom-call | flops 3449999872 | bytes 10000 | tf_op jit(solution)/shard_map/drift/pallas_call | solution.py:517
  45.2 1.0 %collective-permute-done.5 = f32[128,128]{1,0:T(8,128)S(1)} collective-permute-done((f32[128,128]{1,0:T(8,128)S(1)}, f32[128,128]{1,0:T(8,128)S(1)}, u32[]{:S(2)}, u32[]{:S(2)}) %collective-permute-start.5) | collective-permute-done | bytes 65568 | tf_op jit(solution)/shard_map/ppermute | solution.py:55
  46.3 0.9 %collective-permute-start.6 = (f32[128,128]{1,0:T(8,128)S(1)}, f32[128,128]{1,0:T(8,128)S(1)}, u32[]{:S(2)}, u32[]{:S(2)}) collective-permute-start(f32[128,128]{1,0:T(8,128)S(1)} %add.28), channel_id=1, source_target_pairs={{0,64},{1,65},{2,66},{3,67},{4,68},{5,69},{6,70},{7,71},{8,72},{9,... | collective-permute-start | bytes 196616 | tf_op jit(solution)/shard_map/ppermute | solution.py:55
  47.2 3.1 %drift.8.refs_5_ = f32[192,1024]{1,0:T(8,128)} custom-call(s32[1]{0:T(128)} %bitcast.dir_ref.refs_0_, bf16[864,128]{1,0:T(8,128)(2,1)} %get-tuple-element.26.refs_1_.refs_7_.refs_9_.phi_any, f32[864,1024]{1,0:T(8,128)} %get-tuple-element.33.refs_2_, f32[1760,128]{1,0:T(8,128)} %collective-permute-done.4.halo_any.refs_3_), custom_call_target="tpu_custom_call" | custom-call | flops 3449999872 | bytes 10000 | tf_op jit(solution)/shard_map/drift/pallas_call | solution.py:517
  50.3 0.4 collective-permute-done.6
  50.6 0.3 collective-permute-start.9
  50.9 6.1 %collective-permute-start.7 = (f32[128,128]{1,0:T(8,128)S(1)}, f32[128,128]{1,0:T(8,128)S(1)}, u32[]{:S(2)}, u32[]{:S(2)}) collective-permute-start(f32[128,128]{1,0:T(8,128)S(1)} %add.29.refs_0_), channel_id=1, source_target_pairs={{0,128},{1,129},{2,130},{3,131},{4,132},{5,133},{6,134},{7,135},{8... | collective-permute-start | bytes 196616 | tf_op jit(solution)/shard_map/ppermute | solution.py:55
  57.0 5.4 %drift.9.refs_6_ = f32[480,1024]{1,0:T(8,128)} custom-call(s32[1]{0:T(128)} %bitcast.dir_ref.refs_0_, bf16[864,128]{1,0:T(8,128)(2,1)} %get-tuple-element.26.refs_1_.refs_7_.refs_9_.phi_any, f32[864,1024]{1,0:T(8,128)} %get-tuple-element.33.refs_2_, f32[1760,128]{1,0:T(8,128)} %collective-permute-done.4.halo_any.refs_3_), custom_call_target="tpu_custom_call" | custom-call | flops 3449999872 | bytes 10000 | tf_op jit(solution)/shard_map/drift/pallas_call | solution.py:517
  62.5 0.0 collective-permute-done.7
  62.5 0.1 collective-permute-start.8
  62.6 1.2 %collective-permute-done.8 = f32[128,128]{1,0:T(8,128)S(1)} collective-permute-done((f32[128,128]{1,0:T(8,128)S(1)}, f32[128,128]{1,0:T(8,128)S(1)}, u32[]{:S(2)}, u32[]{:S(2)}) %collective-permute-start.8) | collective-permute-done | bytes 65568 | tf_op jit(solution)/shard_map/ppermute | solution.py:55
  63.8 8.3 %second_step.1 = (f32[6912,128]{1,0:T(8,128)}, f32[1728,128]{1,0:T(8,128)}, f32[4,2,32]{2,1,0:T(2,128)}) custom-call(s32[1]{0:T(128)} %bitcast.dir_ref.refs_0_, s32[1]{0:T(128)} %bitcast.1.refs_1_, f32[864,1024]{1,0:T(8,128)} %get-tuple-element.33.refs_2_, f32[1760,128]{1,0:T(8,128)} %collective-permute-done.4.halo_any.refs_3_, f32[192,1024]{1,0:T(8,128)} %drift.7.refs_4_, ...), custom_call_target="tpu_custom_call" | custom-call | flops 2300000000 | bytes 10000 | tf_op jit(solution)/shard_map/second_step/pallas_call | solution.py:710
  72.2 1.0 %collective-permute-done.9.halo_any = f32[1728,128]{1,0:T(8,128)} collective-permute-done((f32[1728,128]{1,0:T(8,128)}, f32[1728,128]{1,0:T(8,128)}, u32[]{:S(2)}, u32[]{:S(2)}) %collective-permute-start.9) | collective-permute-done | bytes 884768 | tf_op jit(solution)/shard_map/ppermute | solution.py:55
  73.2 2.4 %last.1 = f32[6912,128]{1,0:T(8,128)} custom-call(s32[1]{0:T(128)} %bitcast.dir_ref.refs_0_, f32[6912,128]{1,0:T(8,128)} %get-tuple-element.44.h_any, f32[1728,128]{1,0:T(8,128)} %get-tuple-element.45.pre_any, f32[1728,128]{1,0:T(8,128)} %collective-permute-done.9.halo_any, ...), custom_call_target="tpu_custom_call", output_to_operand_aliasing={{}: (1, {})} | custom-call | tf_op jit(solution)/shard_map/last/pallas_call | solution.py:759
  (12 shorter events, 0.1 us)
Async XLA Ops:
  6.2 5.6 %collective-permute-start = (f32[128,128]{1,0:T(8,128)}, f32[128,128]{1,0:T(8,128)S(1)}, u32[]{:S(2)}, u32[]{:S(2)}) collective-permute-start(f32[128,128]{1,0:T(8,128)} %get-tuple-element.25), channel_id=1, source_target_pairs={{0,32},{1,33},{2,34},{3,35},{4,36},{5,37},{6,38},{7,39},{8,40},{9,... | collective-permute-start | bytes 196616 | tf_op jit(solution)/shard_map/ppermute | solution.py:55
  7.8 3.9 %copy-start.1 = (f32[128,128]{1,0:T(8,128)S(1)}, f32[128,128]{1,0:T(8,128)}, u32[]{:S(2)}) copy-start(f32[128,128]{1,0:T(8,128)} %get-tuple-element.25) | copy-start | bytes 196612
  11.8 4.4 %collective-permute-start.1 = (f32[128,128]{1,0:T(8,128)S(1)}, f32[128,128]{1,0:T(8,128)S(1)}, u32[]{:S(2)}, u32[]{:S(2)}) collective-permute-start(f32[128,128]{1,0:T(8,128)S(1)} %add.24.refs_0_), channel_id=1, source_target_pairs={{0,64},{1,65},{2,66},{3,67},{4,68},{5,69},{6,70},{7,71},{8,72},{9,... | collective-permute-start | bytes 196616 | tf_op jit(solution)/shard_map/ppermute | solution.py:55
  13.1 28.0 %collective-permute-start.4 = (f32[1760,128]{1,0:T(8,128)}, f32[1760,128]{1,0:T(8,128)}, u32[]{:S(2)}, u32[]{:S(2)}) collective-permute-start(f32[1760,128]{1,0:T(8,128)} %hold.2), channel_id=1, source_target_pairs={{0,15},{1,0},{2,1},{3,2},{4,3},{5,4},{6,5},{7,6},{8,7},{9,8},{10,9... | collective-permute-start | bytes 2703368 | tf_op jit(solution)/shard_map/ppermute | solution.py:55
  16.2 13.4 %copy-start = (s32[64,2,32]{0,2,1:T(8,128)S(1)}, s32[64,2,32]{0,2,1:T(8,128)}, u32[]{:S(2)}) copy-start(s32[64,2,32]{0,2,1:T(8,128)} %param.5) | copy-start | bytes 49156
  16.2 12.0 %collective-permute-start.2 = (f32[128,128]{1,0:T(8,128)S(1)}, f32[128,128]{1,0:T(8,128)S(1)}, u32[]{:S(2)}, u32[]{:S(2)}) collective-permute-start(f32[128,128]{1,0:T(8,128)S(1)} %add.25), channel_id=1, source_target_pairs={{0,128},{1,129},{2,130},{3,131},{4,132},{5,133},{6,134},{7,135},{8... | collective-permute-start | bytes 196616 | tf_op jit(solution)/shard_map/ppermute | solution.py:55
  28.2 1.3 %collective-permute-start.3 = (f32[128,128]{1,0:T(8,128)S(1)}, f32[128,128]{1,0:T(8,128)S(1)}, u32[]{:S(2)}, u32[]{:S(2)}) collective-permute-start(f32[128,128]{1,0:T(8,128)S(1)} %add.26), channel_id=1, source_target_pairs={{0,16},{1,17},{2,18},{3,19},{4,20},{5,21},{6,22},{7,23},{8,24},{9,... | collective-permute-start | bytes 196616 | tf_op jit(solution)/shard_map/ppermute | solution.py:55
  41.9 4.4 %collective-permute-start.5 = (f32[128,128]{1,0:T(8,128)S(1)}, f32[128,128]{1,0:T(8,128)S(1)}, u32[]{:S(2)}, u32[]{:S(2)}) collective-permute-start(f32[128,128]{1,0:T(8,128)S(1)} %inflow.1), channel_id=1, source_target_pairs={{0,32},{1,33},{2,34},{3,35},{4,36},{5,37},{6,38},{7,39},{8,40},{9,... | collective-permute-start | bytes 196616 | tf_op jit(solution)/shard_map/ppermute | solution.py:55
  46.3 4.4 %collective-permute-start.6 = (f32[128,128]{1,0:T(8,128)S(1)}, f32[128,128]{1,0:T(8,128)S(1)}, u32[]{:S(2)}, u32[]{:S(2)}) collective-permute-start(f32[128,128]{1,0:T(8,128)S(1)} %add.28), channel_id=1, source_target_pairs={{0,64},{1,65},{2,66},{3,67},{4,68},{5,69},{6,70},{7,71},{8,72},{9,... | collective-permute-start | bytes 196616 | tf_op jit(solution)/shard_map/ppermute | solution.py:55
  50.6 22.5 %collective-permute-start.9 = (f32[1728,128]{1,0:T(8,128)}, f32[1728,128]{1,0:T(8,128)}, u32[]{:S(2)}, u32[]{:S(2)}) collective-permute-start(f32[1728,128]{1,0:T(8,128)} %hold.3), channel_id=1, source_target_pairs={{0,15},{1,0},{2,1},{3,2},{4,3},{5,4},{6,5},{7,6},{8,7},{9,8},{10,9... | collective-permute-start | bytes 2654216 | tf_op jit(solution)/shard_map/ppermute | solution.py:55
  50.9 11.6 %collective-permute-start.7 = (f32[128,128]{1,0:T(8,128)S(1)}, f32[128,128]{1,0:T(8,128)S(1)}, u32[]{:S(2)}, u32[]{:S(2)}) collective-permute-start(f32[128,128]{1,0:T(8,128)S(1)} %add.29.refs_0_), channel_id=1, source_target_pairs={{0,128},{1,129},{2,130},{3,131},{4,132},{5,133},{6,134},{7,135},{8... | collective-permute-start | bytes 196616 | tf_op jit(solution)/shard_map/ppermute | solution.py:55
  62.5 1.3 %collective-permute-start.8 = (f32[128,128]{1,0:T(8,128)S(1)}, f32[128,128]{1,0:T(8,128)S(1)}, u32[]{:S(2)}, u32[]{:S(2)}) collective-permute-start(f32[128,128]{1,0:T(8,128)S(1)} %add.30), channel_id=1, source_target_pairs={{0,16},{1,17},{2,18},{3,19},{4,20},{5,21},{6,22},{7,23},{8,24},{9,... | collective-permute-start | bytes 196616 | tf_op jit(solution)/shard_map/ppermute | solution.py:55

commit v6 on v5

--- a/solution.py
+++ b/solution.py
@@ -234,9 +234,10 @@
     low_ref[rows, cols] = (value - high.astype(F32)).astype(BF16)
 
 
-PARTS = 3
+PARTS = 9
+LAST_PARTS = 3
 HALO = 2 * NSLOT
-PIECES = (((0, 288), (288, 576)), ((0, 192), (192, 192), (384, 480)))
+PIECES = (((0, 192), (192, 672)), ((0, 192), (192, 192), (384, 480)))
 FIRST_COST, SECOND_COST, HOLD_COST = 5, 2, 3
 DRIFT_COST = 3
 
@@ -456,14 +457,15 @@
 
 
 def drift_kernel(dir_ref, phi_any, *refs, start, size, first_step):
-    steps = size // 3
+    steps = 96
+    count = size // steps
     if first_step:
         state_any, out_any, phi, state, out, coef, sems, out_sems = refs
-        spans = [(pl.ds((start + q * steps) * 8, steps * 8), pl.ds(q * steps * 8, steps * 8)) for q in range(3)]
+        spans = [(pl.ds((start + q * steps) * 8, steps * 8), pl.ds(q * steps * 8, steps * 8)) for q in range(count)]
         pairs = [[(state_any.at[a], state.at[b])] for a, b in spans]
     else:
         state_any, halo_any, out_any, phi, state, halo, out, coef, sems, out_sems = refs
-        spans = [(pl.ds(start + q * steps, steps), pl.ds(q * steps, steps)) for q in range(3)]
+        spans = [(pl.ds(start + q * steps, steps), pl.ds(q * steps, steps)) for q in range(count)]
         pairs = [[(state_any.at[a], state.at[b])] for a, b in spans]
         pairs[0].append((halo_any.at[pl.ds(start * 2, size * 2)], halo))
     flat_pairs = [(phi_any.at[pl.ds(start, size)], phi)] + [pair for group in pairs for pair in group]
@@ -474,7 +476,7 @@
     step = 32
     at = 1
     outs = []
-    for q in range(3):
+    for q in range(count):
         settle(copies[at : at + len(pairs[q])])
         at += len(pairs[q])
 
@@ -524,8 +526,8 @@
         + [
             pltpu.VMEM((size, CELLS), F32),
             pltpu.VMEM((size, 768), F32),
-            pltpu.SemaphoreType.DMA((5,)),
-            pltpu.SemaphoreType.DMA((3,)),
+            pltpu.SemaphoreType.DMA((2 + size // 96,)),
+            pltpu.SemaphoreType.DMA((size // 96,)),
         ],
         compiler_params=params(),
         cost_estimate=cost(DRIFT_COST),
@@ -670,7 +672,6 @@
     copies = fetch(sems, (phi_any, phi), (halo_any.at[pl.ds(0, HALO)], halo))
     parts = fetch_parts(part_sems, PIECES[1], drifted_any, drifted, h_any, h, 1)
     heat = put_fields(forward, m0_ref, at_ref, tag_ref, right, keep, table)
-    put_heat(heat, table, heat_ref)
     copies[0].wait()
     products(4, phi, right, prod)
     cx[...] = coefs_of(phi[...], 1)
@@ -698,6 +699,7 @@
         outs[-1].start()
     outs.append(pltpu.make_async_copy(pre_ref, pre_any, out_sems.at[PARTS]))
     outs[-1].start()
+    put_heat(heat, table, heat_ref)
     settle(outs)
 
 
@@ -734,8 +736,8 @@
 
 def last_kernel(dir_ref, h_any, pre_any, halo_any, phi_any, out_any, pre, halo, phi, sems, out_sems):
     del h_any
-    size = HALO // PARTS
-    spans = [pl.ds(p * size, size) for p in range(PARTS)]
+    size = HALO // LAST_PARTS
+    spans = [pl.ds(p * size, size) for p in range(LAST_PARTS)]
     pairs = [(phi_any, phi)]
     for rows in spans:
         pairs += [(pre_any.at[rows], pre.at[rows]), (halo_any.at[rows], halo.at[rows])]
@@ -766,8 +768,8 @@
             pltpu.VMEM((NSLOT * 2, 128), F32),
             pltpu.VMEM((NSLOT * 2, 128), F32),
             pltpu.VMEM((NSLOT, 128), BF16),
-            pltpu.SemaphoreType.DMA((1 + 2 * PARTS,)),
-            pltpu.SemaphoreType.DMA((PARTS,)),
+            pltpu.SemaphoreType.DMA((1 + 2 * LAST_PARTS,)),
+            pltpu.SemaphoreType.DMA((LAST_PARTS,)),
         ],
         compiler_params=params(),
         name="last",

time: 76.2 us -> 75.2 us (0.987)
  Pallas kernels: 46.1 us -> 45.2 us
  transfers between devices with their start and end apart: 10 -> 10, of which waited for: 7 -> 7; matrix products, arithmetic and copies ran while one was open for 0% -> 0% of each run, Pallas kernels for 50% -> 49%
where the time goes in v6:
time: 75.2 us; the launch traced here: 74.7 us
  Pallas kernels  45.2 us (60%)
  starting transfers between devices  19.6 us (26%)
  waiting for transfers between devices  8.84 us (12%)
  between operations  1 us (1%)
    pallas_call x5, Pallas kernels, drift(): pl.pallas_call(kernel, in_specs=[smem()] + [anywhere()] * (1 + len(states...  21.4 us
    ppermute x10, starting transfers between devices, permute(): lax.ppermute(value, AXES, [(i, index_of(*move(*device_of(i)))) for i in r...  19.6 us
    ppermute x10, waiting for transfers between devices, permute(): lax.ppermute(value, AXES, [(i, index_of(*move(*device_of(i)))) for i in r...  8.84 us
    pallas_call x1, Pallas kernels, first_step(): pl.pallas_call(kernel, in_specs=[smem(), smem()] + [anywhere()] * (1 + n)...  7.75 us
    pallas_call x1, Pallas kernels, second_step(): pl.pallas_call(kernel, in_specs=[smem(), smem()] + [anywhere()] * (2 + n)...  7.68 us
    pallas_call x1, Pallas kernels, unpack(): pl.pallas_call(unpack_kernel, in_specs=[smem(), anywhere(), spec()], out_...  5.25 us
    pallas_call x1, Pallas kernels, last(): pl.pallas_call(last_kernel, in_specs=[smem()] + [anywhere()] * 4, out_spe...  2.38 us
  transfers between devices with their start and end apart: 10, of which 7 were waited for; matrix products, arithmetic and copies ran while one was open for 0% of the time, Pallas kernels for 49%

profile of v6, /device:TPU:4, one launch (start us, length us, event | category | flops | bytes accessed | tf_op | source)
XLA Modules:
  0.0 74.7 jit_solution(14854128518592614538)
XLA Ops:
  0.6 5.2 %unpack.1 = (f32[1760,128]{1,0:T(8,128)}, f32[128,128]{1,0:T(8,128)}, bf16[48,896]{1,0:T(8,128)(2,1)}, bf16[864,128]{1,0:T(8,128)(2,1)}) custom-call(s32[1]{0:T(128)} %bitcast.dir_ref.refs_0_, f32[6912,128]{1,0:T(8,128)} %bitcast.17, s32[864]{0:T(1024)} %order_ref.1), custom_call_target="tpu_custom_call" | custom-call | tf_op jit(solution)/shard_map/unpack/pallas_call | solution.py:294
  5.9 1.7 %collective-permute-start = (f32[128,128]{1,0:T(8,128)}, f32[128,128]{1,0:T(8,128)S(1)}, u32[]{:S(2)}, u32[]{:S(2)}) collective-permute-start(f32[128,128]{1,0:T(8,128)} %get-tuple-element.25), channel_id=1, source_target_pairs={{0,32},{1,33},{2,34},{3,35},{4,36},{5,37},{6,38},{7,39},{8,40},{9,... | collective-permute-start | bytes 196616 | tf_op jit(solution)/shard_map/ppermute | solution.py:55
  7.6 3.1 %drift.5.refs_3_ = f32[192,1024]{1,0:T(8,128)} custom-call(s32[1]{0:T(128)} %bitcast.dir_ref.refs_0_, bf16[864,128]{1,0:T(8,128)(2,1)} %get-tuple-element.26.refs_1_.refs_7_.refs_9_.phi_any, f32[6912,128]{1,0:T(8,128)} %bitcast.18), custom_call_target="tpu_custom_call" | custom-call | flops 3449999872 | bytes 10000 | tf_op jit(solution)/shard_map/drift/pallas_call | solution.py:519
  10.7 0.0 collective-permute-done
  10.7 0.0 copy-done.1
  10.7 1.3 %collective-permute-start.1 = (f32[128,128]{1,0:T(8,128)S(1)}, f32[128,128]{1,0:T(8,128)S(1)}, u32[]{:S(2)}, u32[]{:S(2)}) collective-permute-start(f32[128,128]{1,0:T(8,128)S(1)} %add.24.refs_0_), channel_id=1, source_target_pairs={{0,64},{1,65},{2,66},{3,67},{4,68},{5,69},{6,70},{7,71},{8,72},{9,... | collective-permute-start | bytes 196616 | tf_op jit(solution)/shard_map/ppermute | solution.py:55
  12.0 2.9 %collective-permute-start.4 = (f32[1760,128]{1,0:T(8,128)}, f32[1760,128]{1,0:T(8,128)}, u32[]{:S(2)}, u32[]{:S(2)}) collective-permute-start(f32[1760,128]{1,0:T(8,128)} %hold.2), channel_id=1, source_target_pairs={{0,15},{1,0},{2,1},{3,2},{4,3},{5,4},{6,5},{7,6},{8,7},{9,8},{10,9... | collective-permute-start | bytes 2703368 | tf_op jit(solution)/shard_map/ppermute | solution.py:55
  15.0 0.1 collective-permute-done.1
  15.1 0.0 copy-start
  15.1 6.1 %collective-permute-start.2 = (f32[128,128]{1,0:T(8,128)S(1)}, f32[128,128]{1,0:T(8,128)S(1)}, u32[]{:S(2)}, u32[]{:S(2)}) collective-permute-start(f32[128,128]{1,0:T(8,128)S(1)} %add.25), channel_id=1, source_target_pairs={{0,128},{1,129},{2,130},{3,131},{4,132},{5,133},{6,134},{7,135},{8... | collective-permute-start | bytes 196616 | tf_op jit(solution)/shard_map/ppermute | solution.py:55
  21.2 6.7 %drift.6.refs_4_ = f32[672,1024]{1,0:T(8,128)} custom-call(s32[1]{0:T(128)} %bitcast.dir_ref.refs_0_, bf16[864,128]{1,0:T(8,128)(2,1)} %get-tuple-element.26.refs_1_.refs_7_.refs_9_.phi_any, f32[6912,128]{1,0:T(8,128)} %bitcast.19), custom_call_target="tpu_custom_call" | custom-call | flops 3449999872 | bytes 10000 | tf_op jit(solution)/shard_map/drift/pallas_call | solution.py:519
  27.8 0.0 collective-permute-done.2
  27.9 0.1 collective-permute-start.3
  28.0 1.2 %collective-permute-done.3 = f32[128,128]{1,0:T(8,128)S(1)} collective-permute-done((f32[128,128]{1,0:T(8,128)S(1)}, f32[128,128]{1,0:T(8,128)S(1)}, u32[]{:S(2)}, u32[]{:S(2)}) %collective-permute-start.3) | collective-permute-done | bytes 65568 | tf_op jit(solution)/shard_map/ppermute | solution.py:55
  29.2 7.7 %first_step.1 = (f32[864,1024]{1,0:T(8,128)}, f32[1728,128]{1,0:T(8,128)}, f32[128,128]{1,0:T(8,128)S(1)}) custom-call(s32[1]{0:T(128)} %bitcast.dir_ref.refs_0_, s32[1]{0:T(128)} %bitcast.1.refs_1_, f32[6912,128]{1,0:T(8,128)} %bitcast.20, f32[192,1024]{1,0:T(8,128)} %drift.5.refs_3_, f32[672,1024]{1,0:T(8,128)} %drift.6.refs_4_, ...), custom_call_target="tpu_custom_call" | custom-call | flops 5750000128 | bytes 10000 | tf_op jit(solution)/shard_map/first_step/pallas_call | solution.py:618
  37.0 3.1 %collective-permute-done.4.halo_any.refs_3_ = f32[1760,128]{1,0:T(8,128)} collective-permute-done((f32[1760,128]{1,0:T(8,128)}, f32[1760,128]{1,0:T(8,128)}, u32[]{:S(2)}, u32[]{:S(2)}) %collective-permute-start.4) | collective-permute-done | bytes 901152 | tf_op jit(solution)/shard_map/ppermute | solution.py:55
  40.1 0.7 inflow.1
  40.8 0.2 collective-permute-start.5
  41.0 3.1 %drift.7.refs_4_ = f32[192,1024]{1,0:T(8,128)} custom-call(s32[1]{0:T(128)} %bitcast.dir_ref.refs_0_, bf16[864,128]{1,0:T(8,128)(2,1)} %get-tuple-element.26.refs_1_.refs_7_.refs_9_.phi_any, f32[864,1024]{1,0:T(8,128)} %get-tuple-element.33.refs_2_, f32[1760,128]{1,0:T(8,128)} %collective-permute-done.4.halo_any.refs_3_), custom_call_target="tpu_custom_call" | custom-call | flops 3449999872 | bytes 10000 | tf_op jit(solution)/shard_map/drift/pallas_call | solution.py:519
  44.2 1.0 %collective-permute-done.5 = f32[128,128]{1,0:T(8,128)S(1)} collective-permute-done((f32[128,128]{1,0:T(8,128)S(1)}, f32[128,128]{1,0:T(8,128)S(1)}, u32[]{:S(2)}, u32[]{:S(2)}) %collective-permute-start.5) | collective-permute-done | bytes 65568 | tf_op jit(solution)/shard_map/ppermute | solution.py:55
  45.2 1.1 %collective-permute-start.6 = (f32[128,128]{1,0:T(8,128)S(1)}, f32[128,128]{1,0:T(8,128)S(1)}, u32[]{:S(2)}, u32[]{:S(2)}) collective-permute-start(f32[128,128]{1,0:T(8,128)S(1)} %add.28), channel_id=1, source_target_pairs={{0,64},{1,65},{2,66},{3,67},{4,68},{5,69},{6,70},{7,71},{8,72},{9,... | collective-permute-start | bytes 196616 | tf_op jit(solution)/shard_map/ppermute | solution.py:55
  46.3 3.2 %drift.8.refs_5_ = f32[192,1024]{1,0:T(8,128)} custom-call(s32[1]{0:T(128)} %bitcast.dir_ref.refs_0_, bf16[864,128]{1,0:T(8,128)(2,1)} %get-tuple-element.26.refs_1_.refs_7_.refs_9_.phi_any, f32[864,1024]{1,0:T(8,128)} %get-tuple-element.33.refs_2_, f32[1760,128]{1,0:T(8,128)} %collective-permute-done.4.halo_any.refs_3_), custom_call_target="tpu_custom_call" | custom-call | flops 3449999872 | bytes 10000 | tf_op jit(solution)/shard_map/drift/pallas_call | solution.py:519
  49.4 0.3 collective-permute-done.6
  49.7 0.1 collective-permute-start.9
  49.8 6.0 %collective-permute-start.7 = (f32[128,128]{1,0:T(8,128)S(1)}, f32[128,128]{1,0:T(8,128)S(1)}, u32[]{:S(2)}, u32[]{:S(2)}) collective-permute-start(f32[128,128]{1,0:T(8,128)S(1)} %add.29.refs_0_), channel_id=1, source_target_pairs={{0,128},{1,129},{2,130},{3,131},{4,132},{5,133},{6,134},{7,135},{8... | collective-permute-start | bytes 196616 | tf_op jit(solution)/shard_map/ppermute | solution.py:55
  55.9 5.3 %drift.9.refs_6_ = f32[480,1024]{1,0:T(8,128)} custom-call(s32[1]{0:T(128)} %bitcast.dir_ref.refs_0_, bf16[864,128]{1,0:T(8,128)(2,1)} %get-tuple-element.26.refs_1_.refs_7_.refs_9_.phi_any, f32[864,1024]{1,0:T(8,128)} %get-tuple-element.33.refs_2_, f32[1760,128]{1,0:T(8,128)} %collective-permute-done.4.halo_any.refs_3_), custom_call_target="tpu_custom_call" | custom-call | flops 3449999872 | bytes 10000 | tf_op jit(solution)/shard_map/drift/pallas_call | solution.py:519
  61.2 0.0 collective-permute-done.7
  61.2 0.1 collective-permute-start.8
  61.3 1.2 %collective-permute-done.8 = f32[128,128]{1,0:T(8,128)S(1)} collective-permute-done((f32[128,128]{1,0:T(8,128)S(1)}, f32[128,128]{1,0:T(8,128)S(1)}, u32[]{:S(2)}, u32[]{:S(2)}) %collective-permute-start.8) | collective-permute-done | bytes 65568 | tf_op jit(solution)/shard_map/ppermute | solution.py:55
  62.6 7.7 %second_step.1 = (f32[6912,128]{1,0:T(8,128)}, f32[1728,128]{1,0:T(8,128)}, f32[4,2,32]{2,1,0:T(2,128)}) custom-call(s32[1]{0:T(128)} %bitcast.dir_ref.refs_0_, s32[1]{0:T(128)} %bitcast.1.refs_1_, f32[864,1024]{1,0:T(8,128)} %get-tuple-element.33.refs_2_, f32[1760,128]{1,0:T(8,128)} %collective-permute-done.4.halo_any.refs_3_, f32[192,1024]{1,0:T(8,128)} %drift.7.refs_4_, ...), custom_call_target="tpu_custom_call" | custom-call | flops 2300000000 | bytes 10000 | tf_op jit(solution)/shard_map/second_step/pallas_call | solution.py:712
  70.3 1.9 %collective-permute-done.9.halo_any = f32[1728,128]{1,0:T(8,128)} collective-permute-done((f32[1728,128]{1,0:T(8,128)}, f32[1728,128]{1,0:T(8,128)}, u32[]{:S(2)}, u32[]{:S(2)}) %collective-permute-start.9) | collective-permute-done | bytes 884768 | tf_op jit(solution)/shard_map/ppermute | solution.py:55
  72.2 2.4 %last.1 = f32[6912,128]{1,0:T(8,128)} custom-call(s32[1]{0:T(128)} %bitcast.dir_ref.refs_0_, f32[6912,128]{1,0:T(8,128)} %get-tuple-element.44.h_any, f32[1728,128]{1,0:T(8,128)} %get-tuple-element.45.pre_any, f32[1728,128]{1,0:T(8,128)} %collective-permute-done.9.halo_any, ...), custom_call_target="tpu_custom_call", output_to_operand_aliasing={{}: (1, {})} | custom-call | tf_op jit(solution)/shard_map/last/pallas_call | solution.py:761
  (12 shorter events, 0.1 us)
Async XLA Ops:
  5.9 4.8 %collective-permute-start = (f32[128,128]{1,0:T(8,128)}, f32[128,128]{1,0:T(8,128)S(1)}, u32[]{:S(2)}, u32[]{:S(2)}) collective-permute-start(f32[128,128]{1,0:T(8,128)} %get-tuple-element.25), channel_id=1, source_target_pairs={{0,32},{1,33},{2,34},{3,35},{4,36},{5,37},{6,38},{7,39},{8,40},{9,... | collective-permute-start | bytes 196616 | tf_op jit(solution)/shard_map/ppermute | solution.py:55
  7.6 3.1 %copy-start.1 = (f32[128,128]{1,0:T(8,128)S(1)}, f32[128,128]{1,0:T(8,128)}, u32[]{:S(2)}) copy-start(f32[128,128]{1,0:T(8,128)} %get-tuple-element.25) | copy-start | bytes 196612
  10.7 4.4 %collective-permute-start.1 = (f32[128,128]{1,0:T(8,128)S(1)}, f32[128,128]{1,0:T(8,128)S(1)}, u32[]{:S(2)}, u32[]{:S(2)}) collective-permute-start(f32[128,128]{1,0:T(8,128)S(1)} %add.24.refs_0_), channel_id=1, source_target_pairs={{0,64},{1,65},{2,66},{3,67},{4,68},{5,69},{6,70},{7,71},{8,72},{9,... | collective-permute-start | bytes 196616 | tf_op jit(solution)/shard_map/ppermute | solution.py:55
  12.0 28.0 %collective-permute-start.4 = (f32[1760,128]{1,0:T(8,128)}, f32[1760,128]{1,0:T(8,128)}, u32[]{:S(2)}, u32[]{:S(2)}) collective-permute-start(f32[1760,128]{1,0:T(8,128)} %hold.2), channel_id=1, source_target_pairs={{0,15},{1,0},{2,1},{3,2},{4,3},{5,4},{6,5},{7,6},{8,7},{9,8},{10,9... | collective-permute-start | bytes 2703368 | tf_op jit(solution)/shard_map/ppermute | solution.py:55
  15.1 14.1 %copy-start = (s32[64,2,32]{0,2,1:T(8,128)S(1)}, s32[64,2,32]{0,2,1:T(8,128)}, u32[]{:S(2)}) copy-start(s32[64,2,32]{0,2,1:T(8,128)} %param.5) | copy-start | bytes 49156
  15.1 12.7 %collective-permute-start.2 = (f32[128,128]{1,0:T(8,128)S(1)}, f32[128,128]{1,0:T(8,128)S(1)}, u32[]{:S(2)}, u32[]{:S(2)}) collective-permute-start(f32[128,128]{1,0:T(8,128)S(1)} %add.25), channel_id=1, source_target_pairs={{0,128},{1,129},{2,130},{3,131},{4,132},{5,133},{6,134},{7,135},{8... | collective-permute-start | bytes 196616 | tf_op jit(solution)/shard_map/ppermute | solution.py:55
  27.9 1.3 %collective-permute-start.3 = (f32[128,128]{1,0:T(8,128)S(1)}, f32[128,128]{1,0:T(8,128)S(1)}, u32[]{:S(2)}, u32[]{:S(2)}) collective-permute-start(f32[128,128]{1,0:T(8,128)S(1)} %add.26), channel_id=1, source_target_pairs={{0,16},{1,17},{2,18},{3,19},{4,20},{5,21},{6,22},{7,23},{8,24},{9,... | collective-permute-start | bytes 196616 | tf_op jit(solution)/shard_map/ppermute | solution.py:55
  40.8 4.4 %collective-permute-start.5 = (f32[128,128]{1,0:T(8,128)S(1)}, f32[128,128]{1,0:T(8,128)S(1)}, u32[]{:S(2)}, u32[]{:S(2)}) collective-permute-start(f32[128,128]{1,0:T(8,128)S(1)} %inflow.1), channel_id=1, source_target_pairs={{0,32},{1,33},{2,34},{3,35},{4,36},{5,37},{6,38},{7,39},{8,40},{9,... | collective-permute-start | bytes 196616 | tf_op jit(solution)/shard_map/ppermute | solution.py:55
  45.2 4.5 %collective-permute-start.6 = (f32[128,128]{1,0:T(8,128)S(1)}, f32[128,128]{1,0:T(8,128)S(1)}, u32[]{:S(2)}, u32[]{:S(2)}) collective-permute-start(f32[128,128]{1,0:T(8,128)S(1)} %add.28), channel_id=1, source_target_pairs={{0,64},{1,65},{2,66},{3,67},{4,68},{5,69},{6,70},{7,71},{8,72},{9,... | collective-permute-start | bytes 196616 | tf_op jit(solution)/shard_map/ppermute | solution.py:55
  49.7 22.4 %collective-permute-start.9 = (f32[1728,128]{1,0:T(8,128)}, f32[1728,128]{1,0:T(8,128)}, u32[]{:S(2)}, u32[]{:S(2)}) collective-permute-start(f32[1728,128]{1,0:T(8,128)} %hold.3), channel_id=1, source_target_pairs={{0,15},{1,0},{2,1},{3,2},{4,3},{5,4},{6,5},{7,6},{8,7},{9,8},{10,9... | collective-permute-start | bytes 2654216 | tf_op jit(solution)/shard_map/ppermute | solution.py:55
  49.8 11.4 %collective-permute-start.7 = (f32[128,128]{1,0:T(8,128)S(1)}, f32[128,128]{1,0:T(8,128)S(1)}, u32[]{:S(2)}, u32[]{:S(2)}) collective-permute-start(f32[128,128]{1,0:T(8,128)S(1)} %add.29.refs_0_), channel_id=1, source_target_pairs={{0,128},{1,129},{2,130},{3,131},{4,132},{5,133},{6,134},{7,135},{8... | collective-permute-start | bytes 196616 | tf_op jit(solution)/shard_map/ppermute | solution.py:55
  61.2 1.3 %collective-permute-start.8 = (f32[128,128]{1,0:T(8,128)S(1)}, f32[128,128]{1,0:T(8,128)S(1)}, u32[]{:S(2)}, u32[]{:S(2)}) collective-permute-start(f32[128,128]{1,0:T(8,128)S(1)} %add.30), channel_id=1, source_target_pairs={{0,16},{1,17},{2,18},{3,19},{4,20},{5,21},{6,22},{7,23},{8,24},{9,... | collective-permute-start | bytes 196616 | tf_op jit(solution)/shard_map/ppermute | solution.py:55

commit v7 on v6

--- a/solution.py
+++ b/solution.py
@@ -248,7 +248,7 @@
 
 def unpack_kernel(
     dir_ref, in_ref, order_ref, near_any, m_ref, left_any, phi_any,
-    left_ref, phi_ref, flux, whole, high_ref, low_ref, table, padded, sems, out_sems,
+    left_ref, phi_ref, flux, flux_high, flux_low, whole, high_ref, low_ref, table, padded, sems, out_sems,
 ):
     forward = dir_ref[0]
     size = NSLOT // PARTS
@@ -257,6 +257,7 @@
     put_phi(order_ref, padded, table, phi_ref)
     put_left(order_ref, padded, table, left_ref)
     clear_tail(high_ref, low_ref)
+    clear_tail(flux_high, flux_low)
     step = 96
 
     for p in range(PARTS):
@@ -276,17 +277,16 @@
     col = column_of(forward, 3)
     near = column_rows(whole, col)
     outs = fetch(out_sems, (near, near_any.at[pl.ds(0, HALO)]), (left_ref, left_any), (phi_ref, phi_any))
-    put_moments(forward, left_ref, high_ref, low_ref, m_ref)
     cx = coefs_of(phi_ref[...], 1)
     for half in range(2):
         share = cx * whole[pl.ds(half * 4 + col, NSLOT, stride=8), :]
-        split_into(share, pl.ds(0, NSLOT), pl.ds(half * 128, 128), high_ref, low_ref)
-    cols = pl.ds(0, COL)
-    for half, parts in enumerate(sums_of(left_ref[...], high_ref[:, cols], low_ref[:, cols])):
+        split_into(share, pl.ds(0, NSLOT), pl.ds(half * 128, 128), flux_high, flux_low)
+    for half, parts in enumerate(sums_of(left_ref[...], flux_high[...], flux_low[...])):
         for k, part in enumerate(parts):
             flux[pl.ds((half * 2 + k) * 8, 8), :] = part
     outs += [pltpu.make_async_copy(flux, near_any.at[pl.ds(HALO, 32)], out_sems.at[3])]
     outs[-1].start()
+    put_moments(forward, left_ref, high_ref, low_ref, m_ref)
     settle(outs)
 
 
@@ -302,6 +302,8 @@
             pltpu.VMEM((48, NPAD), BF16),
             pltpu.VMEM((NSLOT, 128), BF16),
             pltpu.VMEM((32, 128), F32),
+            pltpu.VMEM((NPAD, COL), BF16),
+            pltpu.VMEM((NPAD, COL), BF16),
             pltpu.VMEM((NSLOT * 8, 128), F32),
             pltpu.VMEM((NPAD, CELLS), BF16),
             pltpu.VMEM((NPAD, CELLS), BF16),

time: 75.2 us -> 74.6 us (level)
  transfers between devices with their start and end apart: 10 -> 10, of which waited for: 7 -> 7; matrix products, arithmetic and copies ran while one was open for 0% -> 0% of each run, Pallas kernels for 49% -> 50%
where the time goes in v7:
time: 74.6 us; the launch traced here: 74.2 us
  Pallas kernels  44.7 us (60%)
  starting transfers between devices  19.6 us (26%)
  waiting for transfers between devices  8.86 us (12%)
  between operations  1 us (1%)
    pallas_call x5, Pallas kernels, drift(): pl.pallas_call(kernel, in_specs=[smem()] + [anywhere()] * (1 + len(states...  21.4 us
    ppermute x10, starting transfers between devices, permute(): lax.ppermute(value, AXES, [(i, index_of(*move(*device_of(i)))) for i in r...  19.6 us
    ppermute x10, waiting for transfers between devices, permute(): lax.ppermute(value, AXES, [(i, index_of(*move(*device_of(i)))) for i in r...  8.86 us
    pallas_call x1, Pallas kernels, first_step(): pl.pallas_call(kernel, in_specs=[smem(), smem()] + [anywhere()] * (1 + n)...  7.74 us
    pallas_call x1, Pallas kernels, second_step(): pl.pallas_call(kernel, in_specs=[smem(), smem()] + [anywhere()] * (2 + n)...  7.68 us
    pallas_call x1, Pallas kernels, unpack(): pl.pallas_call(unpack_kernel, in_specs=[smem(), anywhere(), spec()], out_...  4.69 us
    pallas_call x1, Pallas kernels, last(): pl.pallas_call(last_kernel, in_specs=[smem()] + [anywhere()] * 4, out_spe...  2.38 us
  transfers between devices with their start and end apart: 10, of which 7 were waited for; matrix products, arithmetic and copies ran while one was open for 0% of the time, Pallas kernels for 50%

profile of v7, /device:TPU:4, one launch (start us, length us, event | category | flops | bytes accessed | tf_op | source)
XLA Modules:
  0.0 74.2 jit_solution(9406867779245393040)
XLA Ops:
  0.6 4.7 %unpack.1 = (f32[1760,128]{1,0:T(8,128)}, f32[128,128]{1,0:T(8,128)}, bf16[48,896]{1,0:T(8,128)(2,1)}, bf16[864,128]{1,0:T(8,128)(2,1)}) custom-call(s32[1]{0:T(128)} %bitcast.dir_ref.refs_0_, f32[6912,128]{1,0:T(8,128)} %bitcast.17, s32[864]{0:T(1024)} %order_ref.1), custom_call_target="tpu_custom_call" | custom-call | tf_op jit(solution)/shard_map/unpack/pallas_call | solution.py:294
  5.3 1.7 %collective-permute-start = (f32[128,128]{1,0:T(8,128)}, f32[128,128]{1,0:T(8,128)S(1)}, u32[]{:S(2)}, u32[]{:S(2)}) collective-permute-start(f32[128,128]{1,0:T(8,128)} %get-tuple-element.25), channel_id=1, source_target_pairs={{0,32},{1,33},{2,34},{3,35},{4,36},{5,37},{6,38},{7,39},{8,40},{9,... | collective-permute-start | bytes 196616 | tf_op jit(solution)/shard_map/ppermute | solution.py:55
  7.0 3.1 %drift.5.refs_3_ = f32[192,1024]{1,0:T(8,128)} custom-call(s32[1]{0:T(128)} %bitcast.dir_ref.refs_0_, bf16[864,128]{1,0:T(8,128)(2,1)} %get-tuple-element.26.refs_1_.refs_7_.refs_9_.phi_any, f32[6912,128]{1,0:T(8,128)} %bitcast.18), custom_call_target="tpu_custom_call" | custom-call | flops 3449999872 | bytes 10000 | tf_op jit(solution)/shard_map/drift/pallas_call | solution.py:521
  10.1 0.0 collective-permute-done
  10.1 0.0 copy-done.1
  10.2 1.3 %collective-permute-start.1 = (f32[128,128]{1,0:T(8,128)S(1)}, f32[128,128]{1,0:T(8,128)S(1)}, u32[]{:S(2)}, u32[]{:S(2)}) collective-permute-start(f32[128,128]{1,0:T(8,128)S(1)} %add.24.refs_0_), channel_id=1, source_target_pairs={{0,64},{1,65},{2,66},{3,67},{4,68},{5,69},{6,70},{7,71},{8,72},{9,... | collective-permute-start | bytes 196616 | tf_op jit(solution)/shard_map/ppermute | solution.py:55
  11.5 2.9 %collective-permute-start.4 = (f32[1760,128]{1,0:T(8,128)}, f32[1760,128]{1,0:T(8,128)}, u32[]{:S(2)}, u32[]{:S(2)}) collective-permute-start(f32[1760,128]{1,0:T(8,128)} %hold.2), channel_id=1, source_target_pairs={{0,15},{1,0},{2,1},{3,2},{4,3},{5,4},{6,5},{7,6},{8,7},{9,8},{10,9... | collective-permute-start | bytes 2703368 | tf_op jit(solution)/shard_map/ppermute | solution.py:55
  14.4 0.1 collective-permute-done.1
  14.5 0.0 copy-start
  14.5 6.1 %collective-permute-start.2 = (f32[128,128]{1,0:T(8,128)S(1)}, f32[128,128]{1,0:T(8,128)S(1)}, u32[]{:S(2)}, u32[]{:S(2)}) collective-permute-start(f32[128,128]{1,0:T(8,128)S(1)} %add.25), channel_id=1, source_target_pairs={{0,128},{1,129},{2,130},{3,131},{4,132},{5,133},{6,134},{7,135},{8... | collective-permute-start | bytes 196616 | tf_op jit(solution)/shard_map/ppermute | solution.py:55
  20.6 6.7 %drift.6.refs_4_ = f32[672,1024]{1,0:T(8,128)} custom-call(s32[1]{0:T(128)} %bitcast.dir_ref.refs_0_, bf16[864,128]{1,0:T(8,128)(2,1)} %get-tuple-element.26.refs_1_.refs_7_.refs_9_.phi_any, f32[6912,128]{1,0:T(8,128)} %bitcast.19), custom_call_target="tpu_custom_call" | custom-call | flops 3449999872 | bytes 10000 | tf_op jit(solution)/shard_map/drift/pallas_call | solution.py:521
  27.3 0.0 collective-permute-done.2
  27.3 0.1 collective-permute-start.3
  27.4 1.2 %collective-permute-done.3 = f32[128,128]{1,0:T(8,128)S(1)} collective-permute-done((f32[128,128]{1,0:T(8,128)S(1)}, f32[128,128]{1,0:T(8,128)S(1)}, u32[]{:S(2)}, u32[]{:S(2)}) %collective-permute-start.3) | collective-permute-done | bytes 65568 | tf_op jit(solution)/shard_map/ppermute | solution.py:55
  28.7 7.7 %first_step.1 = (f32[864,1024]{1,0:T(8,128)}, f32[1728,128]{1,0:T(8,128)}, f32[128,128]{1,0:T(8,128)S(1)}) custom-call(s32[1]{0:T(128)} %bitcast.dir_ref.refs_0_, s32[1]{0:T(128)} %bitcast.1.refs_1_, f32[6912,128]{1,0:T(8,128)} %bitcast.20, f32[192,1024]{1,0:T(8,128)} %drift.5.refs_3_, f32[672,1024]{1,0:T(8,128)} %drift.6.refs_4_, ...), custom_call_target="tpu_custom_call" | custom-call | flops 5750000128 | bytes 10000 | tf_op jit(solution)/shard_map/first_step/pallas_call | solution.py:620
  36.4 3.1 %collective-permute-done.4.halo_any.refs_3_ = f32[1760,128]{1,0:T(8,128)} collective-permute-done((f32[1760,128]{1,0:T(8,128)}, f32[1760,128]{1,0:T(8,128)}, u32[]{:S(2)}, u32[]{:S(2)}) %collective-permute-start.4) | collective-permute-done | bytes 901152 | tf_op jit(solution)/shard_map/ppermute | solution.py:55
  39.5 0.7 %inflow.1 = f32[128,128]{1,0:T(8,128)S(1)} custom-call(s32[1]{0:T(128)} %bitcast.dir_ref.refs_0_, f32[1760,128]{1,0:T(8,128)} %collective-permute-done.4.halo_any.refs_3_, f32[128,128]{1,0:T(8,128)S(1)} %get-tuple-element.35.m_any), custom_call_target="tpu_custom_call" | custom-call | tf_op jit(solution)/shard_map/inflow/pallas_call | solution.py:658
  40.3 0.2 collective-permute-start.5
  40.5 3.1 %drift.7.refs_4_ = f32[192,1024]{1,0:T(8,128)} custom-call(s32[1]{0:T(128)} %bitcast.dir_ref.refs_0_, bf16[864,128]{1,0:T(8,128)(2,1)} %get-tuple-element.26.refs_1_.refs_7_.refs_9_.phi_any, f32[864,1024]{1,0:T(8,128)} %get-tuple-element.33.refs_2_, f32[1760,128]{1,0:T(8,128)} %collective-permute-done.4.halo_any.refs_3_), custom_call_target="tpu_custom_call" | custom-call | flops 3449999872 | bytes 10000 | tf_op jit(solution)/shard_map/drift/pallas_call | solution.py:521
  43.6 1.0 %collective-permute-done.5 = f32[128,128]{1,0:T(8,128)S(1)} collective-permute-done((f32[128,128]{1,0:T(8,128)S(1)}, f32[128,128]{1,0:T(8,128)S(1)}, u32[]{:S(2)}, u32[]{:S(2)}) %collective-permute-start.5) | collective-permute-done | bytes 65568 | tf_op jit(solution)/shard_map/ppermute | solution.py:55
  44.6 1.1 %collective-permute-start.6 = (f32[128,128]{1,0:T(8,128)S(1)}, f32[128,128]{1,0:T(8,128)S(1)}, u32[]{:S(2)}, u32[]{:S(2)}) collective-permute-start(f32[128,128]{1,0:T(8,128)S(1)} %add.28), channel_id=1, source_target_pairs={{0,64},{1,65},{2,66},{3,67},{4,68},{5,69},{6,70},{7,71},{8,72},{9,... | collective-permute-start | bytes 196616 | tf_op jit(solution)/shard_map/ppermute | solution.py:55
  45.7 3.2 %drift.8.refs_5_ = f32[192,1024]{1,0:T(8,128)} custom-call(s32[1]{0:T(128)} %bitcast.dir_ref.refs_0_, bf16[864,128]{1,0:T(8,128)(2,1)} %get-tuple-element.26.refs_1_.refs_7_.refs_9_.phi_any, f32[864,1024]{1,0:T(8,128)} %get-tuple-element.33.refs_2_, f32[1760,128]{1,0:T(8,128)} %collective-permute-done.4.halo_any.refs_3_), custom_call_target="tpu_custom_call" | custom-call | flops 3449999872 | bytes 10000 | tf_op jit(solution)/shard_map/drift/pallas_call | solution.py:521
  48.9 0.3 collective-permute-done.6
  49.2 0.1 collective-permute-start.9
  49.3 6.0 %collective-permute-start.7 = (f32[128,128]{1,0:T(8,128)S(1)}, f32[128,128]{1,0:T(8,128)S(1)}, u32[]{:S(2)}, u32[]{:S(2)}) collective-permute-start(f32[128,128]{1,0:T(8,128)S(1)} %add.29.refs_0_), channel_id=1, source_target_pairs={{0,128},{1,129},{2,130},{3,131},{4,132},{5,133},{6,134},{7,135},{8... | collective-permute-start | bytes 196616 | tf_op jit(solution)/shard_map/ppermute | solution.py:55
  55.3 5.3 %drift.9.refs_6_ = f32[480,1024]{1,0:T(8,128)} custom-call(s32[1]{0:T(128)} %bitcast.dir_ref.refs_0_, bf16[864,128]{1,0:T(8,128)(2,1)} %get-tuple-element.26.refs_1_.refs_7_.refs_9_.phi_any, f32[864,1024]{1,0:T(8,128)} %get-tuple-element.33.refs_2_, f32[1760,128]{1,0:T(8,128)} %collective-permute-done.4.halo_any.refs_3_), custom_call_target="tpu_custom_call" | custom-call | flops 3449999872 | bytes 10000 | tf_op jit(solution)/shard_map/drift/pallas_call | solution.py:521
  60.6 0.0 collective-permute-done.7
  60.7 0.1 collective-permute-start.8
  60.8 1.2 %collective-permute-done.8 = f32[128,128]{1,0:T(8,128)S(1)} collective-permute-done((f32[128,128]{1,0:T(8,128)S(1)}, f32[128,128]{1,0:T(8,128)S(1)}, u32[]{:S(2)}, u32[]{:S(2)}) %collective-permute-start.8) | collective-permute-done | bytes 65568 | tf_op jit(solution)/shard_map/ppermute | solution.py:55
  62.0 7.7 %second_step.1 = (f32[6912,128]{1,0:T(8,128)}, f32[1728,128]{1,0:T(8,128)}, f32[4,2,32]{2,1,0:T(2,128)}) custom-call(s32[1]{0:T(128)} %bitcast.dir_ref.refs_0_, s32[1]{0:T(128)} %bitcast.1.refs_1_, f32[864,1024]{1,0:T(8,128)} %get-tuple-element.33.refs_2_, f32[1760,128]{1,0:T(8,128)} %collective-permute-done.4.halo_any.refs_3_, f32[192,1024]{1,0:T(8,128)} %drift.7.refs_4_, ...), custom_call_target="tpu_custom_call" | custom-call | flops 2300000000 | bytes 10000 | tf_op jit(solution)/shard_map/second_step/pallas_call | solution.py:714
  69.7 1.9 %collective-permute-done.9.halo_any = f32[1728,128]{1,0:T(8,128)} collective-permute-done((f32[1728,128]{1,0:T(8,128)}, f32[1728,128]{1,0:T(8,128)}, u32[]{:S(2)}, u32[]{:S(2)}) %collective-permute-start.9) | collective-permute-done | bytes 884768 | tf_op jit(solution)/shard_map/ppermute | solution.py:55
  71.6 2.4 %last.1 = f32[6912,128]{1,0:T(8,128)} custom-call(s32[1]{0:T(128)} %bitcast.dir_ref.refs_0_, f32[6912,128]{1,0:T(8,128)} %get-tuple-element.44.h_any, f32[1728,128]{1,0:T(8,128)} %get-tuple-element.45.pre_any, f32[1728,128]{1,0:T(8,128)} %collective-permute-done.9.halo_any, ...), custom_call_target="tpu_custom_call", output_to_operand_aliasing={{}: (1, {})} | custom-call | tf_op jit(solution)/shard_map/last/pallas_call | solution.py:763
  (12 shorter events, 0.1 us)
Async XLA Ops:
  5.3 4.8 %collective-permute-start = (f32[128,128]{1,0:T(8,128)}, f32[128,128]{1,0:T(8,128)S(1)}, u32[]{:S(2)}, u32[]{:S(2)}) collective-permute-start(f32[128,128]{1,0:T(8,128)} %get-tuple-element.25), channel_id=1, source_target_pairs={{0,32},{1,33},{2,34},{3,35},{4,36},{5,37},{6,38},{7,39},{8,40},{9,... | collective-permute-start | bytes 196616 | tf_op jit(solution)/shard_map/ppermute | solution.py:55
  7.0 3.1 %copy-start.1 = (f32[128,128]{1,0:T(8,128)S(1)}, f32[128,128]{1,0:T(8,128)}, u32[]{:S(2)}) copy-start(f32[128,128]{1,0:T(8,128)} %get-tuple-element.25) | copy-start | bytes 196612
  10.2 4.4 %collective-permute-start.1 = (f32[128,128]{1,0:T(8,128)S(1)}, f32[128,128]{1,0:T(8,128)S(1)}, u32[]{:S(2)}, u32[]{:S(2)}) collective-permute-start(f32[128,128]{1,0:T(8,128)S(1)} %add.24.refs_0_), channel_id=1, source_target_pairs={{0,64},{1,65},{2,66},{3,67},{4,68},{5,69},{6,70},{7,71},{8,72},{9,... | collective-permute-start | bytes 196616 | tf_op jit(solution)/shard_map/ppermute | solution.py:55
  11.5 28.1 %collective-permute-start.4 = (f32[1760,128]{1,0:T(8,128)}, f32[1760,128]{1,0:T(8,128)}, u32[]{:S(2)}, u32[]{:S(2)}) collective-permute-start(f32[1760,128]{1,0:T(8,128)} %hold.2), channel_id=1, source_target_pairs={{0,15},{1,0},{2,1},{3,2},{4,3},{5,4},{6,5},{7,6},{8,7},{9,8},{10,9... | collective-permute-start | bytes 2703368 | tf_op jit(solution)/shard_map/ppermute | solution.py:55
  14.5 14.1 %copy-start = (s32[64,2,32]{0,2,1:T(8,128)S(1)}, s32[64,2,32]{0,2,1:T(8,128)}, u32[]{:S(2)}) copy-start(s32[64,2,32]{0,2,1:T(8,128)} %param.5) | copy-start | bytes 49156
  14.5 12.7 %collective-permute-start.2 = (f32[128,128]{1,0:T(8,128)S(1)}, f32[128,128]{1,0:T(8,128)S(1)}, u32[]{:S(2)}, u32[]{:S(2)}) collective-permute-start(f32[128,128]{1,0:T(8,128)S(1)} %add.25), channel_id=1, source_target_pairs={{0,128},{1,129},{2,130},{3,131},{4,132},{5,133},{6,134},{7,135},{8... | collective-permute-start | bytes 196616 | tf_op jit(solution)/shard_map/ppermute | solution.py:55
  27.3 1.3 %collective-permute-start.3 = (f32[128,128]{1,0:T(8,128)S(1)}, f32[128,128]{1,0:T(8,128)S(1)}, u32[]{:S(2)}, u32[]{:S(2)}) collective-permute-start(f32[128,128]{1,0:T(8,128)S(1)} %add.26), channel_id=1, source_target_pairs={{0,16},{1,17},{2,18},{3,19},{4,20},{5,21},{6,22},{7,23},{8,24},{9,... | collective-permute-start | bytes 196616 | tf_op jit(solution)/shard_map/ppermute | solution.py:55
  40.3 4.4 %collective-permute-start.5 = (f32[128,128]{1,0:T(8,128)S(1)}, f32[128,128]{1,0:T(8,128)S(1)}, u32[]{:S(2)}, u32[]{:S(2)}) collective-permute-start(f32[128,128]{1,0:T(8,128)S(1)} %inflow.1), channel_id=1, source_target_pairs={{0,32},{1,33},{2,34},{3,35},{4,36},{5,37},{6,38},{7,39},{8,40},{9,... | collective-permute-start | bytes 196616 | tf_op jit(solution)/shard_map/ppermute | solution.py:55
  44.6 4.5 %collective-permute-start.6 = (f32[128,128]{1,0:T(8,128)S(1)}, f32[128,128]{1,0:T(8,128)S(1)}, u32[]{:S(2)}, u32[]{:S(2)}) collective-permute-start(f32[128,128]{1,0:T(8,128)S(1)} %add.28), channel_id=1, source_target_pairs={{0,64},{1,65},{2,66},{3,67},{4,68},{5,69},{6,70},{7,71},{8,72},{9,... | collective-permute-start | bytes 196616 | tf_op jit(solution)/shard_map/ppermute | solution.py:55
  49.2 22.4 %collective-permute-start.9 = (f32[1728,128]{1,0:T(8,128)}, f32[1728,128]{1,0:T(8,128)}, u32[]{:S(2)}, u32[]{:S(2)}) collective-permute-start(f32[1728,128]{1,0:T(8,128)} %hold.3), channel_id=1, source_target_pairs={{0,15},{1,0},{2,1},{3,2},{4,3},{5,4},{6,5},{7,6},{8,7},{9,8},{10,9... | collective-permute-start | bytes 2654216 | tf_op jit(solution)/shard_map/ppermute | solution.py:55
  49.3 11.4 %collective-permute-start.7 = (f32[128,128]{1,0:T(8,128)S(1)}, f32[128,128]{1,0:T(8,128)S(1)}, u32[]{:S(2)}, u32[]{:S(2)}) collective-permute-start(f32[128,128]{1,0:T(8,128)S(1)} %add.29.refs_0_), channel_id=1, source_target_pairs={{0,128},{1,129},{2,130},{3,131},{4,132},{5,133},{6,134},{7,135},{8... | collective-permute-start | bytes 196616 | tf_op jit(solution)/shard_map/ppermute | solution.py:55
  60.7 1.3 %collective-permute-start.8 = (f32[128,128]{1,0:T(8,128)S(1)}, f32[128,128]{1,0:T(8,128)S(1)}, u32[]{:S(2)}, u32[]{:S(2)}) collective-permute-start(f32[128,128]{1,0:T(8,128)S(1)} %add.30), channel_id=1, source_target_pairs={{0,16},{1,17},{2,18},{3,19},{4,20},{5,21},{6,22},{7,23},{8,24},{9,... | collective-permute-start | bytes 196616 | tf_op jit(solution)/shard_map/ppermute | solution.py:55

commit v8 on v7

--- a/solution.py
+++ b/solution.py
@@ -238,7 +238,7 @@
 LAST_PARTS = 3
 HALO = 2 * NSLOT
 PIECES = (((0, 192), (192, 672)), ((0, 192), (192, 192), (384, 480)))
-FIRST_COST, SECOND_COST, HOLD_COST = 5, 2, 3
+FIRST_COST, SECOND_COST, HOLD_COST = 5, 5, 3
 DRIFT_COST = 3
 
 

time: 74.6 us -> 75.3 us (level)
  waiting for transfers between devices: 8.86 us -> 14.9 us
  starting transfers between devices: 19.6 us -> 13.6 us
    ppermute x10, waiting for transfers between devices: 8.86 us -> 14.9 us  [permute(): lax.ppermute(value, AXES, [(i, index_of(*move(*device_of(i)))) for i in r...]
    ppermute x10, starting transfers between devices: 19.6 us -> 13.6 us  [permute(): lax.ppermute(value, AXES, [(i, index_of(*move(*device_of(i)))) for i in r...]
  transfers between devices with their start and end apart: 10 -> 10, of which waited for: 7 -> 8; matrix products, arithmetic and copies ran while one was open for 0% -> 0% of each run, Pallas kernels for 50% -> 50%
where the time goes in v8:
time: 75.3 us; the launch traced here: 74.3 us
  Pallas kernels  44.7 us (59%)
  waiting for transfers between devices  14.9 us (20%)
  starting transfers between devices  13.6 us (18%)
  between operations  0.99 us (1%)
    pallas_call x5, Pallas kernels, drift(): pl.pallas_call(kernel, in_specs=[smem()] + [anywhere()] * (1 + len(states...  21.4 us
    ppermute x10, waiting for transfers between devices, permute(): lax.ppermute(value, AXES, [(i, index_of(*move(*device_of(i)))) for i in r...  14.9 us
    ppermute x10, starting transfers between devices, permute(): lax.ppermute(value, AXES, [(i, index_of(*move(*device_of(i)))) for i in r...  13.6 us
    pallas_call x1, Pallas kernels, first_step(): pl.pallas_call(kernel, in_specs=[smem(), smem()] + [anywhere()] * (1 + n)...  7.74 us
    pallas_call x1, Pallas kernels, second_step(): pl.pallas_call(kernel, in_specs=[smem(), smem()] + [anywhere()] * (2 + n)...  7.68 us
    pallas_call x1, Pallas kernels, unpack(): pl.pallas_call(unpack_kernel, in_specs=[smem(), anywhere(), spec()], out_...  4.69 us
    pallas_call x1, Pallas kernels, last(): pl.pallas_call(last_kernel, in_specs=[smem()] + [anywhere()] * 4, out_spe...  2.38 us
  transfers between devices with their start and end apart: 10, of which 8 were waited for; matrix products, arithmetic and copies ran while one was open for 0% of the time, Pallas kernels for 50%

profile of v8, /device:TPU:4, one launch (start us, length us, event | category | flops | bytes accessed | tf_op | source)
XLA Modules:
  0.0 74.3 jit_solution(6396687127800210393)
XLA Ops:
  0.6 4.7 %unpack.1 = (f32[1760,128]{1,0:T(8,128)}, f32[128,128]{1,0:T(8,128)}, bf16[48,896]{1,0:T(8,128)(2,1)}, bf16[864,128]{1,0:T(8,128)(2,1)}) custom-call(s32[1]{0:T(128)} %bitcast.dir_ref.refs_0_, f32[6912,128]{1,0:T(8,128)} %bitcast.17, s32[864]{0:T(1024)} %order_ref.1), custom_call_target="tpu_custom_call" | custom-call | tf_op jit(solution)/shard_map/unpack/pallas_call | solution.py:294
  5.3 1.7 %collective-permute-start = (f32[128,128]{1,0:T(8,128)}, f32[128,128]{1,0:T(8,128)S(1)}, u32[]{:S(2)}, u32[]{:S(2)}) collective-permute-start(f32[128,128]{1,0:T(8,128)} %get-tuple-element.25), channel_id=1, source_target_pairs={{0,32},{1,33},{2,34},{3,35},{4,36},{5,37},{6,38},{7,39},{8,40},{9,... | collective-permute-start | bytes 196616 | tf_op jit(solution)/shard_map/ppermute | solution.py:55
  7.0 3.1 %drift.5.refs_3_ = f32[192,1024]{1,0:T(8,128)} custom-call(s32[1]{0:T(128)} %bitcast.dir_ref.refs_0_, bf16[864,128]{1,0:T(8,128)(2,1)} %get-tuple-element.26.refs_1_.refs_7_.refs_9_.phi_any, f32[6912,128]{1,0:T(8,128)} %bitcast.18), custom_call_target="tpu_custom_call" | custom-call | flops 3449999872 | bytes 10000 | tf_op jit(solution)/shard_map/drift/pallas_call | solution.py:521
  10.1 0.0 collective-permute-done
  10.1 0.0 copy-done.1
  10.2 1.3 %collective-permute-start.1 = (f32[128,128]{1,0:T(8,128)S(1)}, f32[128,128]{1,0:T(8,128)S(1)}, u32[]{:S(2)}, u32[]{:S(2)}) collective-permute-start(f32[128,128]{1,0:T(8,128)S(1)} %add.24.refs_0_), channel_id=1, source_target_pairs={{0,64},{1,65},{2,66},{3,67},{4,68},{5,69},{6,70},{7,71},{8,72},{9,... | collective-permute-start | bytes 196616 | tf_op jit(solution)/shard_map/ppermute | solution.py:55
  11.5 2.9 %collective-permute-start.4 = (f32[1760,128]{1,0:T(8,128)}, f32[1760,128]{1,0:T(8,128)}, u32[]{:S(2)}, u32[]{:S(2)}) collective-permute-start(f32[1760,128]{1,0:T(8,128)} %hold.2), channel_id=1, source_target_pairs={{0,15},{1,0},{2,1},{3,2},{4,3},{5,4},{6,5},{7,6},{8,7},{9,8},{10,9... | collective-permute-start | bytes 2703368 | tf_op jit(solution)/shard_map/ppermute | solution.py:55
  14.4 0.1 collective-permute-done.1
  14.5 0.0 copy-start
  14.5 6.1 %collective-permute-start.2 = (f32[128,128]{1,0:T(8,128)S(1)}, f32[128,128]{1,0:T(8,128)S(1)}, u32[]{:S(2)}, u32[]{:S(2)}) collective-permute-start(f32[128,128]{1,0:T(8,128)S(1)} %add.25), channel_id=1, source_target_pairs={{0,128},{1,129},{2,130},{3,131},{4,132},{5,133},{6,134},{7,135},{8... | collective-permute-start | bytes 196616 | tf_op jit(solution)/shard_map/ppermute | solution.py:55
  20.6 6.7 %drift.6.refs_4_ = f32[672,1024]{1,0:T(8,128)} custom-call(s32[1]{0:T(128)} %bitcast.dir_ref.refs_0_, bf16[864,128]{1,0:T(8,128)(2,1)} %get-tuple-element.26.refs_1_.refs_7_.refs_9_.phi_any, f32[6912,128]{1,0:T(8,128)} %bitcast.19), custom_call_target="tpu_custom_call" | custom-call | flops 3449999872 | bytes 10000 | tf_op jit(solution)/shard_map/drift/pallas_call | solution.py:521
  27.3 0.0 collective-permute-done.2
  27.3 0.1 collective-permute-start.3
  27.4 1.2 %collective-permute-done.3 = f32[128,128]{1,0:T(8,128)S(1)} collective-permute-done((f32[128,128]{1,0:T(8,128)S(1)}, f32[128,128]{1,0:T(8,128)S(1)}, u32[]{:S(2)}, u32[]{:S(2)}) %collective-permute-start.3) | collective-permute-done | bytes 65568 | tf_op jit(solution)/shard_map/ppermute | solution.py:55
  28.7 7.7 %first_step.1 = (f32[864,1024]{1,0:T(8,128)}, f32[1728,128]{1,0:T(8,128)}, f32[128,128]{1,0:T(8,128)S(1)}) custom-call(s32[1]{0:T(128)} %bitcast.dir_ref.refs_0_, s32[1]{0:T(128)} %bitcast.1.refs_1_, f32[6912,128]{1,0:T(8,128)} %bitcast.20, f32[192,1024]{1,0:T(8,128)} %drift.5.refs_3_, f32[672,1024]{1,0:T(8,128)} %drift.6.refs_4_, ...), custom_call_target="tpu_custom_call" | custom-call | flops 5750000128 | bytes 10000 | tf_op jit(solution)/shard_map/first_step/pallas_call | solution.py:620
  36.4 3.1 %collective-permute-done.4.halo_any.refs_3_ = f32[1760,128]{1,0:T(8,128)} collective-permute-done((f32[1760,128]{1,0:T(8,128)}, f32[1760,128]{1,0:T(8,128)}, u32[]{:S(2)}, u32[]{:S(2)}) %collective-permute-start.4) | collective-permute-done | bytes 901152 | tf_op jit(solution)/shard_map/ppermute | solution.py:55
  39.5 0.7 %inflow.1 = f32[128,128]{1,0:T(8,128)S(1)} custom-call(s32[1]{0:T(128)} %bitcast.dir_ref.refs_0_, f32[1760,128]{1,0:T(8,128)} %collective-permute-done.4.halo_any.refs_3_, f32[128,128]{1,0:T(8,128)S(1)} %get-tuple-element.35.m_any), custom_call_target="tpu_custom_call" | custom-call | tf_op jit(solution)/shard_map/inflow/pallas_call | solution.py:658
  40.3 0.2 collective-permute-start.5
  40.5 3.1 %drift.7.refs_4_ = f32[192,1024]{1,0:T(8,128)} custom-call(s32[1]{0:T(128)} %bitcast.dir_ref.refs_0_, bf16[864,128]{1,0:T(8,128)(2,1)} %get-tuple-element.26.refs_1_.refs_7_.refs_9_.phi_any, f32[864,1024]{1,0:T(8,128)} %get-tuple-element.33.refs_2_, f32[1760,128]{1,0:T(8,128)} %collective-permute-done.4.halo_any.refs_3_), custom_call_target="tpu_custom_call" | custom-call | flops 3449999872 | bytes 10000 | tf_op jit(solution)/shard_map/drift/pallas_call | solution.py:521
  43.6 1.0 %collective-permute-done.5 = f32[128,128]{1,0:T(8,128)S(1)} collective-permute-done((f32[128,128]{1,0:T(8,128)S(1)}, f32[128,128]{1,0:T(8,128)S(1)}, u32[]{:S(2)}, u32[]{:S(2)}) %collective-permute-start.5) | collective-permute-done | bytes 65568 | tf_op jit(solution)/shard_map/ppermute | solution.py:55
  44.6 1.1 %collective-permute-start.6 = (f32[128,128]{1,0:T(8,128)S(1)}, f32[128,128]{1,0:T(8,128)S(1)}, u32[]{:S(2)}, u32[]{:S(2)}) collective-permute-start(f32[128,128]{1,0:T(8,128)S(1)} %add.28), channel_id=1, source_target_pairs={{0,64},{1,65},{2,66},{3,67},{4,68},{5,69},{6,70},{7,71},{8,72},{9,... | collective-permute-start | bytes 196616 | tf_op jit(solution)/shard_map/ppermute | solution.py:55
  45.7 3.2 %drift.8.refs_5_ = f32[192,1024]{1,0:T(8,128)} custom-call(s32[1]{0:T(128)} %bitcast.dir_ref.refs_0_, bf16[864,128]{1,0:T(8,128)(2,1)} %get-tuple-element.26.refs_1_.refs_7_.refs_9_.phi_any, f32[864,1024]{1,0:T(8,128)} %get-tuple-element.33.refs_2_, f32[1760,128]{1,0:T(8,128)} %collective-permute-done.4.halo_any.refs_3_), custom_call_target="tpu_custom_call" | custom-call | flops 3449999872 | bytes 10000 | tf_op jit(solution)/shard_map/drift/pallas_call | solution.py:521
  48.9 0.8 %collective-permute-done.6 = f32[128,128]{1,0:T(8,128)S(1)} collective-permute-done((f32[128,128]{1,0:T(8,128)S(1)}, f32[128,128]{1,0:T(8,128)S(1)}, u32[]{:S(2)}, u32[]{:S(2)}) %collective-permute-start.6) | collective-permute-done | bytes 65568 | tf_op jit(solution)/shard_map/ppermute | solution.py:55
  49.7 0.1 collective-permute-start.7
  49.8 0.1 collective-permute-start.9
  49.9 5.3 %drift.9.refs_6_ = f32[480,1024]{1,0:T(8,128)} custom-call(s32[1]{0:T(128)} %bitcast.dir_ref.refs_0_, bf16[864,128]{1,0:T(8,128)(2,1)} %get-tuple-element.26.refs_1_.refs_7_.refs_9_.phi_any, f32[864,1024]{1,0:T(8,128)} %get-tuple-element.33.refs_2_, f32[1760,128]{1,0:T(8,128)} %collective-permute-done.4.halo_any.refs_3_), custom_call_target="tpu_custom_call" | custom-call | flops 3449999872 | bytes 10000 | tf_op jit(solution)/shard_map/drift/pallas_call | solution.py:521
  55.2 0.3 collective-permute-done.7
  55.6 0.1 collective-permute-start.8
  55.7 1.2 %collective-permute-done.8 = f32[128,128]{1,0:T(8,128)S(1)} collective-permute-done((f32[128,128]{1,0:T(8,128)S(1)}, f32[128,128]{1,0:T(8,128)S(1)}, u32[]{:S(2)}, u32[]{:S(2)}) %collective-permute-start.8) | collective-permute-done | bytes 65568 | tf_op jit(solution)/shard_map/ppermute | solution.py:55
  56.9 7.7 %second_step.1 = (f32[6912,128]{1,0:T(8,128)}, f32[1728,128]{1,0:T(8,128)}, f32[4,2,32]{2,1,0:T(2,128)}) custom-call(s32[1]{0:T(128)} %bitcast.dir_ref.refs_0_, s32[1]{0:T(128)} %bitcast.1.refs_1_, f32[864,1024]{1,0:T(8,128)} %get-tuple-element.33.refs_2_, f32[1760,128]{1,0:T(8,128)} %collective-permute-done.4.halo_any.refs_3_, f32[192,1024]{1,0:T(8,128)} %drift.7.refs_4_, ...), custom_call_target="tpu_custom_call" | custom-call | flops 5750000128 | bytes 10000 | tf_op jit(solution)/shard_map/second_step/pallas_call | solution.py:714
  64.6 7.1 %collective-permute-done.9.halo_any = f32[1728,128]{1,0:T(8,128)} collective-permute-done((f32[1728,128]{1,0:T(8,128)}, f32[1728,128]{1,0:T(8,128)}, u32[]{:S(2)}, u32[]{:S(2)}) %collective-permute-start.9) | collective-permute-done | bytes 884768 | tf_op jit(solution)/shard_map/ppermute | solution.py:55
  71.7 2.4 %last.1 = f32[6912,128]{1,0:T(8,128)} custom-call(s32[1]{0:T(128)} %bitcast.dir_ref.refs_0_, f32[6912,128]{1,0:T(8,128)} %get-tuple-element.44.h_any, f32[1728,128]{1,0:T(8,128)} %get-tuple-element.45.pre_any, f32[1728,128]{1,0:T(8,128)} %collective-permute-done.9.halo_any, ...), custom_call_target="tpu_custom_call", output_to_operand_aliasing={{}: (1, {})} | custom-call | tf_op jit(solution)/shard_map/last/pallas_call | solution.py:763
  (12 shorter events, 0.1 us)
Async XLA Ops:
  5.3 4.8 %collective-permute-start = (f32[128,128]{1,0:T(8,128)}, f32[128,128]{1,0:T(8,128)S(1)}, u32[]{:S(2)}, u32[]{:S(2)}) collective-permute-start(f32[128,128]{1,0:T(8,128)} %get-tuple-element.25), channel_id=1, source_target_pairs={{0,32},{1,33},{2,34},{3,35},{4,36},{5,37},{6,38},{7,39},{8,40},{9,... | collective-permute-start | bytes 196616 | tf_op jit(solution)/shard_map/ppermute | solution.py:55
  7.0 3.1 %copy-start.1 = (f32[128,128]{1,0:T(8,128)S(1)}, f32[128,128]{1,0:T(8,128)}, u32[]{:S(2)}) copy-start(f32[128,128]{1,0:T(8,128)} %get-tuple-element.25) | copy-start | bytes 196612
  10.2 4.4 %collective-permute-start.1 = (f32[128,128]{1,0:T(8,128)S(1)}, f32[128,128]{1,0:T(8,128)S(1)}, u32[]{:S(2)}, u32[]{:S(2)}) collective-permute-start(f32[128,128]{1,0:T(8,128)S(1)} %add.24.refs_0_), channel_id=1, source_target_pairs={{0,64},{1,65},{2,66},{3,67},{4,68},{5,69},{6,70},{7,71},{8,72},{9,... | collective-permute-start | bytes 196616 | tf_op jit(solution)/shard_map/ppermute | solution.py:55
  11.5 28.1 %collective-permute-start.4 = (f32[1760,128]{1,0:T(8,128)}, f32[1760,128]{1,0:T(8,128)}, u32[]{:S(2)}, u32[]{:S(2)}) collective-permute-start(f32[1760,128]{1,0:T(8,128)} %hold.2), channel_id=1, source_target_pairs={{0,15},{1,0},{2,1},{3,2},{4,3},{5,4},{6,5},{7,6},{8,7},{9,8},{10,9... | collective-permute-start | bytes 2703368 | tf_op jit(solution)/shard_map/ppermute | solution.py:55
  14.5 14.1 %copy-start = (s32[64,2,32]{0,2,1:T(8,128)S(1)}, s32[64,2,32]{0,2,1:T(8,128)}, u32[]{:S(2)}) copy-start(s32[64,2,32]{0,2,1:T(8,128)} %param.5) | copy-start | bytes 49156
  14.5 12.7 %collective-permute-start.2 = (f32[128,128]{1,0:T(8,128)S(1)}, f32[128,128]{1,0:T(8,128)S(1)}, u32[]{:S(2)}, u32[]{:S(2)}) collective-permute-start(f32[128,128]{1,0:T(8,128)S(1)} %add.25), channel_id=1, source_target_pairs={{0,128},{1,129},{2,130},{3,131},{4,132},{5,133},{6,134},{7,135},{8... | collective-permute-start | bytes 196616 | tf_op jit(solution)/shard_map/ppermute | solution.py:55
  27.3 1.3 %collective-permute-start.3 = (f32[128,128]{1,0:T(8,128)S(1)}, f32[128,128]{1,0:T(8,128)S(1)}, u32[]{:S(2)}, u32[]{:S(2)}) collective-permute-start(f32[128,128]{1,0:T(8,128)S(1)} %add.26), channel_id=1, source_target_pairs={{0,16},{1,17},{2,18},{3,19},{4,20},{5,21},{6,22},{7,23},{8,24},{9,... | collective-permute-start | bytes 196616 | tf_op jit(solution)/shard_map/ppermute | solution.py:55
  40.3 4.4 %collective-permute-start.5 = (f32[128,128]{1,0:T(8,128)S(1)}, f32[128,128]{1,0:T(8,128)S(1)}, u32[]{:S(2)}, u32[]{:S(2)}) collective-permute-start(f32[128,128]{1,0:T(8,128)S(1)} %inflow.1), channel_id=1, source_target_pairs={{0,32},{1,33},{2,34},{3,35},{4,36},{5,37},{6,38},{7,39},{8,40},{9,... | collective-permute-start | bytes 196616 | tf_op jit(solution)/shard_map/ppermute | solution.py:55
  44.6 5.1 %collective-permute-start.6 = (f32[128,128]{1,0:T(8,128)S(1)}, f32[128,128]{1,0:T(8,128)S(1)}, u32[]{:S(2)}, u32[]{:S(2)}) collective-permute-start(f32[128,128]{1,0:T(8,128)S(1)} %add.28), channel_id=1, source_target_pairs={{0,64},{1,65},{2,66},{3,67},{4,68},{5,69},{6,70},{7,71},{8,72},{9,... | collective-permute-start | bytes 196616 | tf_op jit(solution)/shard_map/ppermute | solution.py:55
  49.7 5.9 %collective-permute-start.7 = (f32[128,128]{1,0:T(8,128)S(1)}, f32[128,128]{1,0:T(8,128)S(1)}, u32[]{:S(2)}, u32[]{:S(2)}) collective-permute-start(f32[128,128]{1,0:T(8,128)S(1)} %add.29.refs_0_), channel_id=1, source_target_pairs={{0,128},{1,129},{2,130},{3,131},{4,132},{5,133},{6,134},{7,135},{8... | collective-permute-start | bytes 196616 | tf_op jit(solution)/shard_map/ppermute | solution.py:55
  49.8 21.9 %collective-permute-start.9 = (f32[1728,128]{1,0:T(8,128)}, f32[1728,128]{1,0:T(8,128)}, u32[]{:S(2)}, u32[]{:S(2)}) collective-permute-start(f32[1728,128]{1,0:T(8,128)} %hold.3), channel_id=1, source_target_pairs={{0,15},{1,0},{2,1},{3,2},{4,3},{5,4},{6,5},{7,6},{8,7},{9,8},{10,9... | collective-permute-start | bytes 2654216 | tf_op jit(solution)/shard_map/ppermute | solution.py:55
  55.6 1.3 %collective-permute-start.8 = (f32[128,128]{1,0:T(8,128)S(1)}, f32[128,128]{1,0:T(8,128)S(1)}, u32[]{:S(2)}, u32[]{:S(2)}) collective-permute-start(f32[128,128]{1,0:T(8,128)S(1)} %add.30), channel_id=1, source_target_pairs={{0,16},{1,17},{2,18},{3,19},{4,20},{5,21},{6,22},{7,23},{8,24},{9,... | collective-permute-start | bytes 196616 | tf_op jit(solution)/shard_map/ppermute | solution.py:55
